TPU v7x, 32 devices: a whole 2x2x4 slice. The times are simulated.
32 devices in a mesh: dp: 4 (over x, core), seq: 8 (over z, y).
Axes of the slice: x: 2, y: 2, z: 4, core: 2. Of those that a mesh axis runs over, the one named last changes fastest.
Arguments:
- inputs: bfloat16 [8, 2048, 512], P('dp', 'seq'), may hold values from -6 to 6
- encoder: bfloat16 [8, 2048, 512], P('dp', 'seq'), may hold values from -6 to 6
- tgt_seg: int32 [8, 2048], P('dp'), may hold values from 0 to 7, never falling along the last dimension, each value on 1 to 1024 neighbouring positions
- src_len: int32 [8, 8], P('dp'), may hold values from 1 to 1024, 2048 in all within a row
- cotangent: bfloat16 [8, 2048, 512], P('dp', 'seq'), may hold values from -6 to 6
- self_in: bfloat16 [512, 1536], P(('dp', 'seq')), may hold values from -0.25 to 0.25
- self_out: bfloat16 [512, 512], P(('dp', 'seq')), may hold values from -0.5 to 0.5
- cross_q: bfloat16 [512, 512], P(('dp', 'seq')), may hold values from -0.25 to 0.25
- cross_kv: bfloat16 [512, 1024], P(('dp', 'seq')), may hold values from -0.25 to 0.25
- cross_out: bfloat16 [512, 512], P(('dp', 'seq')), may hold values from -0.5 to 0.5
- ffn_in: bfloat16 [512, 2048], P(('dp', 'seq')), may hold values from -0.25 to 0.25
- ffn_out: bfloat16 [2048, 512], P(('dp', 'seq')), may hold values from -0.125 to 0.125
- norm_params: bfloat16 [512, 6], P(('dp', 'seq')), may hold values from -1 to 1.25, as said below
Outputs:
- outputs: float32 [8, 2048, 512], P('dp', 'seq')
- grad_inputs: float32 [8, 2048, 512], P('dp', 'seq')
- grad_encoder: float32 [8, 2048, 512], P('dp', 'seq')
- grad_self_in: float32 [512, 1536], P(('dp', 'seq'))
- grad_self_out: float32 [512, 512], P(('dp', 'seq'))
- grad_cross_q: float32 [512, 512], P(('dp', 'seq'))
- grad_cross_kv: float32 [512, 1024], P(('dp', 'seq'))
- grad_cross_out: float32 [512, 512], P(('dp', 'seq'))
- grad_ffn_in: float32 [512, 2048], P(('dp', 'seq'))
- grad_ffn_out: float32 [2048, 512], P(('dp', 'seq'))
- grad_norm_params: float32 [512, 6], P(('dp', 'seq'))
Inputs may be any that keep to these rules, and one draw needn't show every extreme that they name: `tgt_seg`: ids never fall along a sequence; each document has 1 to 1024 tokens. `src_len`: each row sums to 2048. `norm_params`: columns 0, 2, 4 are gains, columns 1, 3, 5 shifts.
All inputs are finite; a program needn't handle non-finite values.
Results may differ from a plain program's by a relative error of at most 0.018.
Values may be sent and summed in bfloat16 or wider, within the bound.
No kernel may reach another device: no remote copies, remote signals or barrier semaphores. Data moves between devices by JAX's collectives and lax.ppermute only.
A program may use at most 192 MiB of HBM per device.

v0:
```python
import dataclasses
import functools
import math

import jax
import jax.numpy as jnp
from jax import lax
from jax.experimental import pallas as pl
from jax.experimental.pallas import tpu as pltpu
from jax.sharding import PartitionSpec as P

HEAD_DIM = 64
GROUP = 4
LANES = GROUP * HEAD_DIM
CHUNK = 256
LOG2E = 1.4426950408889634
LN2 = 0.6931471805599453
GELU_A = 0.7978845608028654
GELU_B = 0.044715
BF = jnp.bfloat16
F32 = jnp.float32
SMEM = pl.BlockSpec(memory_space=pltpu.SMEM)
VMEM = pl.BlockSpec(memory_space=pltpu.VMEM)
ANY = pl.BlockSpec(memory_space=pl.ANY)


def dot_f32(left, right):
    return jnp.dot(left, right, preferred_element_type=F32)


def dot_nt(left, right):
    return lax.dot_general(left, right, (((1,), (1,)), ((), ())), preferred_element_type=F32)


def padded_bytes(dims, dtype):
    dims = (1,) * (2 - len(dims)) + tuple(dims)
    lead = math.prod(dims[:-2])
    return lead * (-(-dims[-2] // 16) * 16) * (-(-dims[-1] // 128) * 128) * jnp.dtype(dtype).itemsize


def kernel_call(kernel, *, out_shape, in_specs, out_specs, scratch_shapes=(), spare=4):
    def call(*operands):
        need = spare * 2**20
        for operand, spec in zip(operands, in_specs):
            need += padded_bytes(operand.shape, operand.dtype) if spec is VMEM else 0
        for result in jax.tree.leaves(out_shape):
            need += padded_bytes(result.shape, result.dtype)
        for scratch in scratch_shapes:
            if getattr(scratch, "memory_space", None) == pltpu.VMEM:
                need += padded_bytes(scratch.shape, scratch.dtype)
        return pl.pallas_call(
            kernel,
            out_shape=out_shape,
            in_specs=in_specs,
            out_specs=out_specs,
            scratch_shapes=scratch_shapes,
            compiler_params=pltpu.CompilerParams(vmem_limit_bytes=need),
            cost_estimate=pl.CostEstimate(flops=10**6, bytes_accessed=2**10, transcendentals=0),
        )(*operands)

    return call


def shape(dims, dtype=BF):
    return jax.ShapeDtypeStruct(dims, dtype)


def chunk(i):
    return pl.ds(pl.multiple_of(i * CHUNK, CHUNK), CHUNK)


@dataclasses.dataclass(frozen=True)
class Size:
    half: int
    length: int
    own: int
    z_count: int
    x_count: int
    pieces: int
    tile_rows: int
    hidden: int
    first: int


def stack_heads(tile):
    head = lax.broadcasted_iota(jnp.int32, tile.shape, 1) // HEAD_DIM
    zero = jnp.zeros_like(tile)
    return jnp.concatenate([jnp.where(head == h, tile, zero) for h in range(GROUP)], axis=0)


def row_of(column):
    return jnp.transpose(jnp.broadcast_to(column, (column.shape[0], 128)))[0:1, :]


def key_rows(b, keys, total):
    half = keys // 2
    at = pl.multiple_of(b * half, half)
    return pl.ds(at, half), pl.ds(pl.multiple_of(at + total // 2, half), half)


def both_rows(ref, spots, cols):
    return jnp.concatenate([ref[spot, cols] for spot in spots], axis=0)


def attend_kernel(visit_ref, q_ref, kv_ref, qseg_ref, kseg_ref, o_ref, lse_ref, acc_ref, qst_ref):
    width = q_ref.shape[1]
    blocks = qseg_ref.shape[0]
    rows = q_ref.shape[0] // blocks
    total = kv_ref.shape[0]
    keys = total // visit_ref.shape[1]
    groups = width // LANES

    def block(k, carry):
        lo, hi = visit_ref[0, k], visit_ref[1, k]
        q_rows = pl.ds(pl.multiple_of(k * rows, rows), rows)
        qseg = jnp.concatenate([qseg_ref[k]] * GROUP, axis=1)
        for g in range(groups):
            qst_ref[g] = stack_heads(q_ref[q_rows, g * LANES : (g + 1) * LANES])
        acc_ref[...] = jnp.zeros(acc_ref.shape, F32)

        def step(b, carry):
            spots = key_rows(b, keys, total)
            same = kseg_ref[pl.ds(pl.multiple_of(b * keys, keys), keys), :] == qseg
            scores = [
                dot_nt(both_rows(kv_ref, spots, slice(g * LANES, (g + 1) * LANES)), qst_ref[g]) for g in range(groups)
            ]
            out, lows, fades = [], [], []
            for g in range(groups):
                top, tot = carry[g]
                masked = jnp.where(same, scores[g], -1e30)
                new = jnp.maximum(top, jnp.max(masked, axis=0, keepdims=True))
                soft = jnp.exp2(masked - new)
                fade = jnp.exp2(top - new)
                out.append((new, tot * fade + jnp.sum(soft, axis=0, keepdims=True)))
                lows.append(soft.astype(BF))
                fades.append(fade)
            for g in range(groups):
                turned = jnp.transpose(both_rows(kv_ref, spots, slice(width + g * LANES, width + (g + 1) * LANES)))
                for h in range(GROUP):
                    at = g * LANES + h * HEAD_DIM
                    cols = slice(h * rows, (h + 1) * rows)
                    values = turned[h * HEAD_DIM : (h + 1) * HEAD_DIM]
                    acc_ref[at : at + HEAD_DIM] = acc_ref[at : at + HEAD_DIM] * fades[g][:, cols] + dot_f32(
                        values, lows[g][:, cols]
                    )
            return tuple(out)

        start = (jnp.full((1, GROUP * rows), -3e38, F32), jnp.zeros((1, GROUP * rows), F32))
        end = lax.fori_loop(lo, hi, step, (start,) * groups)
        for g in range(groups):
            top, tot = end[g]
            inv = 1.0 / tot
            mixed = [
                acc_ref[g * LANES + h * HEAD_DIM : g * LANES + (h + 1) * HEAD_DIM] * inv[:, h * rows : (h + 1) * rows]
                for h in range(GROUP)
            ]
            o_ref[q_rows, g * LANES : (g + 1) * LANES] = jnp.transpose(jnp.concatenate(mixed, axis=0)).astype(BF)
            lse_ref[k * groups + g] = top + jnp.log2(tot)
        return carry

    lax.fori_loop(0, blocks, block, 0)


def attend_back_kernel(
    visit_ref,
    q_ref,
    do_ref,
    o_ref,
    lse_ref,
    kv_ref,
    qseg_ref,
    kseg_ref,
    dq_ref,
    dkv_ref,
    sum_ref,
    dqt_ref,
    qst_ref,
    dst_ref,
    delta_ref,
):
    width = q_ref.shape[1]
    blocks = qseg_ref.shape[0]
    rows = q_ref.shape[0] // blocks
    total = kv_ref.shape[0]
    keys = total // visit_ref.shape[1]
    groups = width // LANES
    sum_ref[...] = jnp.zeros(sum_ref.shape, F32)

    def block(k, carry):
        lo, hi = visit_ref[0, k], visit_ref[1, k]
        q_rows = pl.ds(pl.multiple_of(k * rows, rows), rows)
        qseg = jnp.concatenate([qseg_ref[k]] * GROUP, axis=1)
        for g in range(groups):
            cols = slice(g * LANES, (g + 1) * LANES)
            qst_ref[g] = stack_heads(q_ref[q_rows, cols])
            d_mixed = do_ref[q_rows, cols]
            dst_ref[g] = stack_heads(d_mixed)
            prod = d_mixed.astype(F32) * o_ref[q_rows, cols].astype(F32)
            delta_ref[g] = row_of(jnp.sum(stack_heads(prod), axis=1, keepdims=True))
        dqt_ref[...] = jnp.zeros(dqt_ref.shape, F32)

        def step(b, carry):
            spots = key_rows(b, keys, total)
            same = kseg_ref[pl.ds(pl.multiple_of(b * keys, keys), keys), :] == qseg
            k_cols = [slice(g * LANES, (g + 1) * LANES) for g in range(groups)]
            v_cols = [slice(width + g * LANES, width + (g + 1) * LANES) for g in range(groups)]
            scores = [dot_nt(both_rows(kv_ref, spots, k_cols[g]), qst_ref[g]) for g in range(groups)]
            d_soft = [dot_nt(both_rows(kv_ref, spots, v_cols[g]), dst_ref[g]) for g in range(groups)]
            softs, d_scores = [], []
            for g in range(groups):
                soft = jnp.where(same, jnp.exp2(scores[g] - lse_ref[k * groups + g]), 0.0)
                d_scores.append((soft * (d_soft[g] - delta_ref[g])).astype(BF))
                softs.append(soft.astype(BF))
            for g in range(groups):
                d_keys, d_values = dot_f32(d_scores[g], qst_ref[g]), dot_f32(softs[g], dst_ref[g])
                for e, spot in enumerate(spots):
                    part = slice(e * keys // 2, (e + 1) * keys // 2)
                    sum_ref[spot, k_cols[g]] += d_keys[part]
                    sum_ref[spot, v_cols[g]] += d_values[part]
                turned = jnp.transpose(both_rows(kv_ref, spots, k_cols[g]))
                for h in range(GROUP):
                    at = slice(g * LANES + h * HEAD_DIM, g * LANES + (h + 1) * HEAD_DIM)
                    keys_t = turned[h * HEAD_DIM : (h + 1) * HEAD_DIM]
                    dqt_ref[at] += dot_f32(keys_t, d_scores[g][:, h * rows : (h + 1) * rows])
            return carry

        lax.fori_loop(lo, hi, step, 0)
        for g in range(groups):
            cols = slice(g * LANES, (g + 1) * LANES)
            dq_ref[q_rows, cols] = (jnp.transpose(dqt_ref[cols]) * HEAD_DIM**-0.5).astype(BF)
        return carry

    lax.fori_loop(0, blocks, block, 0)
    dkv_ref[:, :width] = (sum_ref[:, :width] * LN2).astype(BF)
    dkv_ref[:, width:] = sum_ref[:, width:].astype(BF)


def attend(visits, queries, pairs, qseg, kseg):
    own, width = queries.shape
    blocks = qseg.shape[0]
    rows = own // blocks
    groups = width // LANES
    return kernel_call(
        attend_kernel,
        out_shape=(shape((own, width)), shape((blocks * groups, 1, GROUP * rows), F32)),
        in_specs=[SMEM] + [VMEM] * 4,
        out_specs=(VMEM, VMEM),
        scratch_shapes=[pltpu.VMEM((width, rows), F32), pltpu.VMEM((groups, GROUP * rows, LANES), BF)],
    )(visits, queries, pairs, qseg[:, None, :], kseg.reshape(-1, 1))


def attend_back(visits, queries, d_mixed, mixed, lse, pairs, qseg, kseg):
    own, width = queries.shape
    blocks = qseg.shape[0]
    rows = own // blocks
    groups = width // LANES
    return kernel_call(
        attend_back_kernel,
        out_shape=(shape((own, width)), shape(pairs.shape)),
        in_specs=[SMEM] + [VMEM] * 7,
        out_specs=(VMEM, VMEM),
        scratch_shapes=[
            pltpu.VMEM(pairs.shape, F32),
            pltpu.VMEM((width, rows), F32),
            pltpu.VMEM((groups, GROUP * rows, LANES), BF),
            pltpu.VMEM((groups, GROUP * rows, LANES), BF),
            pltpu.VMEM((groups, 1, GROUP * rows), F32),
        ],
    )(visits, queries, d_mixed, mixed, lse, pairs, qseg[:, None, :], kseg.reshape(-1, 1))


def norm_of(resid):
    centered = resid - jnp.mean(resid, axis=-1, keepdims=True)
    inv = lax.rsqrt(jnp.mean(centered * centered, axis=-1, keepdims=True) + 1e-05)
    return centered * inv, inv


def norm_pull(upstream, hat, inv, gain):
    scaled = upstream * gain
    return inv * (
        scaled - jnp.mean(scaled, axis=-1, keepdims=True) - hat * jnp.mean(scaled * hat, axis=-1, keepdims=True)
    )


def fetch_tiles(place_ref, parts, first, tiles, rows, x_count, whole_ref, sem):
    copies = []
    for e, part in enumerate(parts):
        pieces = part.shape[0]
        for k in range(x_count):
            dp = (place_ref[0] ^ k) * 2 + (place_ref[1] ^ e)
            at = pl.ds(pl.multiple_of(dp * pieces, pieces), pieces)
            for t in range(tiles):
                source = part.at[:, pl.ds(first + (k * tiles + t) * rows, rows)]
                copies.append(pltpu.make_async_copy(source, whole_ref.at[t, at], sem.at[len(copies)]))
    for copy in copies:
        copy.start()
    return copies


def tile_of(ref, t):
    tile = ref[t]
    return tile.reshape(-1, tile.shape[-1])


def own_tokens(near_ref, place_ref, half, z_count):
    y_count = near_ref.shape[0] // z_count
    return jnp.concatenate([near_ref[z * y_count + place_ref[3], :half, :] for z in range(z_count)], axis=0)


def sequence_rows(ref, i, half):
    count = CHUNK // half
    return jnp.concatenate([ref[i * count + j, :half, :] for j in range(count)], axis=0)


def put_pairs(near_ref, far_ref, half, w_k, w_v, kv_ref):
    width = w_k.shape[1]
    count = near_ref.shape[0] * half // CHUNK
    for e, ref in enumerate((near_ref, far_ref)):

        def step(i, carry):
            rows = sequence_rows(ref, i, half)
            at = chunk(i + e * count)
            kv_ref[at, :width] = dot_f32(rows, w_k).astype(BF)
            kv_ref[at, width:] = dot_f32(rows, w_v).astype(BF)
            return carry

        lax.fori_loop(0, count, step, 0)


def grad_rows(place_ref, left_ref, dp_count, e):
    rows = left_ref.shape[0] // dp_count
    out = []
    for k in range(dp_count // 2):
        dp = (place_ref[0] ^ k) * 2 + (place_ref[1] ^ e)
        out.append(left_ref[pl.ds(pl.multiple_of(dp * rows, rows), rows), :])
    return jnp.concatenate(out, axis=0)


def put_grad(target, value, tile, tile_rows):
    x_count, pieces, _, width = target.shape
    rows = value.shape[0] // x_count
    for k in range(x_count):
        part = value[k * rows : (k + 1) * rows].astype(target.dtype)
        target[k, :, tile * tile_rows : (tile + 1) * tile_rows, :] = part.reshape(pieces, tile_rows, width)


def project_kernel(size, place_ref, w_near_ref, w_far_ref, near_ref, far_ref, q_ref, kv_ref, whole_ref, sem):
    copies = fetch_tiles(
        place_ref, (w_near_ref, w_far_ref), size.first, 3, size.tile_rows, size.x_count, whole_ref, sem
    )
    own = own_tokens(near_ref, place_ref, size.half, size.z_count)
    for copy in copies:
        copy.wait()
    q_ref[...] = (dot_f32(own, tile_of(whole_ref, 0)) * (HEAD_DIM**-0.5 * LOG2E)).astype(BF)
    put_pairs(near_ref, far_ref, size.half, tile_of(whole_ref, 1), tile_of(whole_ref, 2), kv_ref)


def project(size, place, weights, near, far):
    width = near.shape[2]
    return kernel_call(
        functools.partial(project_kernel, size),
        out_shape=(
            shape((size.own, width)),
            shape((size.length, 2 * width)),
            shape((3, 2 * size.x_count * size.pieces, size.tile_rows, width)),
        ),
        in_specs=[SMEM, ANY, ANY, VMEM, VMEM],
        out_specs=(VMEM,) * 3,
        scratch_shapes=[pltpu.SemaphoreType.DMA((2 * size.x_count * 3,))],
    )(place, *weights, near, far)


def bridge_kernel(
    size,
    place_ref,
    w_near_ref,
    w_far_ref,
    near_ref,
    source_near_ref,
    source_far_ref,
    mixed_ref,
    q_ref,
    kv_ref,
    whole_ref,
    hat_ref,
    inv_ref,
    norm_ref,
    sem,
):
    copies = fetch_tiles(
        place_ref, (w_near_ref, w_far_ref), size.first, 6, size.tile_rows, size.x_count, whole_ref, sem
    )
    own = own_tokens(near_ref, place_ref, size.half, size.z_count)
    for copy in copies:
        copy.wait()
    norm_ref[...] = jnp.transpose(tile_of(whole_ref, 5)[:, :128].astype(F32))[: norm_ref.shape[0]]
    hat, inv = norm_of(own.astype(F32) + dot_f32(mixed_ref[...], tile_of(whole_ref, 0)))
    hat_ref[...] = hat
    inv_ref[...] = inv
    low = (hat * norm_ref[0:1, :] + norm_ref[1:2, :]).astype(BF)
    q_ref[...] = (dot_f32(low, tile_of(whole_ref, 1)) * (HEAD_DIM**-0.5 * LOG2E)).astype(BF)
    put_pairs(
        source_near_ref, source_far_ref, size.half, tile_of(whole_ref, 2), tile_of(whole_ref, 3), kv_ref
    )


def bridge(size, place, weights, near, source_near, source_far, mixed):
    width = near.shape[2]
    return kernel_call(
        functools.partial(bridge_kernel, size),
        out_shape=(
            shape((size.own, width)),
            shape((size.length, 2 * width)),
            shape((6, 2 * size.x_count * size.pieces, size.tile_rows, width)),
            shape((size.own, width), F32),
            shape((size.own, 1), F32),
            shape((8, width), F32),
        ),
        in_specs=[SMEM, ANY, ANY] + [VMEM] * 4,
        out_specs=(VMEM,) * 6,
        scratch_shapes=[pltpu.SemaphoreType.DMA((2 * size.x_count * 6,))],
    )(place, *weights, near, source_near, source_far, mixed)


def feed_kernel(
    size,
    place_ref,
    w_near_ref,
    w_far_ref,
    mixed_ref,
    whole_two_ref,
    hat_one_ref,
    norm_ref,
    cot_ref,
    out_ref,
    d_two_ref,
    d_mixed_ref,
    sums_ref,
    low_t_ref,
    dz_ref,
    hid_ref,
    down_ref,
    mixed_t_ref,
    w_in_ref,
    w_out_ref,
    z_ref,
    low_ref,
    hat_two_ref,
    inv_two_ref,
    sem,
):
    own, width = hat_one_ref.shape
    hidden = z_ref.shape[1]
    tiles = hidden // width
    tile_rows = size.tile_rows
    copies = []
    for e, part in enumerate((w_near_ref, w_far_ref)):
        pieces, total = part.shape[0], part.shape[1] // size.x_count
        for k in range(size.x_count):
            dp = (place_ref[0] ^ k) * 2 + (place_ref[1] ^ e)
            at = pl.ds(pl.multiple_of(dp * pieces, pieces), pieces)
            for t in range(tiles):
                source = part.at[:, pl.ds(k * total + t * tile_rows, tile_rows)]
                copies.append(pltpu.make_async_copy(source, w_in_ref.at[t, at], sem.at[len(copies)]))
            source = part.at[:, pl.ds(k * total + tiles * tile_rows, total - tiles * tile_rows)]
            copies.append(pltpu.make_async_copy(source, w_out_ref.at[at], sem.at[len(copies)]))
    for copy in copies:
        copy.start()
    mixed_t_ref[...] = jnp.transpose(mixed_ref[...])
    sums_ref[...] = jnp.zeros(sums_ref.shape, F32)
    cross_out = whole_two_ref[4]
    for copy in copies:
        copy.wait()
    per_tile = w_out_ref.shape[0] // tiles

    def w_down(t):
        return w_out_ref[t * per_tile : (t + 1) * per_tile].reshape(width, width)

    def forward(i, carry):
        at = chunk(i)
        one = hat_one_ref[at, :] * norm_ref[0:1, :] + norm_ref[1:2, :]
        hat, inv = norm_of(one + dot_f32(mixed_ref[at, :], cross_out))
        hat_two_ref[at, :] = hat
        inv_two_ref[at, :] = inv
        two = hat * norm_ref[2:3, :] + norm_ref[3:4, :]
        low = two.astype(BF)
        low_ref[at, :] = low
        total = two
        for t in range(tiles):
            cols = slice(t * width, (t + 1) * width)
            z = dot_f32(low, tile_of(w_in_ref, t))
            z_ref[at, cols] = z
            turn = jnp.tanh(GELU_A * (z + GELU_B * (z * z * z)))
            hid = (0.5 * z * (1.0 + turn)).astype(BF)
            hid_ref[at, cols] = hid
            total = total + dot_f32(hid, w_down(t))
        hat, inv = norm_of(total)
        gain = norm_ref[4:5, :]
        out_ref[at, :] = (hat * gain + norm_ref[5:6, :]).astype(BF)
        upstream = sequence_rows(cot_ref, i, size.half).astype(F32)
        sums_ref[4:5, :] += jnp.sum(upstream * hat, axis=0, keepdims=True)
        sums_ref[5:6, :] += jnp.sum(upstream, axis=0, keepdims=True)
        down = norm_pull(upstream, hat, inv, gain)
        low_down = down.astype(BF)
        down_ref[at, :] = low_down
        back = down
        for t in range(tiles):
            cols = slice(t * width, (t + 1) * width)
            d_hid = dot_nt(low_down, w_down(t))
            z = z_ref[at, cols]
            turn = jnp.tanh(GELU_A * (z + GELU_B * (z * z * z)))
            slope = 0.5 * (1.0 + turn) + (0.5 * GELU_A) * z * (1.0 - turn * turn) * (1.0 + (3.0 * GELU_B) * z * z)
            dz = (d_hid * slope).astype(BF)
            dz_ref[at, cols] = dz
            back = back + dot_nt(dz, tile_of(w_in_ref, t))
        hat, inv = hat_two_ref[at, :], inv_two_ref[at, :]
        sums_ref[2:3, :] += jnp.sum(back * hat, axis=0, keepdims=True)
        sums_ref[3:4, :] += jnp.sum(back, axis=0, keepdims=True)
        d_two = norm_pull(back, hat, inv, norm_ref[2:3, :])
        d_two_ref[at, :] = d_two
        d_mixed_ref[at, :] = dot_nt(d_two.astype(BF), cross_out).astype(BF)
        return carry

    lax.fori_loop(0, own // CHUNK, forward, 0)
    low_t_ref[...] = jnp.transpose(low_ref[...])


def feed(size, place, weights, mixed, whole_two, hat_one, norms, cot):
    own, width = hat_one.shape
    hidden = size.hidden
    devices = 2 * size.x_count * size.pieces
    return kernel_call(
        functools.partial(feed_kernel, size),
        out_shape=(
            shape((own, width)),
            shape((own, width), F32),
            shape((own, width)),
            shape((8, width), F32),
            shape((width, own)),
            shape((own, hidden)),
            shape((own, hidden)),
            shape((own, width)),
            shape((width, own)),
        ),
        in_specs=[SMEM, ANY, ANY] + [VMEM] * 5,
        out_specs=(VMEM,) * 9,
        scratch_shapes=[
            pltpu.VMEM((hidden // width, devices, size.tile_rows, width), BF),
            pltpu.VMEM((devices, hidden // devices, width), BF),
            pltpu.VMEM((own, hidden), F32),
            pltpu.VMEM((own, width), BF),
            pltpu.VMEM((own, width), F32),
            pltpu.VMEM((own, 1), F32),
            pltpu.SemaphoreType.DMA((2 * size.x_count * (hidden // width + 1),)),
        ],
    )(place, *weights, mixed, whole_two, hat_one, norms, cot)


def feed_grads_kernel(
    size, e, place_ref, low_t_ref, dz_ref, hid_ref, down_ref, mixed_t_ref, d_two_ref, target
):
    width = low_t_ref.shape[0]
    hidden = dz_ref.shape[1]
    tiles = hidden // width
    lefts = grad_rows(place_ref, low_t_ref, 2 * size.x_count, e)
    for t in range(tiles):
        put_grad(target, dot_f32(lefts, dz_ref[:, t * width : (t + 1) * width]), t, size.tile_rows)
    value = dot_f32(grad_rows(place_ref, mixed_t_ref, 2 * size.x_count, e), d_two_ref[...].astype(BF))
    put_grad(target, value, tiles, size.tile_rows)
    rows = hidden // (2 * size.x_count)
    for k in range(size.x_count):
        dp = (place_ref[0] ^ k) * 2 + (place_ref[1] ^ e)
        cols = pl.ds(pl.multiple_of(dp * rows, rows), rows)
        value = dot_f32(jnp.transpose(hid_ref[:, cols]), down_ref[...]).astype(target.dtype)
        target[k, :, (tiles + 1) * size.tile_rows :, :] = value.reshape(size.pieces, rows // size.pieces, width)


def feed_grads(size, e, place, low_t, dz, hid, down, mixed_t, d_two):
    width = low_t.shape[0]
    tiles = size.hidden // width
    rows = (tiles + 1) * size.tile_rows + size.hidden // (2 * size.x_count * size.pieces)
    return kernel_call(
        functools.partial(feed_grads_kernel, size, e),
        out_shape=shape((size.x_count, size.pieces, rows, width)),
        in_specs=[SMEM] + [VMEM] * 6,
        out_specs=VMEM,
    )(place, low_t, dz, hid, down, mixed_t, d_two)


def back_pairs(size, d_kv_ref, w_k, w_v, kept_ref, send_ref):
    width = w_k.shape[1]
    count = size.length // (2 * CHUNK)
    for e, target in enumerate((kept_ref, send_ref)):

        def step(i, carry):
            at = chunk(i + e * count)
            value = dot_nt(d_kv_ref[at, :width], w_k) + dot_nt(d_kv_ref[at, width:], w_v)
            target[chunk(i), :] = value.astype(target.dtype)
            return carry

        lax.fori_loop(0, count, step, 0)


def turn_rows(size, near_ref, far_ref, left_ref):
    count = size.length // (2 * CHUNK)
    for e, ref in enumerate((near_ref, far_ref)):

        def step(i, carry):
            left_ref[:, chunk(i + e * count)] = jnp.transpose(sequence_rows(ref, i, size.half))
            return carry

        lax.fori_loop(0, count, step, 0)


def back_cross_kernel(
    size,
    place_ref,
    d_kv_ref,
    d_q_ref,
    whole_ref,
    hat_ref,
    inv_ref,
    norm_ref,
    d_two_ref,
    sums_in_ref,
    kept_rows_ref,
    send_rows_ref,
    d_one_ref,
    d_mixed_ref,
    sums_ref,
    low_t_ref,
):
    hat, inv, gain = hat_ref[...], inv_ref[...], norm_ref[0:1, :]
    upstream = d_two_ref[...] + dot_nt(d_q_ref[...], whole_ref[1])
    sums_ref[...] = sums_in_ref[...]
    sums_ref[0:1, :] = jnp.sum(upstream * hat, axis=0, keepdims=True)
    sums_ref[1:2, :] = jnp.sum(upstream, axis=0, keepdims=True)
    d_one = norm_pull(upstream, hat, inv, gain)
    d_one_ref[...] = d_one
    d_mixed_ref[...] = dot_nt(d_one.astype(BF), whole_ref[0]).astype(BF)
    low_t_ref[...] = jnp.transpose((hat * gain + norm_ref[1:2, :]).astype(BF))
    back_pairs(size, d_kv_ref, whole_ref[2], whole_ref[3], kept_rows_ref, send_rows_ref)


def back_cross(size, place, d_kv, d_q, whole, hat, inv, norms, d_two, sums):
    own, width = hat.shape
    return kernel_call(
        functools.partial(back_cross_kernel, size),
        out_shape=(
            shape((size.length // 2, width)),
            shape((size.length // 2, width)),
            shape((own, width), F32),
            shape((own, width)),
            shape((8, width), F32),
            shape((width, own)),
        ),
        in_specs=[SMEM] + [VMEM] * 8,
        out_specs=(VMEM,) * 6,
    )(place, d_kv, d_q, whole, hat, inv, norms, d_two, sums)


def cross_grads_kernel(
    size,
    place_ref,
    near_ref,
    far_ref,
    d_kv_ref,
    d_q_ref,
    low_t_ref,
    mixed_self_ref,
    d_one_ref,
    sums_ref,
    kept_ref,
    send_ref,
    left_ref,
    self_t_ref,
    cols_ref,
):
    width = d_one_ref.shape[1]
    dp_count = 2 * size.x_count
    self_t_ref[...] = jnp.transpose(mixed_self_ref[...])
    pad = jnp.zeros((128 - sums_ref.shape[0], width), F32)
    cols_ref[...] = jnp.zeros(cols_ref.shape, F32)
    cols_ref[:, :128] = jnp.transpose(jnp.concatenate([sums_ref[...], pad], axis=0))
    turn_rows(size, near_ref, far_ref, left_ref)
    for e, target in enumerate((kept_ref, send_ref)):
        value = dot_f32(grad_rows(place_ref, self_t_ref, dp_count, e), d_one_ref[...].astype(BF))
        put_grad(target, value, 0, size.tile_rows)
        put_grad(target, dot_f32(grad_rows(place_ref, low_t_ref, dp_count, e), d_q_ref[...]), 1, size.tile_rows)
        lefts = grad_rows(place_ref, left_ref, dp_count, e)
        for t in range(2):
            put_grad(target, dot_f32(lefts, d_kv_ref[:, t * width : (t + 1) * width]), 2 + t, size.tile_rows)
        put_grad(target, grad_rows(place_ref, cols_ref, dp_count, e), 4, size.tile_rows)


def cross_grads(size, place, near, far, d_kv, d_q, low_t, mixed_self, d_one, sums):
    own, width = d_one.shape
    group = (size.x_count, size.pieces, 5 * size.tile_rows, width)
    return kernel_call(
        functools.partial(cross_grads_kernel, size),
        out_shape=(shape(group), shape(group)),
        in_specs=[SMEM] + [VMEM] * 8,
        out_specs=(VMEM,) * 2,
        scratch_shapes=[
            pltpu.VMEM((width, size.length), BF),
            pltpu.VMEM((width, own), BF),
            pltpu.VMEM((width, width), F32),
        ],
    )(place, near, far, d_kv, d_q, low_t, mixed_self, d_one, sums)


def self_grads_kernel(size, place_ref, near_ref, far_ref, d_kv_ref, d_q_ref, kept_ref, send_ref, left_ref, own_t_ref):
    width = d_q_ref.shape[1]
    dp_count = 2 * size.x_count
    turn_rows(size, near_ref, far_ref, left_ref)
    own_t_ref[...] = jnp.transpose(own_tokens(near_ref, place_ref, size.half, size.z_count))
    for e, target in enumerate((kept_ref, send_ref)):
        put_grad(target, dot_f32(grad_rows(place_ref, own_t_ref, dp_count, e), d_q_ref[...]), 0, size.tile_rows)
        lefts = grad_rows(place_ref, left_ref, dp_count, e)
        for t in range(2):
            put_grad(target, dot_f32(lefts, d_kv_ref[:, t * width : (t + 1) * width]), 1 + t, size.tile_rows)


def self_grads(size, place, near, far, d_kv, d_q):
    own, width = d_q.shape
    group = (size.x_count, size.pieces, 3 * size.tile_rows, width)
    return kernel_call(
        functools.partial(self_grads_kernel, size),
        out_shape=(shape(group), shape(group)),
        in_specs=[SMEM] + [VMEM] * 4,
        out_specs=(VMEM,) * 2,
        scratch_shapes=[pltpu.VMEM((width, size.length), BF), pltpu.VMEM((width, own), BF)],
    )(place, near, far, d_kv, d_q)


def back_self_kernel(size, place_ref, d_kv_ref, d_q_ref, whole_ref, d_one_ref, kept_rows_ref, send_rows_ref):
    back_pairs(size, d_kv_ref, whole_ref[1], whole_ref[2], kept_rows_ref, send_rows_ref)
    mine = d_one_ref[...] + dot_nt(d_q_ref[...], whole_ref[0])
    half = size.half
    y_count = size.length // (2 * half * size.z_count)
    for z in range(size.z_count):
        at = pl.ds(pl.multiple_of((z * y_count + place_ref[3]) * half, half), half)
        total = kept_rows_ref[at, :].astype(F32) + mine[z * half : (z + 1) * half]
        kept_rows_ref[at, :] = total.astype(kept_rows_ref.dtype)


def back_self(size, place, d_kv, d_q, whole, d_one):
    width = d_one.shape[1]
    return kernel_call(
        functools.partial(back_self_kernel, size),
        out_shape=(shape((size.length // 2, width)), shape((size.length // 2, width))),
        in_specs=[SMEM] + [VMEM] * 4,
        out_specs=(VMEM,) * 2,
    )(place, d_kv, d_q, whole, d_one)


def together(*values):
    return lax.optimization_barrier(values)


def unxor(parts, place):
    if len(parts) == 2:
        return jnp.where(place == 0, jnp.stack(parts), jnp.stack(parts[::-1]))
    out = jnp.zeros((len(parts),) + parts[0].shape, parts[0].dtype)
    for k, part in enumerate(parts):
        out = lax.dynamic_update_index_in_dim(out, part, place ^ k, 0)
    return out


def body(
    inputs,
    encoder,
    tgt_seg,
    src_len,
    cotangent,
    self_in,
    self_out,
    cross_q,
    cross_kv,
    cross_out,
    ffn_in,
    ffn_out,
    norm_params,
):
    held, local_rows, width = inputs.shape
    half = local_rows // 2
    dp_count, seq_count = lax.axis_size("dp"), lax.axis_size("seq")
    length = local_rows * seq_count
    x_count = dp_count // 2
    z_count = 2 * held
    y_count = seq_count // z_count
    dp_place, seq_place = lax.axis_index("dp"), lax.axis_index("seq")
    x_place, c_place = dp_place // 2, dp_place % 2
    z_place, y_place = seq_place // y_count, seq_place % y_count
    place = jnp.stack([x_place, c_place, z_place, y_place]).astype(jnp.int32)
    rows = self_in.shape[0]
    fine = rows % 16 == 0
    pieces = seq_count if fine else 1
    tile_rows = rows * seq_count // pieces

    def over_core(v):
        return lax.ppermute(v, "dp", [(i, i ^ 1) for i in range(dp_count)])

    def over_x(v, k):
        return v if k == 0 else lax.ppermute(v, "dp", [(i, i ^ (2 * k)) for i in range(dp_count)])

    def over_y(v, k):
        return v if k == 0 else lax.ppermute(v, "seq", [(i, i ^ k) for i in range(seq_count)])

    def over_z(v, k):
        return v if k == 0 else lax.ppermute(v, "seq", [(i, i ^ (k * y_count)) for i in range(seq_count)])

    def pick(v, at, axis=0):
        return lax.dynamic_index_in_dim(v, at, axis, keepdims=False)

    def by_core(mine, other, axis=0):
        return jnp.where(
            c_place == 0, jnp.concatenate([mine, other], axis=axis), jnp.concatenate([other, mine], axis=axis)
        )

    def exchange(v):
        return lax.all_to_all(v, "seq", 0, 0, tiled=True)

    def exchange_z(v):
        groups = [[z * y_count + y for z in range(z_count)] for y in range(y_count)]
        return lax.all_to_all(v, "seq", 0, 0, tiled=True, axis_index_groups=groups)

    def tiles_of(v):
        return v.reshape(rows, -1, width).transpose(1, 0, 2).reshape(-1, width)

    def y_gather(v):
        return y_order(y_moves(v))

    def y_moves(v):
        return [over_y(v, k) for k in range(y_count)]

    def y_order(moves):
        return unxor(moves, y_place).swapaxes(0, 1).reshape((seq_count,) + moves[0].shape[1:])

    def with_weights(blocks, weights):
        weights = weights.reshape(-1, width)
        return jnp.concatenate([blocks, jnp.broadcast_to(weights, (z_count,) + weights.shape)], axis=1)

    def coarse_parts(v, outer):
        whole = lax.all_gather(v, ("dp", "seq"), axis=0).reshape((x_count, 2, seq_count) + v.shape)
        inner = whole[:, :, :, : v.shape[0] - outer].reshape(x_count, 2, seq_count, -1, rows, width)
        inner = inner.swapaxes(2, 3).reshape(x_count, 2, -1, width)
        whole = jnp.concatenate([inner, whole[:, :, :, v.shape[0] - outer :].reshape(x_count, 2, -1, width)], axis=2)
        out = []
        for e in range(2):
            mine = pick(whole, c_place ^ e, 1)
            out.append(jnp.concatenate([pick(mine, x_place ^ k) for k in range(x_count)])[None])
        return out

    def x_sum(kept, came):
        total = kept[0].astype(F32) + came[0]
        for k in range(1, x_count):
            total = total + over_x((kept[k].astype(F32) + came[k]).astype(BF), k)
        return total

    def by_owner(v, outer):
        if fine:
            return v
        inner = v[0, : v.shape[1] - outer].reshape(-1, seq_count, rows, width).swapaxes(0, 1)
        inner = inner.reshape(seq_count, -1, width)
        return jnp.concatenate([inner, v[0, v.shape[1] - outer :].reshape(seq_count, -1, width)], axis=1)

    def y_sum(v):
        v = v.reshape((z_count, y_count) + v.shape[1:])
        total = pick(v, y_place, 1)
        for k in range(1, y_count):
            total = total + over_y(pick(v, y_place ^ k, 1).astype(BF), k)
        return total

    def untiled(v):
        return v.reshape(-1, rows, width).transpose(1, 0, 2).reshape(rows, -1)

    def home(v):
        v = v.astype(BF).reshape(2, held, half, width)
        mine, other = pick(v, c_place), over_core(pick(v, 1 - c_place))
        mine, other = mine[:, None], other[:, None]
        return by_core(mine, other, 1).reshape(held, local_rows, width).astype(F32)

    notes = jnp.concatenate([tgt_seg, src_len], axis=1)
    notes = pick(by_core(notes, over_core(notes)), z_place)
    target_all, lengths = notes[:length], notes[length:]
    docs = lengths.shape[0]
    upto = lax.broadcasted_iota(jnp.int32, (docs, docs), 0) <= lax.broadcasted_iota(jnp.int32, (docs, docs), 1)
    ends = jnp.sum(jnp.where(upto, lengths[:, None], 0), axis=0, dtype=jnp.int32)
    positions = jnp.arange(length, dtype=jnp.int32)
    source_all = jnp.sum((positions[:, None] >= ends[None, :]).astype(jnp.int32), axis=1, dtype=jnp.int32)
    qseg = pick(target_all.reshape(z_count, y_count * 2, half), y_place * 2 + c_place, 1)
    keys = 2 * half

    def in_order(segments):
        pairs = segments.reshape(-1, 2, half)
        return jnp.where(c_place == 0, pairs, pairs[:, ::-1]).reshape(-1, keys)

    def visits(segments):
        low = jnp.sum((segments[None, :] < qseg[:, :1]).astype(jnp.int32), axis=1, dtype=jnp.int32)
        high = jnp.sum((segments[None, :] <= qseg[:, -1:]).astype(jnp.int32), axis=1, dtype=jnp.int32)
        table = jnp.stack([low // keys, (high + keys - 1) // keys])
        return jnp.pad(table, ((0, 0), (0, length // keys - z_count)))

    self_kseg, cross_kseg = in_order(target_all), in_order(source_all)
    self_visits, cross_visits = visits(target_all), visits(source_all)

    hidden = ffn_in.shape[1]
    outer = ffn_out.shape[0]
    norm_wide = jnp.pad(norm_params, ((0, 0), (0, width - norm_params.shape[1])))
    first_tiles = tiles_of(self_in)
    rest_tiles = tiles_of(jnp.concatenate([self_out, cross_q, cross_kv, cross_out, norm_wide, ffn_in], axis=1))
    rest_tiles = jnp.concatenate([rest_tiles, ffn_out], axis=0)
    mid = 6 * rows
    size = Size(
        half=half,
        length=length,
        own=z_count * half,
        z_count=z_count,
        x_count=x_count,
        pieces=pieces,
        tile_rows=tile_rows,
        hidden=hidden,
        first=half if fine else 0,
    )
    streams = jnp.stack([inputs, encoder, cotangent]).reshape(3, held, 2, half, width)
    mine = pick(streams, c_place, 2)
    other = over_core(pick(streams, 1 - c_place, 2))
    streams = by_core(mine, other, 1)
    x_blocks, source_blocks, cot = streams[0], streams[1], streams[2]
    if fine:
        w1 = jnp.stack([over_x(first_tiles, k) for k in range(x_count)])
        rest = jnp.stack([over_x(rest_tiles, k) for k in range(x_count)])
        x_blocks = with_weights(x_blocks, w1)
        source_blocks = with_weights(source_blocks, rest[:, :mid])
        cot = with_weights(cot, rest[:, mid:])
    x_near = exchange_z(x_blocks)
    x_near, source_blocks = together(x_near, source_blocks)
    x_near = y_gather(x_near)
    source_near = exchange_z(source_blocks)
    x_far = over_core(x_near)
    weights = (x_near, x_far) if fine else coarse_parts(first_tiles, 0)

    queries, pairs, whole_one = project(size, place, weights, x_near, x_far)
    whole_one = whole_one.reshape(3, width, width)
    queries, source_near, cot = together(queries, source_near, cot)
    source_near = y_gather(source_near)
    cot = exchange_z(cot)
    mixed_self, self_lse = attend(self_visits, queries, pairs, qseg, self_kseg)
    mixed_self, source_near, cot = together(mixed_self, source_near, cot)
    source_far = over_core(source_near)
    mixed_self, source_far = together(mixed_self, source_far)
    w3 = y_moves(cot[:, half:]) if fine else None
    weights = (source_near, source_far) if fine else coarse_parts(rest_tiles[:mid], 0)
    queries_c, pairs_c, whole_two, hat_one, inv_one, norms = bridge(
        size, place, weights, x_near, source_near, source_far, mixed_self
    )
    whole_two = whole_two.reshape(6, width, width)
    mixed_cross, cross_lse = attend(cross_visits, queries_c, pairs_c, qseg, cross_kseg)
    if fine:
        mixed_cross, w3 = together(mixed_cross, w3)
        w3 = y_order(w3)
        weights = (w3, over_core(w3))
    else:
        weights = coarse_parts(rest_tiles[mid:], outer)
    out_low, d_two, d_mixed_c, sums, low_t, dz, hid, down, mixed_ct = feed(
        size, place, weights, mixed_cross, whole_two, hat_one, norms, cot
    )

    out_parts = exchange_z(out_low.reshape(z_count, half, width))
    f_send = feed_grads(size, 1, place, low_t, dz, hid, down, mixed_ct, d_two)
    f_came = over_core(f_send)
    low_t, f_send = together(low_t, f_send)
    f_kept = feed_grads(size, 0, place, low_t, dz, hid, down, mixed_ct, d_two)
    d_mixed_c, f_kept, f_came = together(d_mixed_c, f_kept, f_came)
    f_sum = x_sum(f_kept, f_came)
    d_queries_c, d_pairs_c = attend_back(
        cross_visits, queries_c, d_mixed_c, mixed_cross, cross_lse, pairs_c, qseg, cross_kseg
    )
    s_kept, s_send, d_one, d_mixed, sums, low_one_t = back_cross(
        size, place, d_pairs_c, d_queries_c, whole_two, hat_one, inv_one, norms, d_two, sums
    )
    d_one, f_sum, s_send, s_kept, out_parts = together(d_one, f_sum, s_send, s_kept, out_parts)
    s_came = over_core(s_send)
    f_sum = y_sum(by_owner(f_sum, hidden // dp_count))
    c_kept, c_send = cross_grads(
        size, place, source_near, source_far, d_pairs_c, d_queries_c, low_one_t, mixed_self, d_one, sums
    )
    d_mixed, s_came, c_send, f_sum = together(d_mixed, s_came, c_send, f_sum)
    c_came = over_core(c_send)
    s_sum = y_sum((s_kept.astype(F32) + s_came).reshape(seq_count, half, width))
    f_sum = exchange_z(f_sum.astype(BF))
    d_queries, d_pairs = attend_back(
        self_visits, queries, d_mixed, mixed_self, self_lse, pairs, qseg, self_kseg
    )
    d_pairs, s_sum, c_came, f_sum = together(d_pairs, s_sum, c_came, f_sum)
    s_parts = exchange_z(s_sum.astype(BF))
    c_sum = x_sum(c_kept, c_came)
    x_kept, x_send = back_self(size, place, d_pairs, d_queries, whole_one, d_one)
    x_came = over_core(x_send)
    d_pairs, x_send = together(d_pairs, x_send)
    i_kept, i_send = self_grads(size, place, x_near, x_far, d_pairs, d_queries)
    i_came = over_core(i_send)
    x_came, x_kept, i_send, s_parts = together(x_came, x_kept, i_send, s_parts)
    x_total = (x_kept.astype(F32) + x_came).astype(BF)
    x_parts = exchange(x_total.reshape(seq_count, half, width))
    x_total, i_came, i_kept = together(x_total, i_came, i_kept)
    i_sum = x_sum(i_kept, i_came)
    i_kept, s_parts, out_parts, f_sum = together(i_kept, s_parts, out_parts, f_sum)
    grad_source = home(s_parts)
    out_tokens = home(out_parts)
    f_own = jnp.sum(f_sum.astype(F32), axis=0)
    w_sum = y_sum(jnp.concatenate([by_owner(c_sum, 0), by_owner(i_sum, 0)], axis=1))
    w_own = pick(w_sum, z_place)
    for k in range(1, z_count):
        w_own = w_own + over_z(pick(w_sum, z_place ^ k).astype(BF), k)
    c_own, i_own = w_own[: 5 * rows], w_own[5 * rows :]
    grad_tokens = home(jnp.sum(x_parts.reshape(z_count, y_count, half, width).astype(F32), axis=1))
    f_in = hidden // width * rows
    c_own = c_own.reshape(5, rows, width)
    return (
        out_tokens,
        grad_tokens,
        grad_source,
        untiled(i_own),
        c_own[0],
        c_own[1],
        untiled(c_own[2:4]),
        f_own[f_in : f_in + rows],
        untiled(f_own[:f_in]),
        f_own[f_in + rows :],
        c_own[4][:, : norm_params.shape[1]],
    )


def solution(mesh):
    tokens, rows = P("dp", "seq", None), P(("dp", "seq"), None)
    return jax.shard_map(
        body,
        mesh=mesh,
        in_specs=(tokens, tokens, P("dp", None), P("dp", None), tokens) + (rows,) * 8,
        out_specs=(tokens,) * 3 + (rows,) * 8,
        check_vma=False,
    )
```

profile of v0, /device:TPU:0, one launch (start us, length us, event | category | flops | bytes accessed | tf_op | source)
XLA Modules:
  0.0 353.1 jit_solution(9750316350893564695)
XLA Ops:
  3.1 3.0 collective-permute-start.2
  12.7 5.5 %all-to-all-start = ((bf16[4,224,512]{2,1,0:T(8,128)(2,1)}), bf16[4,224,512]{2,1,0:T(8,128)(2,1)S(1)}, u32[]{:S(2)}, u32[]{:S(2)}) async-start(bf16[4,224,512]{2,1,0:T(8,128)(2,1)} %pad_maximum_fusion.4), calls=%async_computation | async-start | bytes 1835008 | tf_op jit(solution)/shard_map/all_to_all | solution.py:826
  20.1 4.6 %collective-permute-done.3 = bf16[224,512]{1,0:T(8,128)(2,1)S(1)} collective-permute-done((bf16[224,512]{1,0:T(8,128)(2,1)S(1)}, bf16[224,512]{1,0:T(8,128)(2,1)S(1)}, u32[]{:S(2)}, u32[]{:S(2)}) %collective-permute-start.3) | collective-permute-done | bytes 229408 | tf_op jit(solution)/shard_map/ppermute | solution.py:805
  25.9 14.2 %all-to-all-done = bf16[4,224,512]{2,1,0:T(8,128)(2,1)S(1)} async-done(((bf16[4,224,512]{2,1,0:T(8,128)(2,1)}), bf16[4,224,512]{2,1,0:T(8,128)(2,1)S(1)}, u32[]{:S(2)}, u32[]{:S(2)}) %all-to-all-start) | async-done | bytes 917536 | tf_op jit(solution)/shard_map/all_to_all | solution.py:826
  41.6 3.5 %all-to-all-start.1 = ((bf16[4,320,512]{2,1,0:T(8,128)(2,1)}), bf16[4,320,512]{2,1,0:T(8,128)(2,1)S(1)}, u32[]{:S(2)}, u32[]{:S(2)}) async-start(bf16[4,320,512]{2,1,0:T(8,128)(2,1)} %pad_maximum_fusion.3), calls=%async_computation.1 | async-start | bytes 2621440 | tf_op jit(solution)/shard_map/all_to_all | solution.py:826
  45.2 16.2 %collective-permute-done.4 = bf16[4,224,512]{2,1,0:T(8,128)(2,1)S(1)} collective-permute-done((bf16[4,224,512]{2,1,0:T(8,128)(2,1)S(1)}, bf16[4,224,512]{2,1,0:T(8,128)(2,1)S(1)}, u32[]{:S(2)}, u32[]{:S(2)}) %collective-permute-start.4) | collective-permute-done | bytes 917536 | tf_op jit(solution)/shard_map/ppermute | solution.py:808
  65.8 7.0 %shard_map.212 = (bf16[512,512]{1,0:T(8,128)(2,1)S(1)}, bf16[2048,1024]{1,0:T(8,128)(2,1)S(1)}, bf16[3,32,16,512]{3,2,1,0:T(8,128)(2,1)S(1)}) custom-call(s32[4]{0:T(128)S(1)} %pad_add_fusion.2.place_ref, bf16[8,224,512]{2,1,0:T(8,128)(2,1)S(1)} %bitcast.187, bf16[8,224,512]{2,1,0:T(8,128)(2,1)} %collective-permute-done.5.w_far_ref.far_ref, ...), custom_call_target="tpu_custom_call" | custom-call | flops 1000000 | bytes 1024 | tf_op jit(solution)/shard_map/pallas_call | solution.py:51
  78.0 3.7 %all-to-all-start.2 = ((bf16[4,384,512]{2,1,0:T(8,128)(2,1)}), bf16[4,384,512]{2,1,0:T(8,128)(2,1)S(1)}, u32[]{:S(2)}, u32[]{:S(2)}) async-start(bf16[4,384,512]{2,1,0:T(8,128)(2,1)} %pad_maximum_fusion.2), calls=%async_computation.2 | async-start | bytes 3145728 | tf_op jit(solution)/shard_map/all_to_all | solution.py:826
  91.3 10.3 %shard_map.213 = (bf16[512,512]{1,0:T(8,128)(2,1)S(1)}, f32[8,1,512]{2,1,0:T(1,128)S(1)}) custom-call(s32[2,8]{1,0:T(2,128)S(1)} %pad.11.visit_ref, bf16[512,512]{1,0:T(8,128)(2,1)S(1)} %copy-done.30, bf16[2048,1024]{1,0:T(8,128)(2,1)S(1)} %copy-done.5, s32[4,1,128]{2,1,0:T(1,128)S(1)} %constant_dynamic-slice_fusion.qseg_ref, s32[2048,1]{1,0:T(8,128)S(1)} %copy-done.18), custom_call_target="tpu_custom_call" | custom-call | flops 1000000 | bytes 1024 | tf_op jit(solution)/shard_map/pallas_call | solution.py:51
  102.3 12.0 %collective-permute-done.6 = bf16[4,320,512]{2,1,0:T(8,128)(2,1)} collective-permute-done((bf16[4,320,512]{2,1,0:T(8,128)(2,1)}, bf16[4,320,512]{2,1,0:T(8,128)(2,1)}, u32[]{:S(2)}, u32[]{:S(2)}) %collective-permute-start.6) | collective-permute-done | bytes 1310752 | tf_op jit(solution)/shard_map/ppermute | solution.py:808
  114.4 3.4 maximum_select_fusion
  127.1 8.4 %shard_map.214 = (bf16[512,512]{1,0:T(8,128)(2,1)S(1)}, bf16[2048,1024]{1,0:T(8,128)(2,1)S(1)}, bf16[6,32,16,512]{3,2,1,0:T(8,128)(2,1)S(1)}, f32[512,512]{1,0:T...) custom-call(s32[4]{0:T(128)S(1)} %pad_add_fusion.2.place_ref, bf16[8,320,512]{2,1,0:T(8,128)(2,1)S(1)} %bitcast.192, ...), custom_call_target="tpu_custom_call" | custom-call | flops 1000000 | bytes 1024 | tf_op jit(solution)/shard_map/pallas_call | solution.py:51
  136.3 7.7 %shard_map.215 = (bf16[512,512]{1,0:T(8,128)(2,1)S(1)}, f32[8,1,512]{2,1,0:T(1,128)S(1)}) custom-call(s32[2,8]{1,0:T(2,128)S(1)} %pad.13.visit_ref, bf16[512,512]{1,0:T(8,128)(2,1)S(1)} %get-tuple-element.100.q_ref, bf16[2048,1024]{1,0:T(8,128)(2,1)S(1)} %get-tuple-element.101.kv_ref, s32[4,1,128]{2,1,0:T(1,128)S(1)} %constant_dynamic-slice_fusion.qseg_ref, ...), custom_call_target="tpu_custom_call" | custom-call | flops 1000000 | bytes 1024 | tf_op jit(solution)/shard_map/pallas_call | solution.py:51
  148.8 4.1 %collective-permute-done.9.w_far_ref = bf16[8,256,512]{2,1,0:T(8,128)(2,1)S(1)} collective-permute-done((bf16[8,256,512]{2,1,0:T(8,128)(2,1)S(1)}, bf16[8,256,512]{2,1,0:T(8,128)(2,1)S(1)}, u32[]{:S(2)}, u32[]{:S(2)}) %collective-permute-start.9) | collective-permute-done | bytes 2097184 | tf_op jit(solution)/shard_map/ppermute | solution.py:802
  153.0 11.0 %shard_map.216 = (bf16[512,512]{1,0:T(8,128)(2,1)S(1)}, f32[512,512]{1,0:T(8,128)S(1)}, bf16[512,512]{1,0:T(8,128)(2,1)S(1)}, f32[8,512]{1,0:T(8,128)S(1)}, bf16...) custom-call(s32[4]{0:T(128)S(1)} %pad_add_fusion.2.place_ref, ...), custom_call_target="tpu_custom_call" | custom-call | flops 1000000 | bytes 1024 | tf_op jit(solution)/shard_map/pallas_call | solution.py:51
  173.9 4.1 %all-to-all-start.3 = ((bf16[4,128,512]{2,1,0:T(8,128)(2,1)}), bf16[4,128,512]{2,1,0:T(8,128)(2,1)}, u32[]{:S(2)}, u32[]{:S(2)}) async-start(bf16[4,128,512]{2,1,0:T(8,128)(2,1)} %bitcast.200), calls=%async_computation.3 | async-start | bytes 1048576 | tf_op jit(solution)/shard_map/all_to_all | solution.py:826
  182.3 12.7 %shard_map.219 = (bf16[512,512]{1,0:T(8,128)(2,1)S(1)}, bf16[2048,1024]{1,0:T(8,128)(2,1)S(1)}) custom-call(s32[2,8]{1,0:T(2,128)S(1)} %pad.13.visit_ref, bf16[512,512]{1,0:T(8,128)(2,1)S(1)} %copy-done.33, bf16[512,512]{1,0:T(8,128)(2,1)S(1)} %copy-done.51, bf16[512,512]{1,0:T(8,128)(2,1)S(1)} %copy-done.37, f32[8,1,512]{2,1,0:T(1,128)S(1)} %get-tuple-element.119.lse_ref, ...), custom_call_target="tpu_custom_call" | custom-call | flops 1000000 | bytes 1024 | tf_op jit(solution)/shard_map/pallas_call | solution.py:51
  195.1 5.6 %shard_map.220 = (bf16[1024,512]{1,0:T(8,128)(2,1)S(1)}, bf16[1024,512]{1,0:T(8,128)(2,1)S(1)}, f32[512,512]{1,0:T(8,128)S(1)}, bf16[512,512]{1,0:T(8,128)(2,1)S...) custom-call(s32[4]{0:T(128)S(1)} %pad_add_fusion.2.place_ref, ...), custom_call_target="tpu_custom_call" | custom-call | flops 1000000 | bytes 1024 | tf_op jit(solution)/shard_map/pallas_call | solution.py:51
  204.3 3.2 bitcast_add_fusion
  218.0 7.2 %shard_map.221 = (bf16[2,8,80,512]{3,2,1,0:T(8,128)(2,1)S(1)}, bf16[2,8,80,512]{3,2,1,0:T(8,128)(2,1)}) custom-call(s32[4]{0:T(128)S(1)} %pad_add_fusion.2.place_ref, bf16[8,320,512]{2,1,0:T(8,128)(2,1)S(1)} %bitcast.194, bf16[8,320,512]{2,1,0:T(8,128)(2,1)} %collective-permute-done.7.w_far_ref.source_far_ref.far_ref, bf16[2048,1024]{1,0:T(8,128)(2,1)S(1)} %copy-done.3, ...), custom_call_target="tpu_custom_call" | custom-call | flops 1000000 | bytes 1024 | tf_op jit(solution)/shard_map/pallas_call | solution.py:51
  228.3 5.7 %all-to-all-start.4 = ((bf16[4,144,512]{2,1,0:T(8,128)(2,1)}), bf16[4,144,512]{2,1,0:T(8,128)(2,1)}, u32[]{:S(2)}, u32[]{:S(2)}) async-start(bf16[4,144,512]{2,1,0:T(8,128)(2,1)} %bitcast_add_fusion.2), calls=%async_computation.4 | async-start | bytes 1179648 | tf_op jit(solution)/shard_map/all_to_all | solution.py:826
  239.8 16.3 %shard_map.222 = (bf16[512,512]{1,0:T(8,128)(2,1)S(1)}, bf16[2048,1024]{1,0:T(8,128)(2,1)S(1)}) custom-call(s32[2,8]{1,0:T(2,128)S(1)} %pad.11.visit_ref, bf16[512,512]{1,0:T(8,128)(2,1)S(1)} %copy-done.31, bf16[512,512]{1,0:T(8,128)(2,1)S(1)} %copy-done.49, bf16[512,512]{1,0:T(8,128)(2,1)S(1)} %copy-done.24, f32[8,1,512]{2,1,0:T(1,128)S(1)} %get-tuple-element.138.lse_ref, ...), custom_call_target="tpu_custom_call" | custom-call | flops 1000000 | bytes 1024 | tf_op jit(solution)/shard_map/pallas_call | solution.py:51
  263.6 5.4 %shard_map.223 = (bf16[1024,512]{1,0:T(8,128)(2,1)S(1)}, bf16[1024,512]{1,0:T(8,128)(2,1)}) custom-call(s32[4]{0:T(128)S(1)} %pad_add_fusion.2.place_ref, bf16[2048,1024]{1,0:T(8,128)(2,1)S(1)} %copy-done.10, bf16[512,512]{1,0:T(8,128)(2,1)S(1)} %copy-done.35, bf16[3,512,512]{2,1,0:T(8,128)(2,1)S(1)} %bitcast.199, f32[512,512]{1,0:T(8,128)S(1)} %get-tuple-element.133.d_one_ref), custom_call_target="tpu_custom_call" | custom-call | flops 1000000 | bytes 1024 | tf_op jit(solution)/shard_map/pallas_call | solution.py:51
  271.5 6.1 %collective-permute-start.21 = (bf16[8,80,512]{2,1,0:T(8,128)(2,1)}, bf16[8,80,512]{2,1,0:T(8,128)(2,1)}, u32[]{:S(2)}, u32[]{:S(2)}) collective-permute-start(bf16[8,80,512]{2,1,0:T(8,128)(2,1)} %fusion.3), channel_id=1, source_target_pairs={{0,16},{8,24},{16,0},{24,8},{1,17},{9,25},{17,1},{25,9},{2,18},{10... | collective-permute-start | bytes 1966088 | tf_op jit(solution)/shard_map/ppermute | solution.py:805
  277.7 4.2 %all-to-all-start.5 = ((bf16[4,128,512]{2,1,0:T(8,128)(2,1)}), bf16[4,128,512]{2,1,0:T(8,128)(2,1)}, u32[]{:S(2)}, u32[]{:S(2)}) async-start(bf16[4,128,512]{2,1,0:T(8,128)(2,1)} %bitcast_add_fusion.4), calls=%async_computation.5 | async-start | bytes 1048576 | tf_op jit(solution)/shard_map/all_to_all | solution.py:826
  284.0 6.2 %shard_map.224 = (bf16[2,8,48,512]{3,2,1,0:T(8,128)(2,1)S(1)}, bf16[2,8,48,512]{3,2,1,0:T(8,128)(2,1)}) custom-call(s32[4]{0:T(128)S(1)} %pad_add_fusion.2.place_ref, bf16[8,224,512]{2,1,0:T(8,128)(2,1)S(1)} %bitcast.190, bf16[8,224,512]{2,1,0:T(8,128)(2,1)} %collective-permute-done.5.w_far_ref.far_ref, bf16[2048,1024]{1,0:T(8,128)(2,1)S(1)} %copy-done.11, ...), custom_call_target="tpu_custom_call" | custom-call | flops 1000000 | bytes 1024 | tf_op jit(solution)/shard_map/pallas_call | solution.py:51
  290.3 3.0 collective-permute-done.21
  293.3 2.8 bitcast_add_fusion.1
  301.6 5.5 %all-to-all-start.6 = ((bf16[8,128,512]{2,1,0:T(8,128)(2,1)}), bf16[8,128,512]{2,1,0:T(8,128)(2,1)}, u32[]{:S(2)}, u32[]{:S(2)}) async-start(bf16[8,128,512]{2,1,0:T(8,128)(2,1)} %bitcast.63), calls=%async_computation.6 | async-start | bytes 2097152 | tf_op jit(solution)/shard_map/all_to_all | solution.py:822
  317.5 16.5 %collective-permute-done.23 = bf16[4,128,512]{2,1,0:T(8,128)(2,1)S(1)} collective-permute-done((bf16[4,128,512]{2,1,0:T(8,128)(2,1)S(1)}, bf16[4,128,512]{2,1,0:T(8,128)(2,1)S(1)}, u32[]{:S(2)}, u32[]{:S(2)}) %collective-permute-start.23) | collective-permute-done | bytes 524320 | tf_op jit(solution)/shard_map/ppermute | solution.py:808
  335.5 3.8 %collective-permute-start.25 = (bf16[128,512]{1,0:T(8,128)(2,1)S(1)}, bf16[128,512]{1,0:T(8,128)(2,1)S(1)}, u32[]{:S(2)}, u32[]{:S(2)}) collective-permute-start(bf16[128,512]{1,0:T(8,128)(2,1)S(1)} %get-tuple-element.224), channel_id=1, source_target_pairs={{0,4},{1,5},{2,6},{3,7},{4,0},{5,1},{6,2},{7,3},{8,12},{9,13},{10,... | collective-permute-start | bytes 393224 | tf_op jit(solution)/shard_map/ppermute | solution.py:811
  340.8 8.4 %collective-permute-done.25 = bf16[128,512]{1,0:T(8,128)(2,1)S(1)} collective-permute-done((bf16[128,512]{1,0:T(8,128)(2,1)S(1)}, bf16[128,512]{1,0:T(8,128)(2,1)S(1)}, u32[]{:S(2)}, u32[]{:S(2)}) %collective-permute-start.25) | collective-permute-done | bytes 131104 | tf_op jit(solution)/shard_map/ppermute | solution.py:811
  (292 shorter events, 120.0 us)
Async XLA Ops:
  2.4 5.7 %collective-permute-start.1 = (bf16[3,2,128,512]{3,2,1,0:T(8,128)(2,1)S(1)}, bf16[3,2,128,512]{3,2,1,0:T(8,128)(2,1)S(1)}, u32[]{:S(2)}, u32[]{:S(2)}) collective-permute-start(bf16[3,2,128,512]{3,2,1,0:T(8,128)(2,1)S(1)} %get-tuple-element.221), channel_id=1, source_target_pairs={{0,8},{8,0},{16,24},{24,16},{1,9},{9,1},{17,25},{25,17},{2,10},{10... | collective-permute-start | bytes 2359304 | tf_op jit(solution)/shard_map/ppermute | solution.py:802
  3.1 5.1 %collective-permute-start.2 = (bf16[48,512]{1,0:T(8,128)(2,1)S(1)}, bf16[48,512]{1,0:T(8,128)(2,1)S(1)}, u32[]{:S(2)}, u32[]{:S(2)}) collective-permute-start(bf16[48,512]{1,0:T(8,128)(2,1)S(1)} %bitcast.229), channel_id=1, source_target_pairs={{0,16},{8,24},{16,0},{24,8},{1,17},{9,25},{17,1},{25,9},{2,18},{10... | collective-permute-start | bytes 147464 | tf_op jit(solution)/shard_map/ppermute | solution.py:805
  12.7 27.5 %all-to-all-start = ((bf16[4,224,512]{2,1,0:T(8,128)(2,1)}), bf16[4,224,512]{2,1,0:T(8,128)(2,1)S(1)}, u32[]{:S(2)}, u32[]{:S(2)}) async-start(bf16[4,224,512]{2,1,0:T(8,128)(2,1)} %pad_maximum_fusion.4), calls=%async_computation | async-start | bytes 1835008 | tf_op jit(solution)/shard_map/all_to_all | solution.py:826
  18.6 6.1 %collective-permute-start.3 = (bf16[224,512]{1,0:T(8,128)(2,1)S(1)}, bf16[224,512]{1,0:T(8,128)(2,1)S(1)}, u32[]{:S(2)}, u32[]{:S(2)}) collective-permute-start(bf16[224,512]{1,0:T(8,128)(2,1)S(1)} %get-tuple-element.236), channel_id=1, source_target_pairs={{0,16},{8,24},{16,0},{24,8},{1,17},{9,25},{17,1},{25,9},{2,18},{10... | collective-permute-start | bytes 688136 | tf_op jit(solution)/shard_map/ppermute | solution.py:805
  40.1 21.3 %collective-permute-start.4 = (bf16[4,224,512]{2,1,0:T(8,128)(2,1)S(1)}, bf16[4,224,512]{2,1,0:T(8,128)(2,1)S(1)}, u32[]{:S(2)}, u32[]{:S(2)}) collective-permute-start(bf16[4,224,512]{2,1,0:T(8,128)(2,1)S(1)} %all-to-all-done), channel_id=1, source_target_pairs={{0,1},{1,0},{2,3},{3,2},{4,5},{5,4},{6,7},{7,6},{8,9},{9,8},{10,11... | collective-permute-start | bytes 2752520 | tf_op jit(solution)/shard_map/ppermute | solution.py:808
  41.6 35.3 %all-to-all-start.1 = ((bf16[4,320,512]{2,1,0:T(8,128)(2,1)}), bf16[4,320,512]{2,1,0:T(8,128)(2,1)S(1)}, u32[]{:S(2)}, u32[]{:S(2)}) async-start(bf16[4,320,512]{2,1,0:T(8,128)(2,1)} %pad_maximum_fusion.3), calls=%async_computation.1 | async-start | bytes 2621440 | tf_op jit(solution)/shard_map/all_to_all | solution.py:826
  61.9 4.0 %collective-permute-start.5 = (bf16[8,224,512]{2,1,0:T(8,128)(2,1)S(1)}, bf16[8,224,512]{2,1,0:T(8,128)(2,1)}, u32[]{:S(2)}, u32[]{:S(2)}) collective-permute-start(bf16[8,224,512]{2,1,0:T(8,128)(2,1)S(1)} %bitcast.186), channel_id=1, source_target_pairs={{0,8},{8,0},{16,24},{24,16},{1,9},{9,1},{17,25},{25,17},{2,10},{10... | collective-permute-start | bytes 5505032 | tf_op jit(solution)/shard_map/ppermute | solution.py:802
  78.0 41.1 %all-to-all-start.2 = ((bf16[4,384,512]{2,1,0:T(8,128)(2,1)}), bf16[4,384,512]{2,1,0:T(8,128)(2,1)S(1)}, u32[]{:S(2)}, u32[]{:S(2)}) async-start(bf16[4,384,512]{2,1,0:T(8,128)(2,1)} %pad_maximum_fusion.2), calls=%async_computation.2 | async-start | bytes 3145728 | tf_op jit(solution)/shard_map/all_to_all | solution.py:826
  83.1 31.2 %collective-permute-start.6 = (bf16[4,320,512]{2,1,0:T(8,128)(2,1)}, bf16[4,320,512]{2,1,0:T(8,128)(2,1)}, u32[]{:S(2)}, u32[]{:S(2)}) collective-permute-start(bf16[4,320,512]{2,1,0:T(8,128)(2,1)} %copy-done.57), channel_id=1, source_target_pairs={{0,1},{1,0},{2,3},{3,2},{4,5},{5,4},{6,7},{7,6},{8,9},{9,8},{10,11... | collective-permute-start | bytes 3932168 | tf_op jit(solution)/shard_map/ppermute | solution.py:808
  119.1 5.3 %collective-permute-start.7 = (bf16[8,320,512]{2,1,0:T(8,128)(2,1)}, bf16[8,320,512]{2,1,0:T(8,128)(2,1)}, u32[]{:S(2)}, u32[]{:S(2)}) collective-permute-start(bf16[8,320,512]{2,1,0:T(8,128)(2,1)} %bitcast.191), channel_id=1, source_target_pairs={{0,8},{8,0},{16,24},{24,16},{1,9},{9,1},{17,25},{25,17},{2,10},{10... | collective-permute-start | bytes 7864328 | tf_op jit(solution)/shard_map/ppermute | solution.py:802
  120.1 25.9 %collective-permute-start.8 = (bf16[4,256,512]{2,1,0:T(8,128)(2,1)}, bf16[4,256,512]{2,1,0:T(8,128)(2,1)}, u32[]{:S(2)}, u32[]{:S(2)}) collective-permute-start(bf16[4,256,512]{2,1,0:T(8,128)(2,1)} %slice.116), channel_id=1, source_target_pairs={{0,1},{1,0},{2,3},{3,2},{4,5},{5,4},{6,7},{7,6},{8,9},{9,8},{10,11... | collective-permute-start | bytes 3145736 | tf_op jit(solution)/shard_map/ppermute | solution.py:808
  148.7 4.2 %collective-permute-start.9 = (bf16[8,256,512]{2,1,0:T(8,128)(2,1)S(1)}, bf16[8,256,512]{2,1,0:T(8,128)(2,1)S(1)}, u32[]{:S(2)}, u32[]{:S(2)}) collective-permute-start(bf16[8,256,512]{2,1,0:T(8,128)(2,1)S(1)} %bitcast.197), channel_id=1, source_target_pairs={{0,8},{8,0},{16,24},{24,16},{1,9},{9,1},{17,25},{25,17},{2,10},{10... | collective-permute-start | bytes 6291464 | tf_op jit(solution)/shard_map/ppermute | solution.py:802
  166.0 4.6 %collective-permute-start.10 = (bf16[2,8,144,512]{3,2,1,0:T(8,128)(2,1)S(1)}, bf16[2,8,144,512]{3,2,1,0:T(8,128)(2,1)S(1)}, u32[]{:S(2)}, u32[]{:S(2)}) collective-permute-start(bf16[2,8,144,512]{3,2,1,0:T(8,128)(2,1)S(1)} %shard_map.217), channel_id=1, source_target_pairs={{0,8},{8,0},{16,24},{24,16},{1,9},{9,1},{17,25},{25,17},{2,10},{10... | collective-permute-start | bytes 7077896 | tf_op jit(solution)/shard_map/ppermute | solution.py:802
  172.4 31.9 %collective-permute-start.11 = (bf16[8,144,512]{2,1,0:T(8,128)(2,1)}, bf16[8,144,512]{2,1,0:T(8,128)(2,1)}, u32[]{:S(2)}, u32[]{:S(2)}) collective-permute-start(bf16[8,144,512]{2,1,0:T(8,128)(2,1)} %fusion.2), channel_id=1, source_target_pairs={{0,16},{8,24},{16,0},{24,8},{1,17},{9,25},{17,1},{25,9},{2,18},{10... | collective-permute-start | bytes 3538952 | tf_op jit(solution)/shard_map/ppermute | solution.py:805
  173.9 33.6 %all-to-all-start.3 = ((bf16[4,128,512]{2,1,0:T(8,128)(2,1)}), bf16[4,128,512]{2,1,0:T(8,128)(2,1)}, u32[]{:S(2)}, u32[]{:S(2)}) async-start(bf16[4,128,512]{2,1,0:T(8,128)(2,1)} %bitcast.200), calls=%async_computation.3 | async-start | bytes 1048576 | tf_op jit(solution)/shard_map/all_to_all | solution.py:826
  207.5 20.8 %collective-permute-start.12 = (bf16[1024,512]{1,0:T(8,128)(2,1)}, bf16[1024,512]{1,0:T(8,128)(2,1)}, u32[]{:S(2)}, u32[]{:S(2)}) collective-permute-start(bf16[1024,512]{1,0:T(8,128)(2,1)} %copy-done.54), channel_id=1, source_target_pairs={{0,8},{8,0},{16,24},{24,16},{1,9},{9,1},{17,25},{25,17},{2,10},{10... | collective-permute-start | bytes 3145736 | tf_op jit(solution)/shard_map/ppermute | solution.py:802
  209.7 16.6 %collective-permute-start.13 = (bf16[4,144,512]{2,1,0:T(8,128)(2,1)}, bf16[4,144,512]{2,1,0:T(8,128)(2,1)}, u32[]{:S(2)}, u32[]{:S(2)}) collective-permute-start(bf16[4,144,512]{2,1,0:T(8,128)(2,1)} %fusion.4), channel_id=1, source_target_pairs={{0,1},{1,0},{2,3},{3,2},{4,5},{5,4},{6,7},{7,6},{8,9},{9,8},{10,11... | collective-permute-start | bytes 1769480 | tf_op jit(solution)/shard_map/ppermute | solution.py:808
  228.3 31.6 %collective-permute-start.15 = (bf16[2,8,80,512]{3,2,1,0:T(8,128)(2,1)}, bf16[2,8,80,512]{3,2,1,0:T(8,128)(2,1)}, u32[]{:S(2)}, u32[]{:S(2)}) collective-permute-start(bf16[2,8,80,512]{3,2,1,0:T(8,128)(2,1)} %get-tuple-element.142), channel_id=1, source_target_pairs={{0,8},{8,0},{16,24},{24,16},{1,9},{9,1},{17,25},{25,17},{2,10},{10... | collective-permute-start | bytes 3932168 | tf_op jit(solution)/shard_map/ppermute | solution.py:802
  228.3 31.6 %all-to-all-start.4 = ((bf16[4,144,512]{2,1,0:T(8,128)(2,1)}), bf16[4,144,512]{2,1,0:T(8,128)(2,1)}, u32[]{:S(2)}, u32[]{:S(2)}) async-start(bf16[4,144,512]{2,1,0:T(8,128)(2,1)} %bitcast_add_fusion.2), calls=%async_computation.4 | async-start | bytes 1179648 | tf_op jit(solution)/shard_map/all_to_all | solution.py:826
  236.1 22.8 %collective-permute-start.14 = (bf16[4,128,512]{2,1,0:T(8,128)(2,1)S(1)}, bf16[4,128,512]{2,1,0:T(8,128)(2,1)S(1)}, u32[]{:S(2)}, u32[]{:S(2)}) collective-permute-start(bf16[4,128,512]{2,1,0:T(8,128)(2,1)S(1)} %fusion.5), channel_id=1, source_target_pairs={{0,1},{1,0},{2,3},{3,2},{4,5},{5,4},{6,7},{7,6},{8,9},{9,8},{10,11... | collective-permute-start | bytes 1572872 | tf_op jit(solution)/shard_map/ppermute | solution.py:808
  269.0 27.9 %collective-permute-start.16 = (bf16[1024,512]{1,0:T(8,128)(2,1)}, bf16[1024,512]{1,0:T(8,128)(2,1)}, u32[]{:S(2)}, u32[]{:S(2)}) collective-permute-start(bf16[1024,512]{1,0:T(8,128)(2,1)} %get-tuple-element.147), channel_id=1, source_target_pairs={{0,8},{8,0},{16,24},{24,16},{1,9},{9,1},{17,25},{25,17},{2,10},{10... | collective-permute-start | bytes 3145736 | tf_op jit(solution)/shard_map/ppermute | solution.py:802
  271.5 21.7 %collective-permute-start.21 = (bf16[8,80,512]{2,1,0:T(8,128)(2,1)}, bf16[8,80,512]{2,1,0:T(8,128)(2,1)}, u32[]{:S(2)}, u32[]{:S(2)}) collective-permute-start(bf16[8,80,512]{2,1,0:T(8,128)(2,1)} %fusion.3), channel_id=1, source_target_pairs={{0,16},{8,24},{16,0},{24,8},{1,17},{9,25},{17,1},{25,9},{2,18},{10... | collective-permute-start | bytes 1966088 | tf_op jit(solution)/shard_map/ppermute | solution.py:805
  277.7 19.2 %all-to-all-start.5 = ((bf16[4,128,512]{2,1,0:T(8,128)(2,1)}), bf16[4,128,512]{2,1,0:T(8,128)(2,1)}, u32[]{:S(2)}, u32[]{:S(2)}) async-start(bf16[4,128,512]{2,1,0:T(8,128)(2,1)} %bitcast_add_fusion.4), calls=%async_computation.5 | async-start | bytes 1048576 | tf_op jit(solution)/shard_map/all_to_all | solution.py:826
  290.2 9.2 %collective-permute-start.17 = (bf16[2,8,48,512]{3,2,1,0:T(8,128)(2,1)}, bf16[2,8,48,512]{3,2,1,0:T(8,128)(2,1)S(1)}, u32[]{:S(2)}, u32[]{:S(2)}) collective-permute-start(bf16[2,8,48,512]{3,2,1,0:T(8,128)(2,1)} %get-tuple-element.150), channel_id=1, source_target_pairs={{0,8},{8,0},{16,24},{24,16},{1,9},{9,1},{17,25},{25,17},{2,10},{10... | collective-permute-start | bytes 2359304 | tf_op jit(solution)/shard_map/ppermute | solution.py:802
  299.5 12.2 %collective-permute-start.22 = (bf16[8,48,512]{2,1,0:T(8,128)(2,1)S(1)}, bf16[8,48,512]{2,1,0:T(8,128)(2,1)}, u32[]{:S(2)}, u32[]{:S(2)}) collective-permute-start(bf16[8,48,512]{2,1,0:T(8,128)(2,1)S(1)} %fusion.7), channel_id=1, source_target_pairs={{0,16},{8,24},{16,0},{24,8},{1,17},{9,25},{17,1},{25,9},{2,18},{10... | collective-permute-start | bytes 1179656 | tf_op jit(solution)/shard_map/ppermute | solution.py:805
  301.6 10.1 %collective-permute-start.20 = (bf16[2,128,512]{2,1,0:T(8,128)(2,1)S(1)}, bf16[2,128,512]{2,1,0:T(8,128)(2,1)S(1)}, u32[]{:S(2)}, u32[]{:S(2)}) collective-permute-start(bf16[2,128,512]{2,1,0:T(8,128)(2,1)S(1)} %get-tuple-element.226), channel_id=1, source_target_pairs={{0,8},{8,0},{16,24},{24,16},{1,9},{9,1},{17,25},{25,17},{2,10},{10... | collective-permute-start | bytes 786440 | tf_op jit(solution)/shard_map/ppermute | solution.py:802
  301.6 37.6 %all-to-all-start.6 = ((bf16[8,128,512]{2,1,0:T(8,128)(2,1)}), bf16[8,128,512]{2,1,0:T(8,128)(2,1)}, u32[]{:S(2)}, u32[]{:S(2)}) async-start(bf16[8,128,512]{2,1,0:T(8,128)(2,1)} %bitcast.63), calls=%async_computation.6 | async-start | bytes 2097152 | tf_op jit(solution)/shard_map/all_to_all | solution.py:822
  313.3 20.7 %collective-permute-start.23 = (bf16[4,128,512]{2,1,0:T(8,128)(2,1)S(1)}, bf16[4,128,512]{2,1,0:T(8,128)(2,1)S(1)}, u32[]{:S(2)}, u32[]{:S(2)}) collective-permute-start(bf16[4,128,512]{2,1,0:T(8,128)(2,1)S(1)} %fusion.6), channel_id=1, source_target_pairs={{0,1},{1,0},{2,3},{3,2},{4,5},{5,4},{6,7},{7,6},{8,9},{9,8},{10,11... | collective-permute-start | bytes 1572872 | tf_op jit(solution)/shard_map/ppermute | solution.py:808
  334.3 6.5 %collective-permute-start.24 = (bf16[128,512]{1,0:T(8,128)(2,1)S(1)}, bf16[128,512]{1,0:T(8,128)(2,1)S(1)}, u32[]{:S(2)}, u32[]{:S(2)}) collective-permute-start(bf16[128,512]{1,0:T(8,128)(2,1)S(1)} %get-tuple-element.222), channel_id=1, source_target_pairs={{0,2},{1,3},{2,0},{3,1},{4,6},{5,7},{6,4},{7,5},{8,10},{9,11},{10,... | collective-permute-start | bytes 393224 | tf_op jit(solution)/shard_map/ppermute | solution.py:811
  335.5 13.7 %collective-permute-start.25 = (bf16[128,512]{1,0:T(8,128)(2,1)S(1)}, bf16[128,512]{1,0:T(8,128)(2,1)S(1)}, u32[]{:S(2)}, u32[]{:S(2)}) collective-permute-start(bf16[128,512]{1,0:T(8,128)(2,1)S(1)} %get-tuple-element.224), channel_id=1, source_target_pairs={{0,4},{1,5},{2,6},{3,7},{4,0},{5,1},{6,2},{7,3},{8,12},{9,13},{10,... | collective-permute-start | bytes 393224 | tf_op jit(solution)/shard_map/ppermute | solution.py:811
  339.2 9.9 %collective-permute-start.26 = (bf16[128,512]{1,0:T(8,128)(2,1)S(1)}, bf16[128,512]{1,0:T(8,128)(2,1)S(1)}, u32[]{:S(2)}, u32[]{:S(2)}) collective-permute-start(bf16[128,512]{1,0:T(8,128)(2,1)S(1)} %get-tuple-element.223), channel_id=1, source_target_pairs={{0,6},{1,7},{2,4},{3,5},{4,2},{5,3},{6,0},{7,1},{8,14},{9,15},{10,... | collective-permute-start | bytes 393224 | tf_op jit(solution)/shard_map/ppermute | solution.py:811
  340.7 11.2 %collective-permute-start.19 = (bf16[2,128,512]{2,1,0:T(8,128)(2,1)S(1)}, bf16[2,128,512]{2,1,0:T(8,128)(2,1)S(1)}, u32[]{:S(2)}, u32[]{:S(2)}) collective-permute-start(bf16[2,128,512]{2,1,0:T(8,128)(2,1)S(1)} %get-tuple-element.228), channel_id=1, source_target_pairs={{0,8},{8,0},{16,24},{24,16},{1,9},{9,1},{17,25},{25,17},{2,10},{10... | collective-permute-start | bytes 786440 | tf_op jit(solution)/shard_map/ppermute | solution.py:802
  (78 other events, 335.2 us)
where the time goes:
time: 359 us; the launch traced here: 353 us
  Pallas kernels  102 us (28%)
  waiting for transfers between devices  90.7 us (25%)
  starting transfers between devices  62.5 us (17%)
  local copies, waits for them, and re-layouts  56.9 us (16%)
  other arithmetic  39.6 us (11%)
    pallas_call x13, Pallas kernels, call(): pl.pallas_call(kernel, out_shape=out_shape, in_specs=in_specs, out_specs=...  102 us
    ppermute x6, waiting for transfers between devices, over_y(): lax.ppermute(v, 'seq', [(i, i ^ k) for i in range(seq_count)])  46 us
    unnamed x160, local copies, waits for them, and re-layouts  42.7 us
    all_to_all x6, starting transfers between devices, exchange_z(): return lax.all_to_all(v, 'seq', 0, 0, tiled=True, axis_index_groups=groups)  26.8 us
    all_to_all x6, waiting for transfers between devices, exchange_z(): return lax.all_to_all(v, 'seq', 0, 0, tiled=True, axis_index_groups=groups)  16.4 us
    ppermute x5, starting transfers between devices, over_x(): lax.ppermute(v, 'dp', [(i, i ^ 2 * k) for i in range(dp_count)])  13.2 us
    ppermute x6, starting transfers between devices, over_y(): lax.ppermute(v, 'seq', [(i, i ^ k) for i in range(seq_count)])  10.5 us
    ppermute x13, waiting for transfers between devices, over_core(): return lax.ppermute(v, 'dp', [(i, i ^ 1) for i in range(dp_count)])  10.4 us
  transfers between devices with their start and end apart: 34, of which 16 were waited for; matrix products, arithmetic and copies ran while one was open for 12% of the time, Pallas kernels for 24%

commit v1 on v0

--- a/solution.py
+++ b/solution.py
@@ -12,6 +12,7 @@
 HEAD_DIM = 64
 GROUP = 4
 LANES = GROUP * HEAD_DIM
+PACE = 1.15e9 * 0.1
 CHUNK = 256
 LOG2E = 1.4426950408889634
 LN2 = 0.6931471805599453
@@ -38,7 +39,7 @@
     return lead * (-(-dims[-2] // 16) * 16) * (-(-dims[-1] // 128) * 128) * jnp.dtype(dtype).itemsize
 
 
-def kernel_call(kernel, *, out_shape, in_specs, out_specs, scratch_shapes=(), spare=4):
+def kernel_call(kernel, *, out_shape, in_specs, out_specs, scratch_shapes=(), spare=3, us=2):
     def call(*operands):
         need = spare * 2**20
         for operand, spec in zip(operands, in_specs):
@@ -55,7 +56,7 @@
             out_specs=out_specs,
             scratch_shapes=scratch_shapes,
             compiler_params=pltpu.CompilerParams(vmem_limit_bytes=need),
-            cost_estimate=pl.CostEstimate(flops=10**6, bytes_accessed=2**10, transcendentals=0),
+            cost_estimate=pl.CostEstimate(flops=int(us * PACE), bytes_accessed=2**10, transcendentals=0),
         )(*operands)
 
     return call
@@ -79,7 +80,10 @@
     pieces: int
     tile_rows: int
     hidden: int
-    first: int
+    feed_rows: int
+    first_one: tuple
+    first_two: tuple
+    first_three: tuple
 
 
 def stack_heads(tile):
@@ -102,7 +106,14 @@
     return jnp.concatenate([ref[spot, cols] for spot in spots], axis=0)
 
 
-def attend_kernel(visit_ref, q_ref, kv_ref, qseg_ref, kseg_ref, o_ref, lse_ref, acc_ref, qst_ref):
+def turn_segments(kseg_ref, seg_ref):
+    count, _, keys = kseg_ref.shape
+    for b in range(count):
+        row = kseg_ref[b].astype(F32)
+        seg_ref[b * keys : (b + 1) * keys, :] = jnp.transpose(jnp.broadcast_to(row, (128, keys)))[:, :1]
+
+
+def attend_part(visit_ref, q_ref, kv_ref, qseg_ref, seg_ref, o_ref, lse_ref, acc_ref, qst_ref):
     width = q_ref.shape[1]
     blocks = qseg_ref.shape[0]
     rows = q_ref.shape[0] // blocks
@@ -113,14 +124,14 @@
     def block(k, carry):
         lo, hi = visit_ref[0, k], visit_ref[1, k]
         q_rows = pl.ds(pl.multiple_of(k * rows, rows), rows)
-        qseg = jnp.concatenate([qseg_ref[k]] * GROUP, axis=1)
+        qseg = jnp.concatenate([qseg_ref[k].astype(F32)] * GROUP, axis=1)
         for g in range(groups):
             qst_ref[g] = stack_heads(q_ref[q_rows, g * LANES : (g + 1) * LANES])
         acc_ref[...] = jnp.zeros(acc_ref.shape, F32)
 
         def step(b, carry):
             spots = key_rows(b, keys, total)
-            same = kseg_ref[pl.ds(pl.multiple_of(b * keys, keys), keys), :] == qseg
+            same = seg_ref[pl.ds(pl.multiple_of(b * keys, keys), keys), :] == qseg
             scores = [
                 dot_nt(both_rows(kv_ref, spots, slice(g * LANES, (g + 1) * LANES)), qst_ref[g]) for g in range(groups)
             ]
@@ -161,7 +172,7 @@
     lax.fori_loop(0, blocks, block, 0)
 
 
-def attend_back_kernel(
+def attend_back_part(
     visit_ref,
     q_ref,
     do_ref,
@@ -169,7 +180,7 @@
     lse_ref,
     kv_ref,
     qseg_ref,
-    kseg_ref,
+    seg_ref,
     dq_ref,
     dkv_ref,
     sum_ref,
@@ -189,7 +200,7 @@
     def block(k, carry):
         lo, hi = visit_ref[0, k], visit_ref[1, k]
         q_rows = pl.ds(pl.multiple_of(k * rows, rows), rows)
-        qseg = jnp.concatenate([qseg_ref[k]] * GROUP, axis=1)
+        qseg = jnp.concatenate([qseg_ref[k].astype(F32)] * GROUP, axis=1)
         for g in range(groups):
             cols = slice(g * LANES, (g + 1) * LANES)
             qst_ref[g] = stack_heads(q_ref[q_rows, cols])
@@ -201,7 +212,7 @@
 
         def step(b, carry):
             spots = key_rows(b, keys, total)
-            same = kseg_ref[pl.ds(pl.multiple_of(b * keys, keys), keys), :] == qseg
+            same = seg_ref[pl.ds(pl.multiple_of(b * keys, keys), keys), :] == qseg
             k_cols = [slice(g * LANES, (g + 1) * LANES) for g in range(groups)]
             v_cols = [slice(width + g * LANES, width + (g + 1) * LANES) for g in range(groups)]
             scores = [dot_nt(both_rows(kv_ref, spots, k_cols[g]), qst_ref[g]) for g in range(groups)]
@@ -235,40 +246,6 @@
     dkv_ref[:, width:] = sum_ref[:, width:].astype(BF)
 
 
-def attend(visits, queries, pairs, qseg, kseg):
-    own, width = queries.shape
-    blocks = qseg.shape[0]
-    rows = own // blocks
-    groups = width // LANES
-    return kernel_call(
-        attend_kernel,
-        out_shape=(shape((own, width)), shape((blocks * groups, 1, GROUP * rows), F32)),
-        in_specs=[SMEM] + [VMEM] * 4,
-        out_specs=(VMEM, VMEM),
-        scratch_shapes=[pltpu.VMEM((width, rows), F32), pltpu.VMEM((groups, GROUP * rows, LANES), BF)],
-    )(visits, queries, pairs, qseg[:, None, :], kseg.reshape(-1, 1))
-
-
-def attend_back(visits, queries, d_mixed, mixed, lse, pairs, qseg, kseg):
-    own, width = queries.shape
-    blocks = qseg.shape[0]
-    rows = own // blocks
-    groups = width // LANES
-    return kernel_call(
-        attend_back_kernel,
-        out_shape=(shape((own, width)), shape(pairs.shape)),
-        in_specs=[SMEM] + [VMEM] * 7,
-        out_specs=(VMEM, VMEM),
-        scratch_shapes=[
-            pltpu.VMEM(pairs.shape, F32),
-            pltpu.VMEM((width, rows), F32),
-            pltpu.VMEM((groups, GROUP * rows, LANES), BF),
-            pltpu.VMEM((groups, GROUP * rows, LANES), BF),
-            pltpu.VMEM((groups, 1, GROUP * rows), F32),
-        ],
-    )(visits, queries, d_mixed, mixed, lse, pairs, qseg[:, None, :], kseg.reshape(-1, 1))
-
-
 def norm_of(resid):
     centered = resid - jnp.mean(resid, axis=-1, keepdims=True)
     inv = lax.rsqrt(jnp.mean(centered * centered, axis=-1, keepdims=True) + 1e-05)
@@ -282,16 +259,26 @@
     )
 
 
-def fetch_tiles(place_ref, parts, first, tiles, rows, x_count, whole_ref, sem):
+def weight_rows(size, weights, total, firsts):
+    out = []
+    per = len(weights) // 2
+    for e in range(2):
+        for k in range(size.x_count):
+            a = min(k, per - 1)
+            out.append((k, e, weights[e * per + a], firsts[a] + (k - a) * total))
+    return out
+
+
+def fetch_tiles(size, place_ref, weights, tiles, firsts, whole_ref, sem):
     copies = []
-    for e, part in enumerate(parts):
+    rows = size.tile_rows
+    for k, e, part, start in weight_rows(size, weights, tiles * rows, firsts):
         pieces = part.shape[0]
-        for k in range(x_count):
-            dp = (place_ref[0] ^ k) * 2 + (place_ref[1] ^ e)
-            at = pl.ds(pl.multiple_of(dp * pieces, pieces), pieces)
-            for t in range(tiles):
-                source = part.at[:, pl.ds(first + (k * tiles + t) * rows, rows)]
-                copies.append(pltpu.make_async_copy(source, whole_ref.at[t, at], sem.at[len(copies)]))
+        dp = (place_ref[0] ^ k) * 2 + (place_ref[1] ^ e)
+        at = pl.ds(pl.multiple_of(dp * pieces, pieces), pieces)
+        for t in range(tiles):
+            source = part.at[:, pl.ds(start + t * rows, rows)]
+            copies.append(pltpu.make_async_copy(source, whole_ref.at[t, at], sem.at[len(copies)]))
     for copy in copies:
         copy.start()
     return copies
@@ -344,53 +331,75 @@
         target[k, :, tile * tile_rows : (tile + 1) * tile_rows, :] = part.reshape(pieces, tile_rows, width)
 
 
-def project_kernel(size, place_ref, w_near_ref, w_far_ref, near_ref, far_ref, q_ref, kv_ref, whole_ref, sem):
-    copies = fetch_tiles(
-        place_ref, (w_near_ref, w_far_ref), size.first, 3, size.tile_rows, size.x_count, whole_ref, sem
-    )
+def attend_scratch(size, width):
+    rows = size.own // size.z_count
+    return [
+        pltpu.VMEM((size.length, 1), F32),
+        pltpu.VMEM((width, rows), F32),
+        pltpu.VMEM((width // LANES, GROUP * rows, LANES), BF),
+    ]
+
+
+def first_kernel(
+    size,
+    visit_ref,
+    place_ref,
+    near_ref,
+    far_ref,
+    qseg_ref,
+    kseg_ref,
+    *refs,
+):
+    weights, (q_ref, kv_ref, whole_ref, o_ref, lse_ref, seg_ref, acc_ref, qst_ref, sem) = refs[:-9], refs[-9:]
+    copies = fetch_tiles(size, place_ref, weights, 3, size.first_one, whole_ref, sem)
     own = own_tokens(near_ref, place_ref, size.half, size.z_count)
+    turn_segments(kseg_ref, seg_ref)
     for copy in copies:
         copy.wait()
     q_ref[...] = (dot_f32(own, tile_of(whole_ref, 0)) * (HEAD_DIM**-0.5 * LOG2E)).astype(BF)
     put_pairs(near_ref, far_ref, size.half, tile_of(whole_ref, 1), tile_of(whole_ref, 2), kv_ref)
-
-
-def project(size, place, weights, near, far):
+    attend_part(visit_ref, q_ref, kv_ref, qseg_ref, seg_ref, o_ref, lse_ref, acc_ref, qst_ref)
+
+
+def lse_shape(size, width):
+    return shape((size.z_count * width // LANES, 1, GROUP * size.half), F32)
+
+
+def first(size, visits, place, weights, near, far, qseg, kseg):
     width = near.shape[2]
     return kernel_call(
-        functools.partial(project_kernel, size),
+        functools.partial(first_kernel, size),
+        us=16,
         out_shape=(
             shape((size.own, width)),
             shape((size.length, 2 * width)),
             shape((3, 2 * size.x_count * size.pieces, size.tile_rows, width)),
+            shape((size.own, width)),
+            lse_shape(size, width),
         ),
-        in_specs=[SMEM, ANY, ANY, VMEM, VMEM],
-        out_specs=(VMEM,) * 3,
-        scratch_shapes=[pltpu.SemaphoreType.DMA((2 * size.x_count * 3,))],
-    )(place, *weights, near, far)
-
-
-def bridge_kernel(
+        in_specs=[SMEM] * 2 + [VMEM] * 4 + [ANY] * len(weights),
+        out_specs=(VMEM,) * 5,
+        scratch_shapes=attend_scratch(size, width) + [pltpu.SemaphoreType.DMA((2 * size.x_count * 3,))],
+    )(visits, place, near, far, qseg, kseg, *weights)
+
+
+def second_kernel(
     size,
+    visit_ref,
     place_ref,
-    w_near_ref,
-    w_far_ref,
     near_ref,
     source_near_ref,
     source_far_ref,
     mixed_ref,
-    q_ref,
-    kv_ref,
-    whole_ref,
-    hat_ref,
-    inv_ref,
-    norm_ref,
-    sem,
+    qseg_ref,
+    kseg_ref,
+    *refs,
 ):
-    copies = fetch_tiles(
-        place_ref, (w_near_ref, w_far_ref), size.first, 6, size.tile_rows, size.x_count, whole_ref, sem
-    )
+    weights = refs[:-12]
+    q_ref, kv_ref, whole_ref, hat_ref, inv_ref, norm_ref, o_ref, lse_ref, seg_ref, acc_ref, qst_ref, sem = refs[-12:]
+    copies = fetch_tiles(size, place_ref, weights, 6, size.first_two, whole_ref, sem)
     own = own_tokens(near_ref, place_ref, size.half, size.z_count)
+    turn_segments(kseg_ref, seg_ref)
     for copy in copies:
         copy.wait()
     norm_ref[...] = jnp.transpose(tile_of(whole_ref, 5)[:, :128].astype(F32))[: norm_ref.shape[0]]
@@ -399,15 +408,15 @@
     inv_ref[...] = inv
     low = (hat * norm_ref[0:1, :] + norm_ref[1:2, :]).astype(BF)
     q_ref[...] = (dot_f32(low, tile_of(whole_ref, 1)) * (HEAD_DIM**-0.5 * LOG2E)).astype(BF)
-    put_pairs(
-        source_near_ref, source_far_ref, size.half, tile_of(whole_ref, 2), tile_of(whole_ref, 3), kv_ref
-    )
-
-
-def bridge(size, place, weights, near, source_near, source_far, mixed):
+    put_pairs(source_near_ref, source_far_ref, size.half, tile_of(whole_ref, 2), tile_of(whole_ref, 3), kv_ref)
+    attend_part(visit_ref, q_ref, kv_ref, qseg_ref, seg_ref, o_ref, lse_ref, acc_ref, qst_ref)
+
+
+def second(size, visits, place, weights, near, source_near, source_far, mixed, qseg, kseg):
     width = near.shape[2]
     return kernel_call(
-        functools.partial(bridge_kernel, size),
+        functools.partial(second_kernel, size),
+        us=17,
         out_shape=(
             shape((size.own, width)),
             shape((size.length, 2 * width)),
@@ -415,55 +424,59 @@
             shape((size.own, width), F32),
             shape((size.own, 1), F32),
             shape((8, width), F32),
+            shape((size.own, width)),
+            lse_shape(size, width),
         ),
-        in_specs=[SMEM, ANY, ANY] + [VMEM] * 4,
-        out_specs=(VMEM,) * 6,
-        scratch_shapes=[pltpu.SemaphoreType.DMA((2 * size.x_count * 6,))],
-    )(place, *weights, near, source_near, source_far, mixed)
+        in_specs=[SMEM] * 2 + [VMEM] * 6 + [ANY] * len(weights),
+        out_specs=(VMEM,) * 8,
+        scratch_shapes=attend_scratch(size, width) + [pltpu.SemaphoreType.DMA((2 * size.x_count * 6,))],
+    )(visits, place, near, source_near, source_far, mixed, qseg, kseg, *weights)
 
 
 def feed_kernel(
     size,
     place_ref,
-    w_near_ref,
-    w_far_ref,
     mixed_ref,
     whole_two_ref,
     hat_one_ref,
     norm_ref,
     cot_ref,
-    out_ref,
-    d_two_ref,
-    d_mixed_ref,
-    sums_ref,
-    low_t_ref,
-    dz_ref,
-    hid_ref,
-    down_ref,
-    mixed_t_ref,
-    w_in_ref,
-    w_out_ref,
-    z_ref,
-    low_ref,
-    hat_two_ref,
-    inv_two_ref,
-    sem,
+    *refs,
 ):
+    weights = refs[:-16]
+    (
+        out_ref,
+        d_two_ref,
+        d_mixed_ref,
+        sums_ref,
+        low_t_ref,
+        dz_ref,
+        hid_ref,
+        down_ref,
+        mixed_t_ref,
+        w_in_ref,
+        w_out_ref,
+        z_ref,
+        low_ref,
+        hat_two_ref,
+        inv_two_ref,
+        sem,
+    ) = refs[-16:]
     own, width = hat_one_ref.shape
     hidden = z_ref.shape[1]
     tiles = hidden // width
     tile_rows = size.tile_rows
     copies = []
-    for e, part in enumerate((w_near_ref, w_far_ref)):
-        pieces, total = part.shape[0], part.shape[1] // size.x_count
-        for k in range(size.x_count):
-            dp = (place_ref[0] ^ k) * 2 + (place_ref[1] ^ e)
-            at = pl.ds(pl.multiple_of(dp * pieces, pieces), pieces)
-            for t in range(tiles):
-                source = part.at[:, pl.ds(k * total + t * tile_rows, tile_rows)]
-                copies.append(pltpu.make_async_copy(source, w_in_ref.at[t, at], sem.at[len(copies)]))
-            source = part.at[:, pl.ds(k * total + tiles * tile_rows, total - tiles * tile_rows)]
-            copies.append(pltpu.make_async_copy(source, w_out_ref.at[at], sem.at[len(copies)]))
+    total = size.feed_rows
+    for k, e, part, start in weight_rows(size, weights, total, size.first_three):
+        pieces = part.shape[0]
+        dp = (place_ref[0] ^ k) * 2 + (place_ref[1] ^ e)
+        at = pl.ds(pl.multiple_of(dp * pieces, pieces), pieces)
+        for t in range(tiles):
+            source = part.at[:, pl.ds(start + t * tile_rows, tile_rows)]
+            copies.append(pltpu.make_async_copy(source, w_in_ref.at[t, at], sem.at[len(copies)]))
+        source = part.at[:, pl.ds(start + tiles * tile_rows, total - tiles * tile_rows)]
+        copies.append(pltpu.make_async_copy(source, w_out_ref.at[at], sem.at[len(copies)]))
     for copy in copies:
         copy.start()
     mixed_t_ref[...] = jnp.transpose(mixed_ref[...])
@@ -531,6 +544,7 @@
     devices = 2 * size.x_count * size.pieces
     return kernel_call(
         functools.partial(feed_kernel, size),
+        us=12,
         out_shape=(
             shape((own, width)),
             shape((own, width), F32),
@@ -542,7 +556,7 @@
             shape((own, width)),
             shape((width, own)),
         ),
-        in_specs=[SMEM, ANY, ANY] + [VMEM] * 5,
+        in_specs=[SMEM] + [VMEM] * 5 + [ANY] * len(weights),
         out_specs=(VMEM,) * 9,
         scratch_shapes=[
             pltpu.VMEM((hidden // width, devices, size.tile_rows, width), BF),
@@ -553,7 +567,7 @@
             pltpu.VMEM((own, 1), F32),
             pltpu.SemaphoreType.DMA((2 * size.x_count * (hidden // width + 1),)),
         ],
-    )(place, *weights, mixed, whole_two, hat_one, norms, cot)
+    )(place, mixed, whole_two, hat_one, norms, cot, *weights)
 
 
 def feed_grads_kernel(
@@ -612,80 +626,94 @@
         lax.fori_loop(0, count, step, 0)
 
 
-def back_cross_kernel(
+def back_scratch(size, width):
+    rows = size.own // size.z_count
+    return [
+        pltpu.VMEM((size.length, 1), F32),
+        pltpu.VMEM((size.length, 2 * width), F32),
+        pltpu.VMEM((width, rows), F32),
+        pltpu.VMEM((width // LANES, GROUP * rows, LANES), BF),
+        pltpu.VMEM((width // LANES, GROUP * rows, LANES), BF),
+        pltpu.VMEM((width // LANES, 1, GROUP * rows), F32),
+    ]
+
+
+def third_kernel(
     size,
+    visit_ref,
     place_ref,
-    d_kv_ref,
-    d_q_ref,
+    q_ref,
+    do_ref,
+    o_ref,
+    lse_ref,
+    kv_ref,
+    qseg_ref,
+    kseg_ref,
+    near_ref,
+    far_ref,
     whole_ref,
     hat_ref,
     inv_ref,
     norm_ref,
     d_two_ref,
     sums_in_ref,
+    mixed_self_ref,
     kept_rows_ref,
     send_rows_ref,
+    kept_ref,
+    send_ref,
     d_one_ref,
     d_mixed_ref,
-    sums_ref,
+    seg_ref,
+    sum_ref,
+    dqt_ref,
+    qst_ref,
+    dst_ref,
+    delta_ref,
+    d_q_ref,
+    d_kv_ref,
+    left_ref,
+    self_t_ref,
     low_t_ref,
+    cols_ref,
 ):
+    width = hat_ref.shape[1]
+    dp_count = 2 * size.x_count
+    turn_segments(kseg_ref, seg_ref)
+    attend_back_part(
+        visit_ref,
+        q_ref,
+        do_ref,
+        o_ref,
+        lse_ref,
+        kv_ref,
+        qseg_ref,
+        seg_ref,
+        d_q_ref,
+        d_kv_ref,
+        sum_ref,
+        dqt_ref,
+        qst_ref,
+        dst_ref,
+        delta_ref,
+    )
     hat, inv, gain = hat_ref[...], inv_ref[...], norm_ref[0:1, :]
     upstream = d_two_ref[...] + dot_nt(d_q_ref[...], whole_ref[1])
-    sums_ref[...] = sums_in_ref[...]
-    sums_ref[0:1, :] = jnp.sum(upstream * hat, axis=0, keepdims=True)
-    sums_ref[1:2, :] = jnp.sum(upstream, axis=0, keepdims=True)
+    gain_sum = jnp.sum(upstream * hat, axis=0, keepdims=True)
+    shift_sum = jnp.sum(upstream, axis=0, keepdims=True)
     d_one = norm_pull(upstream, hat, inv, gain)
     d_one_ref[...] = d_one
-    d_mixed_ref[...] = dot_nt(d_one.astype(BF), whole_ref[0]).astype(BF)
+    low_one = d_one.astype(BF)
+    d_mixed_ref[...] = dot_nt(low_one, whole_ref[0]).astype(BF)
     low_t_ref[...] = jnp.transpose((hat * gain + norm_ref[1:2, :]).astype(BF))
     back_pairs(size, d_kv_ref, whole_ref[2], whole_ref[3], kept_rows_ref, send_rows_ref)
-
-
-def back_cross(size, place, d_kv, d_q, whole, hat, inv, norms, d_two, sums):
-    own, width = hat.shape
-    return kernel_call(
-        functools.partial(back_cross_kernel, size),
-        out_shape=(
-            shape((size.length // 2, width)),
-            shape((size.length // 2, width)),
-            shape((own, width), F32),
-            shape((own, width)),
-            shape((8, width), F32),
-            shape((width, own)),
-        ),
-        in_specs=[SMEM] + [VMEM] * 8,
-        out_specs=(VMEM,) * 6,
-    )(place, d_kv, d_q, whole, hat, inv, norms, d_two, sums)
-
-
-def cross_grads_kernel(
-    size,
-    place_ref,
-    near_ref,
-    far_ref,
-    d_kv_ref,
-    d_q_ref,
-    low_t_ref,
-    mixed_self_ref,
-    d_one_ref,
-    sums_ref,
-    kept_ref,
-    send_ref,
-    left_ref,
-    self_t_ref,
-    cols_ref,
-):
-    width = d_one_ref.shape[1]
-    dp_count = 2 * size.x_count
     self_t_ref[...] = jnp.transpose(mixed_self_ref[...])
-    pad = jnp.zeros((128 - sums_ref.shape[0], width), F32)
+    pad = jnp.zeros((128 - sums_in_ref.shape[0], width), F32)
     cols_ref[...] = jnp.zeros(cols_ref.shape, F32)
-    cols_ref[:, :128] = jnp.transpose(jnp.concatenate([sums_ref[...], pad], axis=0))
+    cols_ref[:, :128] = jnp.transpose(jnp.concatenate([gain_sum, shift_sum, sums_in_ref[2:, :], pad], axis=0))
     turn_rows(size, near_ref, far_ref, left_ref)
     for e, target in enumerate((kept_ref, send_ref)):
-        value = dot_f32(grad_rows(place_ref, self_t_ref, dp_count, e), d_one_ref[...].astype(BF))
-        put_grad(target, value, 0, size.tile_rows)
+        put_grad(target, dot_f32(grad_rows(place_ref, self_t_ref, dp_count, e), low_one), 0, size.tile_rows)
         put_grad(target, dot_f32(grad_rows(place_ref, low_t_ref, dp_count, e), d_q_ref[...]), 1, size.tile_rows)
         lefts = grad_rows(place_ref, left_ref, dp_count, e)
         for t in range(2):
@@ -693,47 +721,84 @@
         put_grad(target, grad_rows(place_ref, cols_ref, dp_count, e), 4, size.tile_rows)
 
 
-def cross_grads(size, place, near, far, d_kv, d_q, low_t, mixed_self, d_one, sums):
-    own, width = d_one.shape
+def third(
+    size, visits, place, q, do, o, lse, kv, qseg, kseg, near, far, whole, hat, inv, norms, d_two, sums, mixed_self
+):
+    own, width = hat.shape
     group = (size.x_count, size.pieces, 5 * size.tile_rows, width)
     return kernel_call(
-        functools.partial(cross_grads_kernel, size),
-        out_shape=(shape(group), shape(group)),
-        in_specs=[SMEM] + [VMEM] * 8,
-        out_specs=(VMEM,) * 2,
-        scratch_shapes=[
+        functools.partial(third_kernel, size),
+        us=30,
+        out_shape=(
+            shape((size.length // 2, width)),
+            shape((size.length // 2, width)),
+            shape(group),
+            shape(group),
+            shape((own, width), F32),
+            shape((own, width)),
+        ),
+        in_specs=[SMEM] * 2 + [VMEM] * 16,
+        out_specs=(VMEM,) * 6,
+        scratch_shapes=back_scratch(size, width)
+        + [
+            pltpu.VMEM((own, width), BF),
+            pltpu.VMEM((size.length, 2 * width), BF),
             pltpu.VMEM((width, size.length), BF),
+            pltpu.VMEM((width, own), BF),
             pltpu.VMEM((width, own), BF),
             pltpu.VMEM((width, width), F32),
         ],
-    )(place, near, far, d_kv, d_q, low_t, mixed_self, d_one, sums)
-
-
-def self_grads_kernel(size, place_ref, near_ref, far_ref, d_kv_ref, d_q_ref, kept_ref, send_ref, left_ref, own_t_ref):
-    width = d_q_ref.shape[1]
-    dp_count = 2 * size.x_count
-    turn_rows(size, near_ref, far_ref, left_ref)
-    own_t_ref[...] = jnp.transpose(own_tokens(near_ref, place_ref, size.half, size.z_count))
-    for e, target in enumerate((kept_ref, send_ref)):
-        put_grad(target, dot_f32(grad_rows(place_ref, own_t_ref, dp_count, e), d_q_ref[...]), 0, size.tile_rows)
-        lefts = grad_rows(place_ref, left_ref, dp_count, e)
-        for t in range(2):
-            put_grad(target, dot_f32(lefts, d_kv_ref[:, t * width : (t + 1) * width]), 1 + t, size.tile_rows)
-
-
-def self_grads(size, place, near, far, d_kv, d_q):
-    own, width = d_q.shape
-    group = (size.x_count, size.pieces, 3 * size.tile_rows, width)
-    return kernel_call(
-        functools.partial(self_grads_kernel, size),
-        out_shape=(shape(group), shape(group)),
-        in_specs=[SMEM] + [VMEM] * 4,
-        out_specs=(VMEM,) * 2,
-        scratch_shapes=[pltpu.VMEM((width, size.length), BF), pltpu.VMEM((width, own), BF)],
-    )(place, near, far, d_kv, d_q)
-
-
-def back_self_kernel(size, place_ref, d_kv_ref, d_q_ref, whole_ref, d_one_ref, kept_rows_ref, send_rows_ref):
+    )(visits, place, q, do, o, lse, kv, qseg, kseg, near, far, whole, hat, inv, norms, d_two, sums, mixed_self)
+
+
+def fourth_kernel(
+    size,
+    visit_ref,
+    place_ref,
+    q_ref,
+    do_ref,
+    o_ref,
+    lse_ref,
+    kv_ref,
+    qseg_ref,
+    kseg_ref,
+    whole_ref,
+    d_one_ref,
+    near_ref,
+    far_ref,
+    kept_rows_ref,
+    send_rows_ref,
+    kept_ref,
+    send_ref,
+    seg_ref,
+    sum_ref,
+    dqt_ref,
+    qst_ref,
+    dst_ref,
+    delta_ref,
+    d_q_ref,
+    d_kv_ref,
+    left_ref,
+    own_t_ref,
+):
+    turn_segments(kseg_ref, seg_ref)
+    attend_back_part(
+        visit_ref,
+        q_ref,
+        do_ref,
+        o_ref,
+        lse_ref,
+        kv_ref,
+        qseg_ref,
+        seg_ref,
+        d_q_ref,
+        d_kv_ref,
+        sum_ref,
+        dqt_ref,
+        qst_ref,
+        dst_ref,
+        delta_ref,
+    )
     back_pairs(size, d_kv_ref, whole_ref[1], whole_ref[2], kept_rows_ref, send_rows_ref)
     mine = d_one_ref[...] + dot_nt(d_q_ref[...], whole_ref[0])
     half = size.half
@@ -742,16 +807,34 @@
         at = pl.ds(pl.multiple_of((z * y_count + place_ref[3]) * half, half), half)
         total = kept_rows_ref[at, :].astype(F32) + mine[z * half : (z + 1) * half]
         kept_rows_ref[at, :] = total.astype(kept_rows_ref.dtype)
-
-
-def back_self(size, place, d_kv, d_q, whole, d_one):
-    width = d_one.shape[1]
+    width = d_one_ref.shape[1]
+    dp_count = 2 * size.x_count
+    turn_rows(size, near_ref, far_ref, left_ref)
+    own_t_ref[...] = jnp.transpose(own_tokens(near_ref, place_ref, half, size.z_count))
+    for e, target in enumerate((kept_ref, send_ref)):
+        put_grad(target, dot_f32(grad_rows(place_ref, own_t_ref, dp_count, e), d_q_ref[...]), 0, size.tile_rows)
+        lefts = grad_rows(place_ref, left_ref, dp_count, e)
+        for t in range(2):
+            put_grad(target, dot_f32(lefts, d_kv_ref[:, t * width : (t + 1) * width]), 1 + t, size.tile_rows)
+
+
+def fourth(size, visits, place, q, do, o, lse, kv, qseg, kseg, whole, d_one, near, far):
+    own, width = d_one.shape
+    group = (size.x_count, size.pieces, 3 * size.tile_rows, width)
     return kernel_call(
-        functools.partial(back_self_kernel, size),
-        out_shape=(shape((size.length // 2, width)), shape((size.length // 2, width))),
-        in_specs=[SMEM] + [VMEM] * 4,
-        out_specs=(VMEM,) * 2,
-    )(place, d_kv, d_q, whole, d_one)
+        functools.partial(fourth_kernel, size),
+        us=27,
+        out_shape=(shape((size.length // 2, width)), shape((size.length // 2, width)), shape(group), shape(group)),
+        in_specs=[SMEM] * 2 + [VMEM] * 11,
+        out_specs=(VMEM,) * 4,
+        scratch_shapes=back_scratch(size, width)
+        + [
+            pltpu.VMEM((own, width), BF),
+            pltpu.VMEM((size.length, 2 * width), BF),
+            pltpu.VMEM((width, size.length), BF),
+            pltpu.VMEM((width, own), BF),
+        ],
+    )(visits, place, q, do, o, lse, kv, qseg, kseg, whole, d_one, near, far)
 
 
 def together(*values):
@@ -852,11 +935,15 @@
             out.append(jnp.concatenate([pick(mine, x_place ^ k) for k in range(x_count)])[None])
         return out
 
-    def x_sum(kept, came):
-        total = kept[0].astype(F32) + came[0]
-        for k in range(1, x_count):
-            total = total + over_x((kept[k].astype(F32) + came[k]).astype(BF), k)
-        return total
+    def x_moves(kept, came):
+        out = [(kept[0].astype(F32) + came[0]).astype(BF)]
+        return out + [over_x((kept[k].astype(F32) + came[k]).astype(BF), k) for k in range(1, x_count)]
+
+    def total(values):
+        out = values[0].astype(F32)
+        for v in values[1:]:
+            out = out + v
+        return out.astype(BF)
 
     def by_owner(v, outer):
         if fine:
@@ -865,12 +952,12 @@
         inner = inner.reshape(seq_count, -1, width)
         return jnp.concatenate([inner, v[0, v.shape[1] - outer :].reshape(seq_count, -1, width)], axis=1)
 
-    def y_sum(v):
+    def y_parts(v):
         v = v.reshape((z_count, y_count) + v.shape[1:])
-        total = pick(v, y_place, 1)
-        for k in range(1, y_count):
-            total = total + over_y(pick(v, y_place ^ k, 1).astype(BF), k)
-        return total
+        return [over_y(pick(v, y_place ^ k, 1), k) for k in range(y_count)]
+
+    def z_parts(v):
+        return [over_z(pick(v, z_place ^ k), k) for k in range(z_count)]
 
     def untiled(v):
         return v.reshape(-1, rows, width).transpose(1, 0, 2).reshape(rows, -1)
@@ -894,7 +981,7 @@
 
     def in_order(segments):
         pairs = segments.reshape(-1, 2, half)
-        return jnp.where(c_place == 0, pairs, pairs[:, ::-1]).reshape(-1, keys)
+        return jnp.where(c_place == 0, pairs, pairs[:, ::-1]).reshape(-1, 1, keys)
 
     def visits(segments):
         low = jnp.sum((segments[None, :] < qseg[:, :1]).astype(jnp.int32), axis=1, dtype=jnp.int32)
@@ -921,45 +1008,52 @@
         pieces=pieces,
         tile_rows=tile_rows,
         hidden=hidden,
-        first=half if fine else 0,
-    )
+        feed_rows=hidden // width * tile_rows + outer * seq_count // pieces,
+        first_one=(half,) if fine else (0,),
+        first_two=(half,) if fine else (0,),
+        first_three=(0,),
+    )
+    qseg = qseg[:, None, :]
     streams = jnp.stack([inputs, encoder, cotangent]).reshape(3, held, 2, half, width)
     mine = pick(streams, c_place, 2)
     other = over_core(pick(streams, 1 - c_place, 2))
     streams = by_core(mine, other, 1)
     x_blocks, source_blocks, cot = streams[0], streams[1], streams[2]
     if fine:
-        w1 = jnp.stack([over_x(first_tiles, k) for k in range(x_count)])
+        x_blocks = with_weights(x_blocks, jnp.stack([over_x(first_tiles, k) for k in range(x_count)]))
         rest = jnp.stack([over_x(rest_tiles, k) for k in range(x_count)])
-        x_blocks = with_weights(x_blocks, w1)
         source_blocks = with_weights(source_blocks, rest[:, :mid])
         cot = with_weights(cot, rest[:, mid:])
     x_near = exchange_z(x_blocks)
     x_near, source_blocks = together(x_near, source_blocks)
-    x_near = y_gather(x_near)
+    x_moves_y = y_moves(x_near)
     source_near = exchange_z(source_blocks)
+    x_near = y_order(x_moves_y)
     x_far = over_core(x_near)
+    x_near, x_far, source_near, cot = together(x_near, x_far, source_near, cot)
+    source_moves = y_moves(source_near)
+    cot = exchange_z(cot)
     weights = (x_near, x_far) if fine else coarse_parts(first_tiles, 0)
 
-    queries, pairs, whole_one = project(size, place, weights, x_near, x_far)
+    queries, pairs, whole_one, mixed_self, self_lse = first(
+        size, self_visits, place, weights, x_near, x_far, qseg, self_kseg
+    )
     whole_one = whole_one.reshape(3, width, width)
-    queries, source_near, cot = together(queries, source_near, cot)
-    source_near = y_gather(source_near)
-    cot = exchange_z(cot)
-    mixed_self, self_lse = attend(self_visits, queries, pairs, qseg, self_kseg)
-    mixed_self, source_near, cot = together(mixed_self, source_near, cot)
+    mixed_self, cot, *source_moves = together(mixed_self, cot, *source_moves)
+    source_near = y_order(source_moves)
     source_far = over_core(source_near)
-    mixed_self, source_far = together(mixed_self, source_far)
-    w3 = y_moves(cot[:, half:]) if fine else None
-    weights = (source_near, source_far) if fine else coarse_parts(rest_tiles[:mid], 0)
-    queries_c, pairs_c, whole_two, hat_one, inv_one, norms = bridge(
-        size, place, weights, x_near, source_near, source_far, mixed_self
+    if fine:
+        w3_moves = y_moves(cot[:, half:])
+        weights = (source_near, source_far)
+    else:
+        weights = coarse_parts(rest_tiles[:mid], 0)
+    queries_c, pairs_c, whole_two, hat_one, inv_one, norms, mixed_cross, cross_lse = second(
+        size, cross_visits, place, weights, x_near, source_near, source_far, mixed_self, qseg, cross_kseg
     )
     whole_two = whole_two.reshape(6, width, width)
-    mixed_cross, cross_lse = attend(cross_visits, queries_c, pairs_c, qseg, cross_kseg)
     if fine:
-        mixed_cross, w3 = together(mixed_cross, w3)
-        w3 = y_order(w3)
+        mixed_cross, *w3_moves = together(mixed_cross, *w3_moves)
+        w3 = y_order(w3_moves)
         weights = (w3, over_core(w3))
     else:
         weights = coarse_parts(rest_tiles[mid:], outer)
@@ -967,55 +1061,86 @@
         size, place, weights, mixed_cross, whole_two, hat_one, norms, cot
     )
 
-    out_parts = exchange_z(out_low.reshape(z_count, half, width))
     f_send = feed_grads(size, 1, place, low_t, dz, hid, down, mixed_ct, d_two)
     f_came = over_core(f_send)
-    low_t, f_send = together(low_t, f_send)
+    low_t, f_send, out_low = together(low_t, f_send, out_low)
     f_kept = feed_grads(size, 0, place, low_t, dz, hid, down, mixed_ct, d_two)
+    out_parts = exchange_z(out_low.reshape(z_count, half, width))
     d_mixed_c, f_kept, f_came = together(d_mixed_c, f_kept, f_came)
-    f_sum = x_sum(f_kept, f_came)
-    d_queries_c, d_pairs_c = attend_back(
-        cross_visits, queries_c, d_mixed_c, mixed_cross, cross_lse, pairs_c, qseg, cross_kseg
-    )
-    s_kept, s_send, d_one, d_mixed, sums, low_one_t = back_cross(
-        size, place, d_pairs_c, d_queries_c, whole_two, hat_one, inv_one, norms, d_two, sums
-    )
-    d_one, f_sum, s_send, s_kept, out_parts = together(d_one, f_sum, s_send, s_kept, out_parts)
-    s_came = over_core(s_send)
-    f_sum = y_sum(by_owner(f_sum, hidden // dp_count))
-    c_kept, c_send = cross_grads(
-        size, place, source_near, source_far, d_pairs_c, d_queries_c, low_one_t, mixed_self, d_one, sums
-    )
-    d_mixed, s_came, c_send, f_sum = together(d_mixed, s_came, c_send, f_sum)
-    c_came = over_core(c_send)
-    s_sum = y_sum((s_kept.astype(F32) + s_came).reshape(seq_count, half, width))
-    f_sum = exchange_z(f_sum.astype(BF))
-    d_queries, d_pairs = attend_back(
-        self_visits, queries, d_mixed, mixed_self, self_lse, pairs, qseg, self_kseg
-    )
-    d_pairs, s_sum, c_came, f_sum = together(d_pairs, s_sum, c_came, f_sum)
-    s_parts = exchange_z(s_sum.astype(BF))
-    c_sum = x_sum(c_kept, c_came)
-    x_kept, x_send = back_self(size, place, d_pairs, d_queries, whole_one, d_one)
-    x_came = over_core(x_send)
-    d_pairs, x_send = together(d_pairs, x_send)
-    i_kept, i_send = self_grads(size, place, x_near, x_far, d_pairs, d_queries)
-    i_came = over_core(i_send)
-    x_came, x_kept, i_send, s_parts = together(x_came, x_kept, i_send, s_parts)
-    x_total = (x_kept.astype(F32) + x_came).astype(BF)
-    x_parts = exchange(x_total.reshape(seq_count, half, width))
-    x_total, i_came, i_kept = together(x_total, i_came, i_kept)
-    i_sum = x_sum(i_kept, i_came)
-    i_kept, s_parts, out_parts, f_sum = together(i_kept, s_parts, out_parts, f_sum)
-    grad_source = home(s_parts)
+    f_moves = x_moves(f_kept, f_came)
+    d_mixed_c, f_first = together(d_mixed_c, f_moves[0])
+    s_kept, s_send, c_kept, c_send, d_one, d_mixed = third(
+        size,
+        cross_visits,
+        place,
+        queries_c,
+        d_mixed_c,
+        mixed_cross,
+        cross_lse,
+        pairs_c,
+        qseg,
+        cross_kseg,
+        source_near,
+        source_far,
+        whole_two,
+        hat_one,
+        inv_one,
+        norms,
+        d_two,
+        sums,
+        mixed_self,
+    )
+    s_kept, s_send, c_kept, c_send, d_one, d_mixed, out_parts, f_first, *f_moves = together(
+        s_kept, s_send, c_kept, c_send, d_one, d_mixed, out_parts, f_first, *f_moves[1:]
+    )
+    s_came, c_came = over_core(s_send), over_core(c_send)
+    f_sum = by_owner(total([f_first, *f_moves]), hidden // dp_count)
+    f_sum, s_came, c_came = together(f_sum, s_came, c_came)
+    s_sum = total([s_kept, s_came]).reshape(seq_count, half, width)
+    fs_moves = y_parts(jnp.concatenate([f_sum, s_sum], axis=1))
+    c_moves = x_moves(c_kept, c_came)
+    d_mixed, fs_first, c_first = together(d_mixed, fs_moves[0], c_moves[0])
+    x_kept, x_send, i_kept, i_send = fourth(
+        size,
+        self_visits,
+        place,
+        queries,
+        d_mixed,
+        mixed_self,
+        self_lse,
+        pairs,
+        qseg,
+        self_kseg,
+        whole_one,
+        d_one,
+        x_near,
+        x_far,
+    )
+    extra = len(fs_moves) - 1
+    x_kept, x_send, i_kept, i_send, fs_first, c_first, out_parts, *moves = together(
+        x_kept, x_send, i_kept, i_send, fs_first, c_first, out_parts, *fs_moves[1:], *c_moves[1:]
+    )
+    x_came, i_came = over_core(x_send), over_core(i_send)
+    fs_parts = z_parts(total([fs_first, *moves[:extra]]))
+    x_came, i_came, fs_first = together(x_came, i_came, fs_parts[0])
+    x_moves_y = y_parts(total([x_kept, x_came]).reshape(seq_count, half, width))
+    x_first, i_came, i_kept = together(x_moves_y[0], i_came, i_kept)
+    i_moves = x_moves(i_kept, i_came)
+    c_sum = by_owner(total([c_first, *moves[extra:]]), 0)
+    i_first, c_sum, *x_moves_y = together(i_moves[0], c_sum, x_first, *x_moves_y[1:])
+    x_parts = exchange_z(total(x_moves_y))
+    i_sum = by_owner(total([i_first, *i_moves[1:]]), 0)
+    w_moves = y_parts(jnp.concatenate([c_sum, i_sum], axis=1))
+    w_first, out_parts, fs_first, *fs_parts = together(w_moves[0], out_parts, fs_first, *fs_parts[1:])
+    fs_parts = [fs_first] + fs_parts
+    grad_source = home(unxor([v[-half:] for v in fs_parts], z_place))
     out_tokens = home(out_parts)
-    f_own = jnp.sum(f_sum.astype(F32), axis=0)
-    w_sum = y_sum(jnp.concatenate([by_owner(c_sum, 0), by_owner(i_sum, 0)], axis=1))
-    w_own = pick(w_sum, z_place)
-    for k in range(1, z_count):
-        w_own = w_own + over_z(pick(w_sum, z_place ^ k).astype(BF), k)
+    f_own = sum((v[:-half].astype(F32) for v in fs_parts[1:]), fs_parts[0][:-half].astype(F32))
+    w_parts = z_parts(total([w_first, *w_moves[1:]]))
+    w_first, x_parts = together(w_parts[0], x_parts)
+    w_own = sum(w_parts[1:], w_first.astype(F32))
     c_own, i_own = w_own[: 5 * rows], w_own[5 * rows :]
-    grad_tokens = home(jnp.sum(x_parts.reshape(z_count, y_count, half, width).astype(F32), axis=1))
+    grad_tokens = home(x_parts)
     f_in = hidden // width * rows
     c_own = c_own.reshape(5, rows, width)
     return (

time: 359 us -> 340 us (0.947); the launches traced: 353 us -> 340 us
  waiting for transfers between devices: 90.7 us -> 119 us
  local copies, waits for them, and re-layouts: 56.9 us -> 32.7 us
  Pallas kernels: 102 us -> 92.4 us
  other arithmetic: 39.6 us -> 30.5 us
    ppermute x3 -> x6, waiting for transfers between devices: 8.41 us -> 27.4 us  [over_z(): lax.ppermute(v, 'seq', [(i, i ^ k * y_count) for i in range(seq_count)])]
    unnamed x160 -> x112, local copies, waits for them, and re-layouts: 42.7 us -> 24.3 us
    ppermute x3 -> x6, starting transfers between devices: 4.98 us -> 20.5 us  [over_z(): lax.ppermute(v, 'seq', [(i, i ^ k * y_count) for i in range(seq_count)])]
    all_to_all x6 -> x5, waiting for transfers between devices: 16.4 us -> 29.3 us  [exchange_z(): return lax.all_to_all(v, 'seq', 0, 0, tiled=True, axis_index_groups=groups)]
    add x8 -> x2, other arithmetic: 12.4 us -> 0.13 us  [the longest x1 0.07 us: body(): sum((v[:-half].astype(F32) for v in fs_parts[1:]), fs_parts[0][:-half].as...]
    pallas_call x13 -> x7, Pallas kernels: 102 us -> 92.4 us  [call(): pl.pallas_call(kernel, out_shape=out_shape, in_specs=in_specs, out_specs=...]
    ppermute x6, waiting for transfers between devices: 46 us -> 40.1 us  [over_y(): lax.ppermute(v, 'seq', [(i, i ^ k) for i in range(seq_count)])]
    convert_element_type x4 -> x11, other arithmetic: 6.47 us -> 12.2 us  [the longest x8 7.12 us: total(): return out.astype(BF)]
  transfers between devices with their start and end apart: 34 -> 35, of which waited for: 16 -> 20; matrix products, arithmetic and copies ran while one was open for 12% -> 6% of each run, Pallas kernels for 24% -> 23%
where the time goes in v1:
time: 340 us
  waiting for transfers between devices  119 us (35%)
  Pallas kernels  92.4 us (27%)
  starting transfers between devices  64.2 us (19%)
  local copies, waits for them, and re-layouts  32.7 us (10%)
  other arithmetic  30.5 us (9%)
    pallas_call x7, Pallas kernels, call(): pl.pallas_call(kernel, out_shape=out_shape, in_specs=in_specs, out_specs=...  92.4 us
    ppermute x6, waiting for transfers between devices, over_y(): lax.ppermute(v, 'seq', [(i, i ^ k) for i in range(seq_count)])  40.1 us
    all_to_all x5, waiting for transfers between devices, exchange_z(): return lax.all_to_all(v, 'seq', 0, 0, tiled=True, axis_index_groups=groups)  29.3 us
    ppermute x6, waiting for transfers between devices, over_z(): lax.ppermute(v, 'seq', [(i, i ^ k * y_count) for i in range(seq_count)])  27.4 us
    unnamed x112, local copies, waits for them, and re-layouts  24.3 us
    all_to_all x5, starting transfers between devices, exchange_z(): return lax.all_to_all(v, 'seq', 0, 0, tiled=True, axis_index_groups=groups)  23.9 us
    ppermute x6, starting transfers between devices, over_z(): lax.ppermute(v, 'seq', [(i, i ^ k * y_count) for i in range(seq_count)])  20.5 us
    ppermute x13, waiting for transfers between devices, over_core(): return lax.ppermute(v, 'dp', [(i, i ^ 1) for i in range(dp_count)])  15.7 us
  transfers between devices with their start and end apart: 35, of which 20 were waited for; matrix products, arithmetic and copies ran while one was open for 6% of the time, Pallas kernels for 23%

profile of v1, /device:TPU:0, one launch (start us, length us, event | category | flops | bytes accessed | tf_op | source)
XLA Modules:
  0.0 340.3 jit_solution(7264626124000607793)
XLA Ops:
  3.1 3.0 collective-permute-start.2
  10.4 5.5 %all-to-all-start = ((bf16[4,224,512]{2,1,0:T(8,128)(2,1)}), bf16[4,224,512]{2,1,0:T(8,128)(2,1)S(1)}, u32[]{:S(2)}, u32[]{:S(2)}) async-start(bf16[4,224,512]{2,1,0:T(8,128)(2,1)} %pad_maximum_fusion.4), calls=%async_computation | async-start | bytes 1835008 | tf_op jit(solution)/shard_map/all_to_all | solution.py:909
  17.9 4.5 %collective-permute-done.3 = bf16[224,512]{1,0:T(8,128)(2,1)S(1)} collective-permute-done((bf16[224,512]{1,0:T(8,128)(2,1)S(1)}, bf16[224,512]{1,0:T(8,128)(2,1)S(1)}, u32[]{:S(2)}, u32[]{:S(2)}) %collective-permute-start.3) | collective-permute-done | bytes 229408 | tf_op jit(solution)/shard_map/ppermute | solution.py:888
  23.6 14.2 %all-to-all-done = bf16[4,224,512]{2,1,0:T(8,128)(2,1)S(1)} async-done(((bf16[4,224,512]{2,1,0:T(8,128)(2,1)}), bf16[4,224,512]{2,1,0:T(8,128)(2,1)S(1)}, u32[]{:S(2)}, u32[]{:S(2)}) %all-to-all-start) | async-done | bytes 917536 | tf_op jit(solution)/shard_map/all_to_all | solution.py:909
  39.3 3.5 %all-to-all-start.1 = ((bf16[4,320,512]{2,1,0:T(8,128)(2,1)}), bf16[4,320,512]{2,1,0:T(8,128)(2,1)S(1)}, u32[]{:S(2)}, u32[]{:S(2)}) async-start(bf16[4,320,512]{2,1,0:T(8,128)(2,1)} %pad_maximum_fusion.2), calls=%async_computation.1 | async-start | bytes 2621440 | tf_op jit(solution)/shard_map/all_to_all | solution.py:909
  42.9 16.2 %collective-permute-done.4 = bf16[4,224,512]{2,1,0:T(8,128)(2,1)S(1)} collective-permute-done((bf16[4,224,512]{2,1,0:T(8,128)(2,1)S(1)}, bf16[4,224,512]{2,1,0:T(8,128)(2,1)S(1)}, u32[]{:S(2)}, u32[]{:S(2)}) %collective-permute-start.4) | collective-permute-done | bytes 917536 | tf_op jit(solution)/shard_map/ppermute | solution.py:891
  61.9 11.5 %all-to-all-done.1 = bf16[4,320,512]{2,1,0:T(8,128)(2,1)S(1)} async-done(((bf16[4,320,512]{2,1,0:T(8,128)(2,1)}), bf16[4,320,512]{2,1,0:T(8,128)(2,1)S(1)}, u32[]{:S(2)}, u32[]{:S(2)}) %all-to-all-start.1) | async-done | bytes 1310752 | tf_op jit(solution)/shard_map/all_to_all | solution.py:909
  74.5 3.7 %all-to-all-start.2 = ((bf16[4,384,512]{2,1,0:T(8,128)(2,1)}), bf16[4,384,512]{2,1,0:T(8,128)(2,1)S(1)}, u32[]{:S(2)}, u32[]{:S(2)}) async-start(bf16[4,384,512]{2,1,0:T(8,128)(2,1)} %pad_maximum_fusion.1), calls=%async_computation.2 | async-start | bytes 3145728 | tf_op jit(solution)/shard_map/all_to_all | solution.py:909
  80.9 14.9 %shard_map.212 = (bf16[512,512]{1,0:T(8,128)(2,1)S(1)}, bf16[2048,1024]{1,0:T(8,128)(2,1)S(1)}, bf16[3,32,16,512]{3,2,1,0:T(8,128)(2,1)S(1)}, bf16[512,512]{1,0:T(8,128)(2,1)S(1)}, f32[8,1,512]{2,1,0:T(1,128)S(1)}) custom-call(s32[2,8]{1,0:T(2,128)S(1)} %pad.11.visit_ref, s32[4]{0:T(128)S(1)} %pad_add_fusion.2.place_ref, bf16[8,224,512]{2,1,0:T(8,128)(2,1)S(1)} %bitcast.197, ...), custom_call_target="tpu_custom_call" | custom-call | flops 1840000000 | bytes 1024 | tf_op jit(solution)/shard_map/pallas_call | solution.py:52
  100.6 10.2 %collective-permute-done.6 = bf16[4,320,512]{2,1,0:T(8,128)(2,1)} collective-permute-done((bf16[4,320,512]{2,1,0:T(8,128)(2,1)}, bf16[4,320,512]{2,1,0:T(8,128)(2,1)}, u32[]{:S(2)}, u32[]{:S(2)}) %collective-permute-start.6) | collective-permute-done | bytes 1310752 | tf_op jit(solution)/shard_map/ppermute | solution.py:891
  110.9 3.6 %all-to-all-done.2.cot_ref = bf16[4,384,512]{2,1,0:T(8,128)(2,1)S(1)} async-done(((bf16[4,384,512]{2,1,0:T(8,128)(2,1)}), bf16[4,384,512]{2,1,0:T(8,128)(2,1)S(1)}, u32[]{:S(2)}, u32[]{:S(2)}) %all-to-all-start.2) | async-done | bytes 1572896 | tf_op jit(solution)/shard_map/all_to_all | solution.py:909
  114.5 4.3 %maximum_select_fusion = bf16[2,4,320,512]{3,2,0,1:T(8,128)(2,1)} fusion(bf16[1,4,320,512]{3,2,0,1:T(8,128)(2,1)} %bitcast.38, bf16[1,4,320,512]{3,2,0,1:T(8,128)(2,1)} %bitcast.212, pred[]{:T(512)S(6)} %eq.8), kind=kLoop, calls=%fused_computation | loop fusion | flops 3932160 | bytes 5242881 | tf_op jit(solution)/shard_map/jit(_where)/select_n | solution.py:846
  120.4 3.6 %collective-permute-done.7.source_far_ref.refs_1_.far_ref = bf16[8,320,512]{2,1,0:T(8,128)(2,1)} collective-permute-done((bf16[8,320,512]{2,1,0:T(8,128)(2,1)}, bf16[8,320,512]{2,1,0:T(8,128)(2,1)}, u32[]{:S(2)}, u32[]{:S(2)}) %collective-permute-start.7) | collective-permute-done | bytes 2621472 | tf_op jit(solution)/shard_map/ppermute | solution.py:885
  125.1 14.0 %shard_map.213 = (bf16[512,512]{1,0:T(8,128)(2,1)S(1)}, bf16[2048,1024]{1,0:T(8,128)(2,1)S(1)}, bf16[6,32,16,512]{3,2,1,0:T(8,128)(2,1)S(1)}, f32[512,512]{1,0:T...) custom-call(s32[2,8]{1,0:T(2,128)S(1)} %pad.13.visit_ref, ...), custom_call_target="tpu_custom_call" | custom-call | flops 1955000064 | bytes 1024 | tf_op jit(solution)/shard_map/pallas_call | solution.py:52
  142.6 3.1 collective-permute-done.8
  145.7 2.9 fusion
  148.8 4.1 %collective-permute-done.9.refs_1_ = bf16[8,256,512]{2,1,0:T(8,128)(2,1)S(1)} collective-permute-done((bf16[8,256,512]{2,1,0:T(8,128)(2,1)S(1)}, bf16[8,256,512]{2,1,0:T(8,128)(2,1)S(1)}, u32[]{:S(2)}, u32[]{:S(2)}) %collective-permute-start.9) | collective-permute-done | bytes 2097184 | tf_op jit(solution)/shard_map/ppermute | solution.py:885
  152.9 11.1 %shard_map.214 = (bf16[512,512]{1,0:T(8,128)(2,1)S(1)}, f32[512,512]{1,0:T(8,128)S(1)}, bf16[512,512]{1,0:T(8,128)(2,1)S(1)}, f32[8,512]{1,0:T(8,128)S(1)}, bf16...) custom-call(s32[4]{0:T(128)S(1)} %pad_add_fusion.2.place_ref, ...), custom_call_target="tpu_custom_call" | custom-call | flops 1380000000 | bytes 1024 | tf_op jit(solution)/shard_map/pallas_call | solution.py:52
  168.1 2.5 collective-permute-done.10
  174.9 4.1 %all-to-all-start.3 = ((bf16[4,128,512]{2,1,0:T(8,128)(2,1)}), bf16[4,128,512]{2,1,0:T(8,128)(2,1)}, u32[]{:S(2)}, u32[]{:S(2)}) async-start(bf16[4,128,512]{2,1,0:T(8,128)(2,1)} %bitcast.206), calls=%async_computation.3 | async-start | bytes 1048576 | tf_op jit(solution)/shard_map/all_to_all | solution.py:909
  184.4 24.4 %shard_map.217 = (bf16[1024,512]{1,0:T(8,128)(2,1)S(1)}, bf16[1024,512]{1,0:T(8,128)(2,1)S(1)}, bf16[2,8,80,512]{3,2,1,0:T(8,128)(2,1)S(1)}, bf16[2,8,80,512]{3,...) custom-call(s32[2,8]{1,0:T(2,128)S(1)} %pad.13.visit_ref, s32[4]{0:T(128)S(1)} %pad_add_fusion.2.place_ref, ...), custom_call_target="tpu_custom_call" | custom-call | flops 3449999872 | bytes 1024 | tf_op jit(solution)/shard_map/pallas_call | solution.py:52
  216.7 2.5 collective-permute-done.12
  222.0 2.6 collective-permute-start.14
  224.6 2.6 fusion.9
  228.4 24.2 %shard_map.218 = (bf16[1024,512]{1,0:T(8,128)(2,1)S(1)}, bf16[1024,512]{1,0:T(8,128)(2,1)}, bf16[2,8,48,512]{3,2,1,0:T(8,128)(2,1)S(1)}, bf16[2,8,48,512]{3,2,1,0:T(8,128)(2,1)}) custom-call(s32[2,8]{1,0:T(2,128)S(1)} %pad.11.visit_ref, s32[4]{0:T(128)S(1)} %pad_add_fusion.2.place_ref, bf16[512,512]{1,0:T(8,128)(2,1)S(1)} %copy-done.24, ...), custom_call_target="tpu_custom_call" | custom-call | flops 3104999936 | bytes 1024 | tf_op jit(solution)/shard_map/pallas_call | solution.py:52
  262.4 13.0 %collective-permute-start.20 = (bf16[272,512]{1,0:T(8,128)(2,1)S(1)}, bf16[272,512]{1,0:T(8,128)(2,1)S(1)}, u32[]{:S(2)}, u32[]{:S(2)}) collective-permute-start(bf16[272,512]{1,0:T(8,128)(2,1)S(1)} %get-tuple-element.266), channel_id=1, source_target_pairs={{0,2},{1,3},{2,0},{3,1},{4,6},{5,7},{6,4},{7,5},{8,10},{9,11},{10,... | collective-permute-start | bytes 835592 | tf_op jit(solution)/shard_map/ppermute | solution.py:894
  278.3 6.0 %collective-permute-done.20 = bf16[272,512]{1,0:T(8,128)(2,1)S(1)} collective-permute-done((bf16[272,512]{1,0:T(8,128)(2,1)S(1)}, bf16[272,512]{1,0:T(8,128)(2,1)S(1)}, u32[]{:S(2)}, u32[]{:S(2)}) %collective-permute-start.20) | collective-permute-done | bytes 278560 | tf_op jit(solution)/shard_map/ppermute | solution.py:894
  284.3 13.1 %collective-permute-done.21 = bf16[272,512]{1,0:T(8,128)(2,1)S(1)} collective-permute-done((bf16[272,512]{1,0:T(8,128)(2,1)S(1)}, bf16[272,512]{1,0:T(8,128)(2,1)S(1)}, u32[]{:S(2)}, u32[]{:S(2)}) %collective-permute-start.21) | collective-permute-done | bytes 278560 | tf_op jit(solution)/shard_map/ppermute | solution.py:894
  300.7 7.0 %all-to-all-start.4 = ((bf16[4,128,512]{2,1,0:T(8,128)(2,1)}), bf16[4,128,512]{2,1,0:T(8,128)(2,1)S(1)}, u32[]{:S(2)}, u32[]{:S(2)}) async-start(bf16[4,128,512]{2,1,0:T(8,128)(2,1)} %add_convert_fusion.9), calls=%async_computation.4 | async-start | bytes 1048576 | tf_op jit(solution)/shard_map/all_to_all | solution.py:909
  311.2 10.5 %collective-permute-done.24 = bf16[4,128,512]{2,1,0:T(8,128)(2,1)S(1)} collective-permute-done((bf16[4,128,512]{2,1,0:T(8,128)(2,1)S(1)}, bf16[4,128,512]{2,1,0:T(8,128)(2,1)S(1)}, u32[]{:S(2)}, u32[]{:S(2)}) %collective-permute-start.24) | collective-permute-done | bytes 524320 | tf_op jit(solution)/shard_map/ppermute | solution.py:891
  321.9 2.6 collective-permute-start.27
  328.4 8.0 %collective-permute-done.28 = bf16[128,512]{1,0:T(8,128)(2,1)S(1)} collective-permute-done((bf16[128,512]{1,0:T(8,128)(2,1)S(1)}, bf16[128,512]{1,0:T(8,128)(2,1)S(1)}, u32[]{:S(2)}, u32[]{:S(2)}) %collective-permute-start.28) | collective-permute-done | bytes 131104 | tf_op jit(solution)/shard_map/ppermute | solution.py:894
  (244 shorter events, 81.6 us)
Async XLA Ops:
  2.3 5.8 %collective-permute-start.1 = (bf16[3,2,128,512]{3,2,1,0:T(8,128)(2,1)S(1)}, bf16[3,2,128,512]{3,2,1,0:T(8,128)(2,1)S(1)}, u32[]{:S(2)}, u32[]{:S(2)}) collective-permute-start(bf16[3,2,128,512]{3,2,1,0:T(8,128)(2,1)S(1)} %get-tuple-element.263), channel_id=1, source_target_pairs={{0,8},{8,0},{16,24},{24,16},{1,9},{9,1},{17,25},{25,17},{2,10},{10... | collective-permute-start | bytes 2359304 | tf_op jit(solution)/shard_map/ppermute | solution.py:885
  3.1 5.1 %collective-permute-start.2 = (bf16[48,512]{1,0:T(8,128)(2,1)S(1)}, bf16[48,512]{1,0:T(8,128)(2,1)S(1)}, u32[]{:S(2)}, u32[]{:S(2)}) collective-permute-start(bf16[48,512]{1,0:T(8,128)(2,1)S(1)} %bitcast.238), channel_id=1, source_target_pairs={{0,16},{8,24},{16,0},{24,8},{1,17},{9,25},{17,1},{25,9},{2,18},{10... | collective-permute-start | bytes 147464 | tf_op jit(solution)/shard_map/ppermute | solution.py:888
  10.4 27.4 %all-to-all-start = ((bf16[4,224,512]{2,1,0:T(8,128)(2,1)}), bf16[4,224,512]{2,1,0:T(8,128)(2,1)S(1)}, u32[]{:S(2)}, u32[]{:S(2)}) async-start(bf16[4,224,512]{2,1,0:T(8,128)(2,1)} %pad_maximum_fusion.4), calls=%async_computation | async-start | bytes 1835008 | tf_op jit(solution)/shard_map/all_to_all | solution.py:909
  16.3 6.1 %collective-permute-start.3 = (bf16[224,512]{1,0:T(8,128)(2,1)S(1)}, bf16[224,512]{1,0:T(8,128)(2,1)S(1)}, u32[]{:S(2)}, u32[]{:S(2)}) collective-permute-start(bf16[224,512]{1,0:T(8,128)(2,1)S(1)} %get-tuple-element.287), channel_id=1, source_target_pairs={{0,16},{8,24},{16,0},{24,8},{1,17},{9,25},{17,1},{25,9},{2,18},{10... | collective-permute-start | bytes 688136 | tf_op jit(solution)/shard_map/ppermute | solution.py:888
  37.8 21.3 %collective-permute-start.4 = (bf16[4,224,512]{2,1,0:T(8,128)(2,1)S(1)}, bf16[4,224,512]{2,1,0:T(8,128)(2,1)S(1)}, u32[]{:S(2)}, u32[]{:S(2)}) collective-permute-start(bf16[4,224,512]{2,1,0:T(8,128)(2,1)S(1)} %all-to-all-done), channel_id=1, source_target_pairs={{0,1},{1,0},{2,3},{3,2},{4,5},{5,4},{6,7},{7,6},{8,9},{9,8},{10,11... | collective-permute-start | bytes 2752520 | tf_op jit(solution)/shard_map/ppermute | solution.py:891
  39.3 34.1 %all-to-all-start.1 = ((bf16[4,320,512]{2,1,0:T(8,128)(2,1)}), bf16[4,320,512]{2,1,0:T(8,128)(2,1)S(1)}, u32[]{:S(2)}, u32[]{:S(2)}) async-start(bf16[4,320,512]{2,1,0:T(8,128)(2,1)} %pad_maximum_fusion.2), calls=%async_computation.1 | async-start | bytes 2621440 | tf_op jit(solution)/shard_map/all_to_all | solution.py:909
  59.5 13.8 %collective-permute-start.5 = (bf16[8,224,512]{2,1,0:T(8,128)(2,1)S(1)}, bf16[8,224,512]{2,1,0:T(8,128)(2,1)}, u32[]{:S(2)}, u32[]{:S(2)}) collective-permute-start(bf16[8,224,512]{2,1,0:T(8,128)(2,1)S(1)} %bitcast.196), channel_id=1, source_target_pairs={{0,8},{8,0},{16,24},{24,16},{1,9},{9,1},{17,25},{25,17},{2,10},{10... | collective-permute-start | bytes 5505032 | tf_op jit(solution)/shard_map/ppermute | solution.py:885
  74.5 40.0 %all-to-all-start.2 = ((bf16[4,384,512]{2,1,0:T(8,128)(2,1)}), bf16[4,384,512]{2,1,0:T(8,128)(2,1)S(1)}, u32[]{:S(2)}, u32[]{:S(2)}) async-start(bf16[4,384,512]{2,1,0:T(8,128)(2,1)} %pad_maximum_fusion.1), calls=%async_computation.2 | async-start | bytes 3145728 | tf_op jit(solution)/shard_map/all_to_all | solution.py:909
  79.6 31.2 %collective-permute-start.6 = (bf16[4,320,512]{2,1,0:T(8,128)(2,1)}, bf16[4,320,512]{2,1,0:T(8,128)(2,1)}, u32[]{:S(2)}, u32[]{:S(2)}) collective-permute-start(bf16[4,320,512]{2,1,0:T(8,128)(2,1)} %copy-done.35), channel_id=1, source_target_pairs={{0,1},{1,0},{2,3},{3,2},{4,5},{5,4},{6,7},{7,6},{8,9},{9,8},{10,11... | collective-permute-start | bytes 3932168 | tf_op jit(solution)/shard_map/ppermute | solution.py:891
  118.8 5.3 %collective-permute-start.7 = (bf16[8,320,512]{2,1,0:T(8,128)(2,1)}, bf16[8,320,512]{2,1,0:T(8,128)(2,1)}, u32[]{:S(2)}, u32[]{:S(2)}) collective-permute-start(bf16[8,320,512]{2,1,0:T(8,128)(2,1)} %bitcast.40.source_near_ref.refs_0_.near_ref), channel_id=1, source_target_pairs={{0,8},{8,0},{16,24},{24,16},{1,9},{9,1},{17,25},{25,17},{2,10},{10... | collective-permute-start | bytes 7864328 | tf_op jit(solution)/shard_map/ppermute | solution.py:885
  119.8 25.9 %collective-permute-start.8 = (bf16[4,256,512]{2,1,0:T(8,128)(2,1)}, bf16[4,256,512]{2,1,0:T(8,128)(2,1)}, u32[]{:S(2)}, u32[]{:S(2)}) collective-permute-start(bf16[4,256,512]{2,1,0:T(8,128)(2,1)} %slice.140), channel_id=1, source_target_pairs={{0,1},{1,0},{2,3},{3,2},{4,5},{5,4},{6,7},{7,6},{8,9},{9,8},{10,11... | collective-permute-start | bytes 3145736 | tf_op jit(solution)/shard_map/ppermute | solution.py:891
  148.7 4.2 %collective-permute-start.9 = (bf16[8,256,512]{2,1,0:T(8,128)(2,1)S(1)}, bf16[8,256,512]{2,1,0:T(8,128)(2,1)S(1)}, u32[]{:S(2)}, u32[]{:S(2)}) collective-permute-start(bf16[8,256,512]{2,1,0:T(8,128)(2,1)S(1)} %bitcast.203), channel_id=1, source_target_pairs={{0,8},{8,0},{16,24},{24,16},{1,9},{9,1},{17,25},{25,17},{2,10},{10... | collective-permute-start | bytes 6291464 | tf_op jit(solution)/shard_map/ppermute | solution.py:885
  166.0 4.6 %collective-permute-start.10 = (bf16[2,8,144,512]{3,2,1,0:T(8,128)(2,1)S(1)}, bf16[2,8,144,512]{3,2,1,0:T(8,128)(2,1)S(1)}, u32[]{:S(2)}, u32[]{:S(2)}) collective-permute-start(bf16[2,8,144,512]{3,2,1,0:T(8,128)(2,1)S(1)} %shard_map.215), channel_id=1, source_target_pairs={{0,8},{8,0},{16,24},{24,16},{1,9},{9,1},{17,25},{25,17},{2,10},{10... | collective-permute-start | bytes 7077896 | tf_op jit(solution)/shard_map/ppermute | solution.py:885
  172.8 40.7 %collective-permute-start.11 = (bf16[8,144,512]{2,1,0:T(8,128)(2,1)}, bf16[8,144,512]{2,1,0:T(8,128)(2,1)}, u32[]{:S(2)}, u32[]{:S(2)}) collective-permute-start(bf16[8,144,512]{2,1,0:T(8,128)(2,1)} %get-tuple-element.251), channel_id=1, source_target_pairs={{0,16},{8,24},{16,0},{24,8},{1,17},{9,25},{17,1},{25,9},{2,18},{10... | collective-permute-start | bytes 3538952 | tf_op jit(solution)/shard_map/ppermute | solution.py:888
  174.9 38.7 %all-to-all-start.3 = ((bf16[4,128,512]{2,1,0:T(8,128)(2,1)}), bf16[4,128,512]{2,1,0:T(8,128)(2,1)}, u32[]{:S(2)}, u32[]{:S(2)}) async-start(bf16[4,128,512]{2,1,0:T(8,128)(2,1)} %bitcast.206), calls=%async_computation.3 | async-start | bytes 1048576 | tf_op jit(solution)/shard_map/all_to_all | solution.py:909
  213.6 5.6 %collective-permute-start.13 = (bf16[2,8,80,512]{3,2,1,0:T(8,128)(2,1)}, bf16[2,8,80,512]{3,2,1,0:T(8,128)(2,1)}, u32[]{:S(2)}, u32[]{:S(2)}) collective-permute-start(bf16[2,8,80,512]{3,2,1,0:T(8,128)(2,1)} %get-tuple-element.154), channel_id=1, source_target_pairs={{0,8},{8,0},{16,24},{24,16},{1,9},{9,1},{17,25},{25,17},{2,10},{10... | collective-permute-start | bytes 3932168 | tf_op jit(solution)/shard_map/ppermute | solution.py:885
  214.7 4.5 %collective-permute-start.12 = (bf16[1024,512]{1,0:T(8,128)(2,1)}, bf16[1024,512]{1,0:T(8,128)(2,1)}, u32[]{:S(2)}, u32[]{:S(2)}) collective-permute-start(bf16[1024,512]{1,0:T(8,128)(2,1)} %copy-done.34), channel_id=1, source_target_pairs={{0,8},{8,0},{16,24},{24,16},{1,9},{9,1},{17,25},{25,17},{2,10},{10... | collective-permute-start | bytes 3145736 | tf_op jit(solution)/shard_map/ppermute | solution.py:885
  222.0 31.4 %collective-permute-start.14 = (bf16[4,272,512]{2,1,0:T(8,128)(2,1)S(1)}, bf16[4,272,512]{2,1,0:T(8,128)(2,1)}, u32[]{:S(2)}, u32[]{:S(2)}) collective-permute-start(bf16[4,272,512]{2,1,0:T(8,128)(2,1)S(1)} %get-tuple-element.255), channel_id=1, source_target_pairs={{0,1},{1,0},{2,3},{3,2},{4,5},{5,4},{6,7},{7,6},{8,9},{9,8},{10,11... | collective-permute-start | bytes 3342344 | tf_op jit(solution)/shard_map/ppermute | solution.py:891
  227.2 26.2 %collective-permute-start.15 = (bf16[8,80,512]{2,1,0:T(8,128)(2,1)S(1)}, bf16[8,80,512]{2,1,0:T(8,128)(2,1)S(1)}, u32[]{:S(2)}, u32[]{:S(2)}) collective-permute-start(bf16[8,80,512]{2,1,0:T(8,128)(2,1)S(1)} %get-tuple-element.253), channel_id=1, source_target_pairs={{0,16},{8,24},{16,0},{24,8},{1,17},{9,25},{17,1},{25,9},{2,18},{10... | collective-permute-start | bytes 1966088 | tf_op jit(solution)/shard_map/ppermute | solution.py:888
  254.3 5.5 %collective-permute-start.16 = (bf16[1024,512]{1,0:T(8,128)(2,1)}, bf16[1024,512]{1,0:T(8,128)(2,1)S(1)}, u32[]{:S(2)}, u32[]{:S(2)}) collective-permute-start(bf16[1024,512]{1,0:T(8,128)(2,1)} %get-tuple-element.173), channel_id=1, source_target_pairs={{0,8},{8,0},{16,24},{24,16},{1,9},{9,1},{17,25},{25,17},{2,10},{10... | collective-permute-start | bytes 3145736 | tf_op jit(solution)/shard_map/ppermute | solution.py:885
  260.2 17.8 %collective-permute-start.18 = (bf16[4,128,512]{2,1,0:T(8,128)(2,1)S(1)}, bf16[4,128,512]{2,1,0:T(8,128)(2,1)S(1)}, u32[]{:S(2)}, u32[]{:S(2)}) collective-permute-start(bf16[4,128,512]{2,1,0:T(8,128)(2,1)S(1)} %get-tuple-element.270), channel_id=1, source_target_pairs={{0,1},{1,0},{2,3},{3,2},{4,5},{5,4},{6,7},{7,6},{8,9},{9,8},{10,11... | collective-permute-start | bytes 1572872 | tf_op jit(solution)/shard_map/ppermute | solution.py:891
  261.5 16.5 %collective-permute-start.19 = (bf16[8,48,512]{2,1,0:T(8,128)(2,1)S(1)}, bf16[8,48,512]{2,1,0:T(8,128)(2,1)S(1)}, u32[]{:S(2)}, u32[]{:S(2)}) collective-permute-start(bf16[8,48,512]{2,1,0:T(8,128)(2,1)S(1)} %get-tuple-element.258), channel_id=1, source_target_pairs={{0,16},{8,24},{16,0},{24,8},{1,17},{9,25},{17,1},{25,9},{2,18},{10... | collective-permute-start | bytes 1179656 | tf_op jit(solution)/shard_map/ppermute | solution.py:888
  262.4 21.9 %collective-permute-start.20 = (bf16[272,512]{1,0:T(8,128)(2,1)S(1)}, bf16[272,512]{1,0:T(8,128)(2,1)S(1)}, u32[]{:S(2)}, u32[]{:S(2)}) collective-permute-start(bf16[272,512]{1,0:T(8,128)(2,1)S(1)} %get-tuple-element.266), channel_id=1, source_target_pairs={{0,2},{1,3},{2,0},{3,1},{4,6},{5,7},{6,4},{7,5},{8,10},{9,11},{10,... | collective-permute-start | bytes 835592 | tf_op jit(solution)/shard_map/ppermute | solution.py:894
  275.4 22.0 %collective-permute-start.21 = (bf16[272,512]{1,0:T(8,128)(2,1)S(1)}, bf16[272,512]{1,0:T(8,128)(2,1)S(1)}, u32[]{:S(2)}, u32[]{:S(2)}) collective-permute-start(bf16[272,512]{1,0:T(8,128)(2,1)S(1)} %get-tuple-element.265), channel_id=1, source_target_pairs={{0,4},{1,5},{2,6},{3,7},{4,0},{5,1},{6,2},{7,3},{8,12},{9,13},{10,... | collective-permute-start | bytes 835592 | tf_op jit(solution)/shard_map/ppermute | solution.py:894
  275.4 22.0 %collective-permute-start.22 = (bf16[272,512]{1,0:T(8,128)(2,1)S(1)}, bf16[272,512]{1,0:T(8,128)(2,1)S(1)}, u32[]{:S(2)}, u32[]{:S(2)}) collective-permute-start(bf16[272,512]{1,0:T(8,128)(2,1)S(1)} %get-tuple-element.264), channel_id=1, source_target_pairs={{0,6},{1,7},{2,4},{3,5},{4,2},{5,3},{6,0},{7,1},{8,14},{9,15},{10,... | collective-permute-start | bytes 835592 | tf_op jit(solution)/shard_map/ppermute | solution.py:894
  299.7 10.0 %collective-permute-start.26 = (bf16[2,128,512]{2,1,0:T(8,128)(2,1)S(1)}, bf16[2,128,512]{2,1,0:T(8,128)(2,1)S(1)}, u32[]{:S(2)}, u32[]{:S(2)}) collective-permute-start(bf16[2,128,512]{2,1,0:T(8,128)(2,1)S(1)} %get-tuple-element.277), channel_id=1, source_target_pairs={{0,8},{8,0},{16,24},{24,16},{1,9},{9,1},{17,25},{25,17},{2,10},{10... | collective-permute-start | bytes 786440 | tf_op jit(solution)/shard_map/ppermute | solution.py:885
  300.7 27.4 %all-to-all-start.4 = ((bf16[4,128,512]{2,1,0:T(8,128)(2,1)}), bf16[4,128,512]{2,1,0:T(8,128)(2,1)S(1)}, u32[]{:S(2)}, u32[]{:S(2)}) async-start(bf16[4,128,512]{2,1,0:T(8,128)(2,1)} %add_convert_fusion.9), calls=%async_computation.4 | async-start | bytes 1048576 | tf_op jit(solution)/shard_map/all_to_all | solution.py:909
  307.7 14.0 %collective-permute-start.24 = (bf16[4,128,512]{2,1,0:T(8,128)(2,1)S(1)}, bf16[4,128,512]{2,1,0:T(8,128)(2,1)S(1)}, u32[]{:S(2)}, u32[]{:S(2)}) collective-permute-start(bf16[4,128,512]{2,1,0:T(8,128)(2,1)S(1)} %get-tuple-element.268), channel_id=1, source_target_pairs={{0,1},{1,0},{2,3},{3,2},{4,5},{5,4},{6,7},{7,6},{8,9},{9,8},{10,11... | collective-permute-start | bytes 1572872 | tf_op jit(solution)/shard_map/ppermute | solution.py:891
  321.9 6.5 %collective-permute-start.27 = (bf16[128,512]{1,0:T(8,128)(2,1)S(1)}, bf16[128,512]{1,0:T(8,128)(2,1)S(1)}, u32[]{:S(2)}, u32[]{:S(2)}) collective-permute-start(bf16[128,512]{1,0:T(8,128)(2,1)S(1)} %get-tuple-element.272), channel_id=1, source_target_pairs={{0,2},{1,3},{2,0},{3,1},{4,6},{5,7},{6,4},{7,5},{8,10},{9,11},{10,... | collective-permute-start | bytes 393224 | tf_op jit(solution)/shard_map/ppermute | solution.py:894
  324.5 11.9 %collective-permute-start.28 = (bf16[128,512]{1,0:T(8,128)(2,1)S(1)}, bf16[128,512]{1,0:T(8,128)(2,1)S(1)}, u32[]{:S(2)}, u32[]{:S(2)}) collective-permute-start(bf16[128,512]{1,0:T(8,128)(2,1)S(1)} %get-tuple-element.274), channel_id=1, source_target_pairs={{0,4},{1,5},{2,6},{3,7},{4,0},{5,1},{6,2},{7,3},{8,12},{9,13},{10,... | collective-permute-start | bytes 393224 | tf_op jit(solution)/shard_map/ppermute | solution.py:894
  326.1 10.4 %collective-permute-start.29 = (bf16[128,512]{1,0:T(8,128)(2,1)S(1)}, bf16[128,512]{1,0:T(8,128)(2,1)S(1)}, u32[]{:S(2)}, u32[]{:S(2)}) collective-permute-start(bf16[128,512]{1,0:T(8,128)(2,1)S(1)} %get-tuple-element.273), channel_id=1, source_target_pairs={{0,6},{1,7},{2,4},{3,5},{4,2},{5,3},{6,0},{7,1},{8,14},{9,15},{10,... | collective-permute-start | bytes 393224 | tf_op jit(solution)/shard_map/ppermute | solution.py:894
  328.1 11.0 %collective-permute-start.25 = (bf16[2,128,512]{2,1,0:T(8,128)(2,1)S(1)}, bf16[2,128,512]{2,1,0:T(8,128)(2,1)S(1)}, u32[]{:S(2)}, u32[]{:S(2)}) collective-permute-start(bf16[2,128,512]{2,1,0:T(8,128)(2,1)S(1)} %get-tuple-element.279), channel_id=1, source_target_pairs={{0,8},{8,0},{16,24},{24,16},{1,9},{9,1},{17,25},{25,17},{2,10},{10... | collective-permute-start | bytes 786440 | tf_op jit(solution)/shard_map/ppermute | solution.py:885
  (55 other events, 242.8 us)

commit v2 on v1

--- a/solution.py
+++ b/solution.py
@@ -13,6 +13,7 @@
 GROUP = 4
 LANES = GROUP * HEAD_DIM
 PACE = 1.15e9 * 0.1
+WIDE = 60
 CHUNK = 256
 LOG2E = 1.4426950408889634
 LN2 = 0.6931471805599453
@@ -23,6 +24,7 @@
 SMEM = pl.BlockSpec(memory_space=pltpu.SMEM)
 VMEM = pl.BlockSpec(memory_space=pltpu.VMEM)
 ANY = pl.BlockSpec(memory_space=pl.ANY)
+NOW, LATER = "now", "later"
 
 
 def dot_f32(left, right):
@@ -56,6 +58,65 @@
             out_specs=out_specs,
             scratch_shapes=scratch_shapes,
             compiler_params=pltpu.CompilerParams(vmem_limit_bytes=need),
+            cost_estimate=pl.CostEstimate(flops=int(us * PACE), bytes_accessed=2**10, transcendentals=0),
+        )(*operands)
+
+    return call
+
+
+class Moves:
+    def __init__(self, now, late, out):
+        self.now, self.late, self.out, self.begun = now, late, out, set()
+
+    def begin(self):
+        for copy in self.now:
+            copy.wait()
+
+    def ready(self):
+        for copy in self.late:
+            copy.wait()
+
+    def done(self, *results):
+        for i in results:
+            self.out[i].start()
+            self.begun.add(i)
+
+    def finish(self):
+        self.done(*(i for i in range(len(self.out)) if i not in self.begun))
+        for copy in self.out:
+            copy.wait()
+
+
+def run_kernel(kernel, *, out_shape, kinds, scratch_shapes=(), us=2):
+    def call(*operands):
+        moved = [i for i, kind in enumerate(kinds) if kind in (NOW, LATER)]
+        count, outs, own = len(kinds), len(out_shape), len(scratch_shapes)
+
+        def wrapped(*refs):
+            ins, results, scratch = list(refs[:count]), refs[count : count + outs], refs[count + outs :]
+            mine, scratch = scratch[:own], scratch[own:]
+            slots, scratch = scratch[: len(moved)], scratch[len(moved) :]
+            made, (in_sem, out_sem) = scratch[:outs], scratch[outs:]
+            now, late = [], []
+            for n, i in enumerate(moved):
+                copy = pltpu.make_async_copy(ins[i], slots[n], in_sem.at[n])
+                copy.start()
+                (now if kinds[i] == NOW else late).append(copy)
+                ins[i] = slots[n]
+            moves = Moves(now, late, [pltpu.make_async_copy(a, b, out_sem.at[n]) for n, (a, b) in enumerate(zip(made, results))])
+            kernel(*ins, *made, *mine, moves=moves)
+            moves.finish()
+
+        return pl.pallas_call(
+            wrapped,
+            out_shape=out_shape,
+            in_specs=[SMEM if kind is SMEM else ANY for kind in kinds],
+            out_specs=(ANY,) * outs,
+            scratch_shapes=list(scratch_shapes)
+            + [pltpu.VMEM(operands[i].shape, operands[i].dtype) for i in moved]
+            + [pltpu.VMEM(v.shape, v.dtype) for v in out_shape]
+            + [pltpu.SemaphoreType.DMA((len(moved),)), pltpu.SemaphoreType.DMA((outs,))],
+            compiler_params=pltpu.CompilerParams(vmem_limit_bytes=WIDE * 2**20),
             cost_estimate=pl.CostEstimate(flops=int(us * PACE), bytes_accessed=2**10, transcendentals=0),
         )(*operands)
 
@@ -195,8 +256,6 @@
     total = kv_ref.shape[0]
     keys = total // visit_ref.shape[1]
     groups = width // LANES
-    sum_ref[...] = jnp.zeros(sum_ref.shape, F32)
-
     def block(k, carry):
         lo, hi = visit_ref[0, k], visit_ref[1, k]
         q_rows = pl.ds(pl.multiple_of(k * rows, rows), rows)
@@ -349,15 +408,18 @@
     qseg_ref,
     kseg_ref,
     *refs,
+    moves,
 ):
     weights, (q_ref, kv_ref, whole_ref, o_ref, lse_ref, seg_ref, acc_ref, qst_ref, sem) = refs[:-9], refs[-9:]
     copies = fetch_tiles(size, place_ref, weights, 3, size.first_one, whole_ref, sem)
+    moves.begin()
     own = own_tokens(near_ref, place_ref, size.half, size.z_count)
     turn_segments(kseg_ref, seg_ref)
     for copy in copies:
         copy.wait()
     q_ref[...] = (dot_f32(own, tile_of(whole_ref, 0)) * (HEAD_DIM**-0.5 * LOG2E)).astype(BF)
     put_pairs(near_ref, far_ref, size.half, tile_of(whole_ref, 1), tile_of(whole_ref, 2), kv_ref)
+    moves.done(0, 1, 2)
     attend_part(visit_ref, q_ref, kv_ref, qseg_ref, seg_ref, o_ref, lse_ref, acc_ref, qst_ref)
 
 
@@ -367,7 +429,7 @@
 
 def first(size, visits, place, weights, near, far, qseg, kseg):
     width = near.shape[2]
-    return kernel_call(
+    return run_kernel(
         functools.partial(first_kernel, size),
         us=16,
         out_shape=(
@@ -377,8 +439,7 @@
             shape((size.own, width)),
             lse_shape(size, width),
         ),
-        in_specs=[SMEM] * 2 + [VMEM] * 4 + [ANY] * len(weights),
-        out_specs=(VMEM,) * 5,
+        kinds=[SMEM] * 2 + [NOW] * 4 + [ANY] * len(weights),
         scratch_shapes=attend_scratch(size, width) + [pltpu.SemaphoreType.DMA((2 * size.x_count * 3,))],
     )(visits, place, near, far, qseg, kseg, *weights)
 
@@ -394,10 +455,12 @@
     qseg_ref,
     kseg_ref,
     *refs,
+    moves,
 ):
     weights = refs[:-12]
     q_ref, kv_ref, whole_ref, hat_ref, inv_ref, norm_ref, o_ref, lse_ref, seg_ref, acc_ref, qst_ref, sem = refs[-12:]
     copies = fetch_tiles(size, place_ref, weights, 6, size.first_two, whole_ref, sem)
+    moves.begin()
     own = own_tokens(near_ref, place_ref, size.half, size.z_count)
     turn_segments(kseg_ref, seg_ref)
     for copy in copies:
@@ -408,13 +471,15 @@
     inv_ref[...] = inv
     low = (hat * norm_ref[0:1, :] + norm_ref[1:2, :]).astype(BF)
     q_ref[...] = (dot_f32(low, tile_of(whole_ref, 1)) * (HEAD_DIM**-0.5 * LOG2E)).astype(BF)
+    moves.ready()
     put_pairs(source_near_ref, source_far_ref, size.half, tile_of(whole_ref, 2), tile_of(whole_ref, 3), kv_ref)
+    moves.done(0, 1, 2, 3, 4, 5)
     attend_part(visit_ref, q_ref, kv_ref, qseg_ref, seg_ref, o_ref, lse_ref, acc_ref, qst_ref)
 
 
 def second(size, visits, place, weights, near, source_near, source_far, mixed, qseg, kseg):
     width = near.shape[2]
-    return kernel_call(
+    return run_kernel(
         functools.partial(second_kernel, size),
         us=17,
         out_shape=(
@@ -427,8 +492,7 @@
             shape((size.own, width)),
             lse_shape(size, width),
         ),
-        in_specs=[SMEM] * 2 + [VMEM] * 6 + [ANY] * len(weights),
-        out_specs=(VMEM,) * 8,
+        kinds=[SMEM] * 2 + [NOW, LATER, LATER, NOW, NOW, NOW] + [ANY] * len(weights),
         scratch_shapes=attend_scratch(size, width) + [pltpu.SemaphoreType.DMA((2 * size.x_count * 6,))],
     )(visits, place, near, source_near, source_far, mixed, qseg, kseg, *weights)
 
@@ -676,9 +740,12 @@
     self_t_ref,
     low_t_ref,
     cols_ref,
+    moves,
 ):
     width = hat_ref.shape[1]
     dp_count = 2 * size.x_count
+    sum_ref[...] = jnp.zeros(sum_ref.shape, F32)
+    moves.begin()
     turn_segments(kseg_ref, seg_ref)
     attend_back_part(
         visit_ref,
@@ -697,6 +764,7 @@
         dst_ref,
         delta_ref,
     )
+    moves.ready()
     hat, inv, gain = hat_ref[...], inv_ref[...], norm_ref[0:1, :]
     upstream = d_two_ref[...] + dot_nt(d_q_ref[...], whole_ref[1])
     gain_sum = jnp.sum(upstream * hat, axis=0, keepdims=True)
@@ -707,6 +775,7 @@
     d_mixed_ref[...] = dot_nt(low_one, whole_ref[0]).astype(BF)
     low_t_ref[...] = jnp.transpose((hat * gain + norm_ref[1:2, :]).astype(BF))
     back_pairs(size, d_kv_ref, whole_ref[2], whole_ref[3], kept_rows_ref, send_rows_ref)
+    moves.done(0, 1, 4, 5)
     self_t_ref[...] = jnp.transpose(mixed_self_ref[...])
     pad = jnp.zeros((128 - sums_in_ref.shape[0], width), F32)
     cols_ref[...] = jnp.zeros(cols_ref.shape, F32)
@@ -726,7 +795,7 @@
 ):
     own, width = hat.shape
     group = (size.x_count, size.pieces, 5 * size.tile_rows, width)
-    return kernel_call(
+    return run_kernel(
         functools.partial(third_kernel, size),
         us=30,
         out_shape=(
@@ -737,8 +806,7 @@
             shape((own, width), F32),
             shape((own, width)),
         ),
-        in_specs=[SMEM] * 2 + [VMEM] * 16,
-        out_specs=(VMEM,) * 6,
+        kinds=[SMEM] * 2 + [NOW] * 7 + [LATER] * 9,
         scratch_shapes=back_scratch(size, width)
         + [
             pltpu.VMEM((own, width), BF),
@@ -780,7 +848,10 @@
     d_kv_ref,
     left_ref,
     own_t_ref,
+    moves,
 ):
+    sum_ref[...] = jnp.zeros(sum_ref.shape, F32)
+    moves.begin()
     turn_segments(kseg_ref, seg_ref)
     attend_back_part(
         visit_ref,
@@ -799,6 +870,7 @@
         dst_ref,
         delta_ref,
     )
+    moves.ready()
     back_pairs(size, d_kv_ref, whole_ref[1], whole_ref[2], kept_rows_ref, send_rows_ref)
     mine = d_one_ref[...] + dot_nt(d_q_ref[...], whole_ref[0])
     half = size.half
@@ -807,6 +879,7 @@
         at = pl.ds(pl.multiple_of((z * y_count + place_ref[3]) * half, half), half)
         total = kept_rows_ref[at, :].astype(F32) + mine[z * half : (z + 1) * half]
         kept_rows_ref[at, :] = total.astype(kept_rows_ref.dtype)
+    moves.done(0, 1)
     width = d_one_ref.shape[1]
     dp_count = 2 * size.x_count
     turn_rows(size, near_ref, far_ref, left_ref)
@@ -821,12 +894,11 @@
 def fourth(size, visits, place, q, do, o, lse, kv, qseg, kseg, whole, d_one, near, far):
     own, width = d_one.shape
     group = (size.x_count, size.pieces, 3 * size.tile_rows, width)
-    return kernel_call(
+    return run_kernel(
         functools.partial(fourth_kernel, size),
         us=27,
         out_shape=(shape((size.length // 2, width)), shape((size.length // 2, width)), shape(group), shape(group)),
-        in_specs=[SMEM] * 2 + [VMEM] * 11,
-        out_specs=(VMEM,) * 4,
+        kinds=[SMEM] * 2 + [NOW] * 7 + [LATER] * 4,
         scratch_shapes=back_scratch(size, width)
         + [
             pltpu.VMEM((own, width), BF),

time: 340 us -> 326 us (0.959); the launches traced: 340 us -> 321 us
  local copies, waits for them, and re-layouts: 32.7 us -> 10.5 us
  waiting for transfers between devices: 119 us -> 124 us
  starting transfers between devices: 64.2 us -> 60.2 us
  Pallas kernels: 92.4 us -> 96 us
    pallas_call x0 -> x4, Pallas kernels: none -> 80.9 us  [call(): pl.pallas_call(wrapped, out_shape=out_shape, in_specs=[SMEM if kind is SM...]
    pallas_call x7 -> x3, Pallas kernels: 92.4 us -> 15.1 us  [call(): pl.pallas_call(kernel, out_shape=out_shape, in_specs=in_specs, out_specs=...]
    unnamed x112 -> x66, local copies, waits for them, and re-layouts: 24.3 us -> 2.88 us
    ppermute x6, starting transfers between devices: 20.5 us -> 10.1 us  [over_z(): lax.ppermute(v, 'seq', [(i, i ^ k * y_count) for i in range(seq_count)])]
    ppermute x6, waiting for transfers between devices: 40.1 us -> 44.6 us  [over_y(): lax.ppermute(v, 'seq', [(i, i ^ k) for i in range(seq_count)])]
    ppermute x5, starting transfers between devices: 8.64 us -> 12.9 us  [over_x(): lax.ppermute(v, 'dp', [(i, i ^ 2 * k) for i in range(dp_count)])]
    ppermute x6, waiting for transfers between devices: 27.4 us -> 23.4 us  [over_z(): lax.ppermute(v, 'seq', [(i, i ^ k * y_count) for i in range(seq_count)])]
  transfers between devices with their start and end apart: 35 -> 35, of which waited for: 20 -> 22; matrix products, arithmetic and copies ran while one was open for 6% -> 6% of each run, Pallas kernels for 23% -> 26%
where the time goes in v2:
time: 326 us; the launch traced here: 321 us
  waiting for transfers between devices  124 us (38%)
  Pallas kernels  96 us (29%)
  starting transfers between devices  60.2 us (18%)
  other arithmetic  28.6 us (9%)
  local copies, waits for them, and re-layouts  10.5 us (3%)
    pallas_call x4, Pallas kernels, call(): pl.pallas_call(wrapped, out_shape=out_shape, in_specs=[SMEM if kind is SM...  80.9 us
    ppermute x6, waiting for transfers between devices, over_y(): lax.ppermute(v, 'seq', [(i, i ^ k) for i in range(seq_count)])  44.6 us
    all_to_all x5, waiting for transfers between devices, exchange_z(): return lax.all_to_all(v, 'seq', 0, 0, tiled=True, axis_index_groups=groups)  29 us
    all_to_all x5, starting transfers between devices, exchange_z(): return lax.all_to_all(v, 'seq', 0, 0, tiled=True, axis_index_groups=groups)  24.7 us
    ppermute x6, waiting for transfers between devices, over_z(): lax.ppermute(v, 'seq', [(i, i ^ k * y_count) for i in range(seq_count)])  23.4 us
    ppermute x13, waiting for transfers between devices, over_core(): return lax.ppermute(v, 'dp', [(i, i ^ 1) for i in range(dp_count)])  18.2 us
    pallas_call x3, Pallas kernels, call(): pl.pallas_call(kernel, out_shape=out_shape, in_specs=in_specs, out_specs=...  15.1 us
    ppermute x5, starting transfers between devices, over_x(): lax.ppermute(v, 'dp', [(i, i ^ 2 * k) for i in range(dp_count)])  12.9 us
  transfers between devices with their start and end apart: 35, of which 22 were waited for; matrix products, arithmetic and copies ran while one was open for 6% of the time, Pallas kernels for 26%

profile of v2, /device:TPU:0, one launch (start us, length us, event | category | flops | bytes accessed | tf_op | source)
XLA Modules:
  0.0 321.1 jit_solution(4571540219862929998)
XLA Ops:
  3.1 3.0 collective-permute-start.2
  10.4 5.5 %all-to-all-start = ((bf16[4,224,512]{2,1,0:T(8,128)(2,1)}), bf16[4,224,512]{2,1,0:T(8,128)(2,1)S(1)}, u32[]{:S(2)}, u32[]{:S(2)}) async-start(bf16[4,224,512]{2,1,0:T(8,128)(2,1)} %pad_maximum_fusion.4), calls=%async_computation | async-start | bytes 1835008 | tf_op jit(solution)/shard_map/all_to_all | solution.py:981
  17.9 4.5 %collective-permute-done.3 = bf16[224,512]{1,0:T(8,128)(2,1)S(1)} collective-permute-done((bf16[224,512]{1,0:T(8,128)(2,1)S(1)}, bf16[224,512]{1,0:T(8,128)(2,1)S(1)}, u32[]{:S(2)}, u32[]{:S(2)}) %collective-permute-start.3) | collective-permute-done | bytes 229408 | tf_op jit(solution)/shard_map/ppermute | solution.py:960
  23.6 14.1 %all-to-all-done = bf16[4,224,512]{2,1,0:T(8,128)(2,1)S(1)} async-done(((bf16[4,224,512]{2,1,0:T(8,128)(2,1)}), bf16[4,224,512]{2,1,0:T(8,128)(2,1)S(1)}, u32[]{:S(2)}, u32[]{:S(2)}) %all-to-all-start) | async-done | bytes 917536 | tf_op jit(solution)/shard_map/all_to_all | solution.py:981
  39.3 3.5 %all-to-all-start.1 = ((bf16[4,320,512]{2,1,0:T(8,128)(2,1)}), bf16[4,320,512]{2,1,0:T(8,128)(2,1)S(1)}, u32[]{:S(2)}, u32[]{:S(2)}) async-start(bf16[4,320,512]{2,1,0:T(8,128)(2,1)} %pad_maximum_fusion.2), calls=%async_computation.1 | async-start | bytes 2621440 | tf_op jit(solution)/shard_map/all_to_all | solution.py:981
  42.9 16.2 %collective-permute-done.4 = bf16[4,224,512]{2,1,0:T(8,128)(2,1)S(1)} collective-permute-done((bf16[4,224,512]{2,1,0:T(8,128)(2,1)S(1)}, bf16[4,224,512]{2,1,0:T(8,128)(2,1)S(1)}, u32[]{:S(2)}, u32[]{:S(2)}) %collective-permute-start.4) | collective-permute-done | bytes 917536 | tf_op jit(solution)/shard_map/ppermute | solution.py:963
  62.3 11.1 %all-to-all-done.1 = bf16[4,320,512]{2,1,0:T(8,128)(2,1)S(1)} async-done(((bf16[4,320,512]{2,1,0:T(8,128)(2,1)}), bf16[4,320,512]{2,1,0:T(8,128)(2,1)S(1)}, u32[]{:S(2)}, u32[]{:S(2)}) %all-to-all-start.1) | async-done | bytes 1310752 | tf_op jit(solution)/shard_map/all_to_all | solution.py:981
  73.4 3.7 %all-to-all-start.2 = ((bf16[4,384,512]{2,1,0:T(8,128)(2,1)}), bf16[4,384,512]{2,1,0:T(8,128)(2,1)S(1)}, u32[]{:S(2)}, u32[]{:S(2)}) async-start(bf16[4,384,512]{2,1,0:T(8,128)(2,1)} %pad_maximum_fusion.1), calls=%async_computation.2 | async-start | bytes 3145728 | tf_op jit(solution)/shard_map/all_to_all | solution.py:981
  80.9 16.4 %shard_map.212 = (bf16[512,512]{1,0:T(8,128)(2,1)}, bf16[2048,1024]{1,0:T(8,128)(2,1)}, bf16[3,32,16,512]{3,2,1,0:T(8,128)(2,1)}, bf16[512,512]{1,0:T(8,128)(2,1)}, f32[8,1,512]{2,1,0:T(1,128)}) custom-call(s32[2,8]{1,0:T(2,128)} %pad.11.refs_0_, s32[4]{0:T(128)} %pad_add_fusion.2.refs_1_.place_ref, bf16[8,224,512]{2,1,0:T(8,128)(2,1)} %bitcast.201, ...), custom_call_target="tpu_custom_call" | custom-call | flops 1840000000 | bytes 1024 | tf_op jit(solution)/shard_map/pallas_call | solution.py:110
  97.4 12.2 %collective-permute-done.6 = bf16[4,320,512]{2,1,0:T(8,128)(2,1)} collective-permute-done((bf16[4,320,512]{2,1,0:T(8,128)(2,1)S(1)}, bf16[4,320,512]{2,1,0:T(8,128)(2,1)}, u32[]{:S(2)}, u32[]{:S(2)}) %collective-permute-start.6) | collective-permute-done | bytes 1310752 | tf_op jit(solution)/shard_map/ppermute | solution.py:963
  109.6 3.8 %all-to-all-done.2.cot_ref = bf16[4,384,512]{2,1,0:T(8,128)(2,1)S(1)} async-done(((bf16[4,384,512]{2,1,0:T(8,128)(2,1)}), bf16[4,384,512]{2,1,0:T(8,128)(2,1)S(1)}, u32[]{:S(2)}, u32[]{:S(2)}) %all-to-all-start.2) | async-done | bytes 1572896 | tf_op jit(solution)/shard_map/all_to_all | solution.py:981
  113.4 3.5 %maximum_select_fusion = bf16[2,4,320,512]{3,2,0,1:T(8,128)(2,1)} fusion(bf16[1,4,320,512]{3,2,0,1:T(8,128)(2,1)} %bitcast.38, bf16[1,4,320,512]{3,2,0,1:T(8,128)(2,1)S(1)} %bitcast.205, pred[]{:T(512)S(6)} %eq.8), kind=kLoop, calls=%fused_computation | loop fusion | flops 3932160 | bytes 5242881 | tf_op jit(solution)/shard_map/jit(_where)/select_n | solution.py:918
  118.8 3.4 %collective-permute-done.7.refs_4_.refs_9_.refs_10_ = bf16[8,320,512]{2,1,0:T(8,128)(2,1)} collective-permute-done((bf16[8,320,512]{2,1,0:T(8,128)(2,1)}, bf16[8,320,512]{2,1,0:T(8,128)(2,1)}, u32[]{:S(2)}, u32[]{:S(2)}) %collective-permute-start.7) | collective-permute-done | bytes 2621472 | tf_op jit(solution)/shard_map/ppermute | solution.py:957
  122.2 15.4 %shard_map.213 = (bf16[512,512]{1,0:T(8,128)(2,1)}, bf16[2048,1024]{1,0:T(8,128)(2,1)}, bf16[6,32,16,512]{3,2,1,0:T(8,128)(2,1)}, f32[512,512]{1,0:T(8,128)}, f3...) custom-call(s32[2,8]{1,0:T(2,128)} %pad.13.refs_0_, ...), custom_call_target="tpu_custom_call" | custom-call | flops 1955000064 | bytes 1024 | tf_op jit(solution)/shard_map/pallas_call | solution.py:110
  137.6 5.1 %collective-permute-done.8 = bf16[4,256,512]{2,1,0:T(8,128)(2,1)S(1)} collective-permute-done((bf16[4,256,512]{2,1,0:T(8,128)(2,1)S(1)}, bf16[4,256,512]{2,1,0:T(8,128)(2,1)S(1)}, u32[]{:S(2)}, u32[]{:S(2)}) %collective-permute-start.8) | collective-permute-done | bytes 1048608 | tf_op jit(solution)/shard_map/ppermute | solution.py:963
  143.3 4.1 %collective-permute-done.9.refs_1_ = bf16[8,256,512]{2,1,0:T(8,128)(2,1)S(1)} collective-permute-done((bf16[8,256,512]{2,1,0:T(8,128)(2,1)S(1)}, bf16[8,256,512]{2,1,0:T(8,128)(2,1)S(1)}, u32[]{:S(2)}, u32[]{:S(2)}) %collective-permute-start.9) | collective-permute-done | bytes 2097184 | tf_op jit(solution)/shard_map/ppermute | solution.py:957
  147.5 11.2 %shard_map.214 = (bf16[512,512]{1,0:T(8,128)(2,1)}, f32[512,512]{1,0:T(8,128)S(1)}, bf16[512,512]{1,0:T(8,128)(2,1)S(1)}, f32[8,512]{1,0:T(8,128)S(1)}, bf16[512...) custom-call(s32[4]{0:T(128)S(1)} %copy-done.8, ...), custom_call_target="tpu_custom_call" | custom-call | flops 1380000000 | bytes 1024 | tf_op jit(solution)/shard_map/pallas_call | solution.py:54
  162.8 2.5 collective-permute-done.10
  168.6 3.5 %all-to-all-start.3 = ((bf16[4,128,512]{2,1,0:T(8,128)(2,1)}), bf16[4,128,512]{2,1,0:T(8,128)(2,1)S(1)}, u32[]{:S(2)}, u32[]{:S(2)}) async-start(bf16[4,128,512]{2,1,0:T(8,128)(2,1)} %bitcast.50), calls=%async_computation.3 | async-start | bytes 1048576 | tf_op jit(solution)/shard_map/all_to_all | solution.py:981
  172.1 23.0 %shard_map.217 = (bf16[1024,512]{1,0:T(8,128)(2,1)}, bf16[1024,512]{1,0:T(8,128)(2,1)}, bf16[2,8,80,512]{3,2,1,0:T(8,128)(2,1)}, bf16[2,8,80,512]{3,2,1,0:T(8,12...) custom-call(s32[2,8]{1,0:T(2,128)} %pad.13.refs_0_, s32[4]{0:T(128)} %pad_add_fusion.2.refs_1_.place_ref, ...), custom_call_target="tpu_custom_call" | custom-call | flops 3449999872 | bytes 1024 | tf_op jit(solution)/shard_map/pallas_call | solution.py:110
  195.4 3.4 %collective-permute-start.13 = (bf16[2,8,80,512]{3,2,1,0:T(8,128)(2,1)}, bf16[2,8,80,512]{3,2,1,0:T(8,128)(2,1)}, u32[]{:S(2)}, u32[]{:S(2)}) collective-permute-start(bf16[2,8,80,512]{3,2,1,0:T(8,128)(2,1)} %get-tuple-element.154), channel_id=1, source_target_pairs={{0,8},{8,0},{16,24},{24,16},{1,9},{9,1},{17,25},{25,17},{2,10},{10... | collective-permute-start | bytes 3932168 | tf_op jit(solution)/shard_map/ppermute | solution.py:957
  199.2 4.1 %collective-permute-done.12 = bf16[1024,512]{1,0:T(8,128)(2,1)} collective-permute-done((bf16[1024,512]{1,0:T(8,128)(2,1)}, bf16[1024,512]{1,0:T(8,128)(2,1)}, u32[]{:S(2)}, u32[]{:S(2)}) %collective-permute-start.12) | collective-permute-done | bytes 1048608 | tf_op jit(solution)/shard_map/ppermute | solution.py:957
  206.6 2.5 fusion.9
  209.7 26.2 %shard_map.218 = (bf16[1024,512]{1,0:T(8,128)(2,1)}, bf16[1024,512]{1,0:T(8,128)(2,1)}, bf16[2,8,48,512]{3,2,1,0:T(8,128)(2,1)}, bf16[2,8,48,512]{3,2,1,0:T(8,128)(2,1)}) custom-call(s32[2,8]{1,0:T(2,128)} %pad.11.refs_0_, s32[4]{0:T(128)} %pad_add_fusion.2.refs_1_.place_ref, bf16[512,512]{1,0:T(8,128)(2,1)} %get-tuple-element.109.refs_2_, ...), custom_call_target="tpu_custom_call" | custom-call | flops 3104999936 | bytes 1024 | tf_op jit(solution)/shard_map/pallas_call | solution.py:110
  238.4 3.3 %collective-permute-done.17 = bf16[2,8,48,512]{3,2,1,0:T(8,128)(2,1)} collective-permute-done((bf16[2,8,48,512]{3,2,1,0:T(8,128)(2,1)}, bf16[2,8,48,512]{3,2,1,0:T(8,128)(2,1)}, u32[]{:S(2)}, u32[]{:S(2)}) %collective-permute-start.17) | collective-permute-done | bytes 786464 | tf_op jit(solution)/shard_map/ppermute | solution.py:957
  246.5 6.3 %collective-permute-start.19 = (bf16[8,48,512]{2,1,0:T(8,128)(2,1)S(1)}, bf16[8,48,512]{2,1,0:T(8,128)(2,1)S(1)}, u32[]{:S(2)}, u32[]{:S(2)}) collective-permute-start(bf16[8,48,512]{2,1,0:T(8,128)(2,1)S(1)} %get-tuple-element.258), channel_id=1, source_target_pairs={{0,16},{8,24},{16,0},{24,8},{1,17},{9,25},{17,1},{25,9},{2,18},{10... | collective-permute-start | bytes 1179656 | tf_op jit(solution)/shard_map/ppermute | solution.py:960
  255.0 2.6 collective-permute-start.21
  262.2 5.3 %collective-permute-done.20 = bf16[272,512]{1,0:T(8,128)(2,1)S(1)} collective-permute-done((bf16[272,512]{1,0:T(8,128)(2,1)S(1)}, bf16[272,512]{1,0:T(8,128)(2,1)S(1)}, u32[]{:S(2)}, u32[]{:S(2)}) %collective-permute-start.20) | collective-permute-done | bytes 278560 | tf_op jit(solution)/shard_map/ppermute | solution.py:966
  267.5 9.9 %collective-permute-done.21 = bf16[272,512]{1,0:T(8,128)(2,1)S(1)} collective-permute-done((bf16[272,512]{1,0:T(8,128)(2,1)S(1)}, bf16[272,512]{1,0:T(8,128)(2,1)S(1)}, u32[]{:S(2)}, u32[]{:S(2)}) %collective-permute-start.21) | collective-permute-done | bytes 278560 | tf_op jit(solution)/shard_map/ppermute | solution.py:966
  280.6 8.4 %all-to-all-start.4 = ((bf16[4,128,512]{2,1,0:T(8,128)(2,1)}), bf16[4,128,512]{2,1,0:T(8,128)(2,1)S(1)}, u32[]{:S(2)}, u32[]{:S(2)}) async-start(bf16[4,128,512]{2,1,0:T(8,128)(2,1)} %add_convert_fusion.9), calls=%async_computation.4 | async-start | bytes 1048576 | tf_op jit(solution)/shard_map/all_to_all | solution.py:981
  291.9 11.1 %collective-permute-done.24 = bf16[4,128,512]{2,1,0:T(8,128)(2,1)S(1)} collective-permute-done((bf16[4,128,512]{2,1,0:T(8,128)(2,1)S(1)}, bf16[4,128,512]{2,1,0:T(8,128)(2,1)S(1)}, u32[]{:S(2)}, u32[]{:S(2)}) %collective-permute-start.24) | collective-permute-done | bytes 524320 | tf_op jit(solution)/shard_map/ppermute | solution.py:963
  309.7 7.5 %collective-permute-done.28 = bf16[128,512]{1,0:T(8,128)(2,1)S(1)} collective-permute-done((bf16[128,512]{1,0:T(8,128)(2,1)S(1)}, bf16[128,512]{1,0:T(8,128)(2,1)S(1)}, u32[]{:S(2)}, u32[]{:S(2)}) %collective-permute-start.28) | collective-permute-done | bytes 131104 | tf_op jit(solution)/shard_map/ppermute | solution.py:966
  (198 shorter events, 63.1 us)
Async XLA Ops:
  2.3 5.8 %collective-permute-start.1 = (bf16[3,2,128,512]{3,2,1,0:T(8,128)(2,1)S(1)}, bf16[3,2,128,512]{3,2,1,0:T(8,128)(2,1)S(1)}, u32[]{:S(2)}, u32[]{:S(2)}) collective-permute-start(bf16[3,2,128,512]{3,2,1,0:T(8,128)(2,1)S(1)} %get-tuple-element.263), channel_id=1, source_target_pairs={{0,8},{8,0},{16,24},{24,16},{1,9},{9,1},{17,25},{25,17},{2,10},{10... | collective-permute-start | bytes 2359304 | tf_op jit(solution)/shard_map/ppermute | solution.py:957
  3.1 5.1 %collective-permute-start.2 = (bf16[48,512]{1,0:T(8,128)(2,1)S(1)}, bf16[48,512]{1,0:T(8,128)(2,1)S(1)}, u32[]{:S(2)}, u32[]{:S(2)}) collective-permute-start(bf16[48,512]{1,0:T(8,128)(2,1)S(1)} %bitcast.235), channel_id=1, source_target_pairs={{0,16},{8,24},{16,0},{24,8},{1,17},{9,25},{17,1},{25,9},{2,18},{10... | collective-permute-start | bytes 147464 | tf_op jit(solution)/shard_map/ppermute | solution.py:960
  10.4 27.4 %all-to-all-start = ((bf16[4,224,512]{2,1,0:T(8,128)(2,1)}), bf16[4,224,512]{2,1,0:T(8,128)(2,1)S(1)}, u32[]{:S(2)}, u32[]{:S(2)}) async-start(bf16[4,224,512]{2,1,0:T(8,128)(2,1)} %pad_maximum_fusion.4), calls=%async_computation | async-start | bytes 1835008 | tf_op jit(solution)/shard_map/all_to_all | solution.py:981
  16.3 6.1 %collective-permute-start.3 = (bf16[224,512]{1,0:T(8,128)(2,1)S(1)}, bf16[224,512]{1,0:T(8,128)(2,1)S(1)}, u32[]{:S(2)}, u32[]{:S(2)}) collective-permute-start(bf16[224,512]{1,0:T(8,128)(2,1)S(1)} %get-tuple-element.287), channel_id=1, source_target_pairs={{0,16},{8,24},{16,0},{24,8},{1,17},{9,25},{17,1},{25,9},{2,18},{10... | collective-permute-start | bytes 688136 | tf_op jit(solution)/shard_map/ppermute | solution.py:960
  37.8 21.3 %collective-permute-start.4 = (bf16[4,224,512]{2,1,0:T(8,128)(2,1)S(1)}, bf16[4,224,512]{2,1,0:T(8,128)(2,1)S(1)}, u32[]{:S(2)}, u32[]{:S(2)}) collective-permute-start(bf16[4,224,512]{2,1,0:T(8,128)(2,1)S(1)} %all-to-all-done), channel_id=1, source_target_pairs={{0,1},{1,0},{2,3},{3,2},{4,5},{5,4},{6,7},{7,6},{8,9},{9,8},{10,11... | collective-permute-start | bytes 2752520 | tf_op jit(solution)/shard_map/ppermute | solution.py:963
  39.3 34.1 %all-to-all-start.1 = ((bf16[4,320,512]{2,1,0:T(8,128)(2,1)}), bf16[4,320,512]{2,1,0:T(8,128)(2,1)S(1)}, u32[]{:S(2)}, u32[]{:S(2)}) async-start(bf16[4,320,512]{2,1,0:T(8,128)(2,1)} %pad_maximum_fusion.2), calls=%async_computation.1 | async-start | bytes 2621440 | tf_op jit(solution)/shard_map/all_to_all | solution.py:981
  59.6 13.8 %collective-permute-start.5 = (bf16[8,224,512]{2,1,0:T(8,128)(2,1)S(1)}, bf16[8,224,512]{2,1,0:T(8,128)(2,1)}, u32[]{:S(2)}, u32[]{:S(2)}) collective-permute-start(bf16[8,224,512]{2,1,0:T(8,128)(2,1)S(1)} %bitcast.200), channel_id=1, source_target_pairs={{0,8},{8,0},{16,24},{24,16},{1,9},{9,1},{17,25},{25,17},{2,10},{10... | collective-permute-start | bytes 5505032 | tf_op jit(solution)/shard_map/ppermute | solution.py:957
  73.4 40.0 %all-to-all-start.2 = ((bf16[4,384,512]{2,1,0:T(8,128)(2,1)}), bf16[4,384,512]{2,1,0:T(8,128)(2,1)S(1)}, u32[]{:S(2)}, u32[]{:S(2)}) async-start(bf16[4,384,512]{2,1,0:T(8,128)(2,1)} %pad_maximum_fusion.1), calls=%async_computation.2 | async-start | bytes 3145728 | tf_op jit(solution)/shard_map/all_to_all | solution.py:981
  78.5 31.0 %collective-permute-start.6 = (bf16[4,320,512]{2,1,0:T(8,128)(2,1)S(1)}, bf16[4,320,512]{2,1,0:T(8,128)(2,1)}, u32[]{:S(2)}, u32[]{:S(2)}) collective-permute-start(bf16[4,320,512]{2,1,0:T(8,128)(2,1)S(1)} %all-to-all-done.1), channel_id=1, source_target_pairs={{0,1},{1,0},{2,3},{3,2},{4,5},{5,4},{6,7},{7,6},{8,9},{9,8},{10,11... | collective-permute-start | bytes 3932168 | tf_op jit(solution)/shard_map/ppermute | solution.py:963
  116.9 5.3 %collective-permute-start.7 = (bf16[8,320,512]{2,1,0:T(8,128)(2,1)}, bf16[8,320,512]{2,1,0:T(8,128)(2,1)}, u32[]{:S(2)}, u32[]{:S(2)}) collective-permute-start(bf16[8,320,512]{2,1,0:T(8,128)(2,1)} %bitcast.40.refs_3_.refs_8_.refs_9_), channel_id=1, source_target_pairs={{0,8},{8,0},{16,24},{24,16},{1,9},{9,1},{17,25},{25,17},{2,10},{10... | collective-permute-start | bytes 7864328 | tf_op jit(solution)/shard_map/ppermute | solution.py:957
  117.0 25.6 %collective-permute-start.8 = (bf16[4,256,512]{2,1,0:T(8,128)(2,1)S(1)}, bf16[4,256,512]{2,1,0:T(8,128)(2,1)S(1)}, u32[]{:S(2)}, u32[]{:S(2)}) collective-permute-start(bf16[4,256,512]{2,1,0:T(8,128)(2,1)S(1)} %slice.140), channel_id=1, source_target_pairs={{0,1},{1,0},{2,3},{3,2},{4,5},{5,4},{6,7},{7,6},{8,9},{9,8},{10,11... | collective-permute-start | bytes 3145736 | tf_op jit(solution)/shard_map/ppermute | solution.py:963
  143.2 4.2 %collective-permute-start.9 = (bf16[8,256,512]{2,1,0:T(8,128)(2,1)S(1)}, bf16[8,256,512]{2,1,0:T(8,128)(2,1)S(1)}, u32[]{:S(2)}, u32[]{:S(2)}) collective-permute-start(bf16[8,256,512]{2,1,0:T(8,128)(2,1)S(1)} %bitcast.198), channel_id=1, source_target_pairs={{0,8},{8,0},{16,24},{24,16},{1,9},{9,1},{17,25},{25,17},{2,10},{10... | collective-permute-start | bytes 6291464 | tf_op jit(solution)/shard_map/ppermute | solution.py:957
  160.7 4.6 %collective-permute-start.10 = (bf16[2,8,144,512]{3,2,1,0:T(8,128)(2,1)S(1)}, bf16[2,8,144,512]{3,2,1,0:T(8,128)(2,1)S(1)}, u32[]{:S(2)}, u32[]{:S(2)}) collective-permute-start(bf16[2,8,144,512]{3,2,1,0:T(8,128)(2,1)S(1)} %shard_map.215), channel_id=1, source_target_pairs={{0,8},{8,0},{16,24},{24,16},{1,9},{9,1},{17,25},{25,17},{2,10},{10... | collective-permute-start | bytes 7077896 | tf_op jit(solution)/shard_map/ppermute | solution.py:957
  167.2 28.2 %collective-permute-start.11 = (bf16[8,144,512]{2,1,0:T(8,128)(2,1)}, bf16[8,144,512]{2,1,0:T(8,128)(2,1)S(1)}, u32[]{:S(2)}, u32[]{:S(2)}) collective-permute-start(bf16[8,144,512]{2,1,0:T(8,128)(2,1)} %get-tuple-element.251), channel_id=1, source_target_pairs={{0,16},{8,24},{16,0},{24,8},{1,17},{9,25},{17,1},{25,9},{2,18},{10... | collective-permute-start | bytes 3538952 | tf_op jit(solution)/shard_map/ppermute | solution.py:960
  168.6 26.4 %all-to-all-start.3 = ((bf16[4,128,512]{2,1,0:T(8,128)(2,1)}), bf16[4,128,512]{2,1,0:T(8,128)(2,1)S(1)}, u32[]{:S(2)}, u32[]{:S(2)}) async-start(bf16[4,128,512]{2,1,0:T(8,128)(2,1)} %bitcast.50), calls=%async_computation.3 | async-start | bytes 1048576 | tf_op jit(solution)/shard_map/all_to_all | solution.py:981
  195.4 8.0 %collective-permute-start.13 = (bf16[2,8,80,512]{3,2,1,0:T(8,128)(2,1)}, bf16[2,8,80,512]{3,2,1,0:T(8,128)(2,1)}, u32[]{:S(2)}, u32[]{:S(2)}) collective-permute-start(bf16[2,8,80,512]{3,2,1,0:T(8,128)(2,1)} %get-tuple-element.154), channel_id=1, source_target_pairs={{0,8},{8,0},{16,24},{24,16},{1,9},{9,1},{17,25},{25,17},{2,10},{10... | collective-permute-start | bytes 3932168 | tf_op jit(solution)/shard_map/ppermute | solution.py:957
  198.8 4.5 %collective-permute-start.12 = (bf16[1024,512]{1,0:T(8,128)(2,1)}, bf16[1024,512]{1,0:T(8,128)(2,1)}, u32[]{:S(2)}, u32[]{:S(2)}) collective-permute-start(bf16[1024,512]{1,0:T(8,128)(2,1)} %get-tuple-element.153), channel_id=1, source_target_pairs={{0,8},{8,0},{16,24},{24,16},{1,9},{9,1},{17,25},{25,17},{2,10},{10... | collective-permute-start | bytes 3145736 | tf_op jit(solution)/shard_map/ppermute | solution.py:957
  206.0 29.8 %collective-permute-start.14 = (bf16[4,272,512]{2,1,0:T(8,128)(2,1)}, bf16[4,272,512]{2,1,0:T(8,128)(2,1)S(1)}, u32[]{:S(2)}, u32[]{:S(2)}) collective-permute-start(bf16[4,272,512]{2,1,0:T(8,128)(2,1)} %get-tuple-element.255), channel_id=1, source_target_pairs={{0,1},{1,0},{2,3},{3,2},{4,5},{5,4},{6,7},{7,6},{8,9},{9,8},{10,11... | collective-permute-start | bytes 3342344 | tf_op jit(solution)/shard_map/ppermute | solution.py:963
  209.1 26.7 %collective-permute-start.15 = (bf16[8,80,512]{2,1,0:T(8,128)(2,1)}, bf16[8,80,512]{2,1,0:T(8,128)(2,1)}, u32[]{:S(2)}, u32[]{:S(2)}) collective-permute-start(bf16[8,80,512]{2,1,0:T(8,128)(2,1)} %get-tuple-element.253), channel_id=1, source_target_pairs={{0,16},{8,24},{16,0},{24,8},{1,17},{9,25},{17,1},{25,9},{2,18},{10... | collective-permute-start | bytes 1966088 | tf_op jit(solution)/shard_map/ppermute | solution.py:960
  235.9 5.8 %collective-permute-start.16 = (bf16[1024,512]{1,0:T(8,128)(2,1)}, bf16[1024,512]{1,0:T(8,128)(2,1)}, u32[]{:S(2)}, u32[]{:S(2)}) collective-permute-start(bf16[1024,512]{1,0:T(8,128)(2,1)} %get-tuple-element.173), channel_id=1, source_target_pairs={{0,8},{8,0},{16,24},{24,16},{1,9},{9,1},{17,25},{25,17},{2,10},{10... | collective-permute-start | bytes 3145736 | tf_op jit(solution)/shard_map/ppermute | solution.py:957
  243.3 16.4 %collective-permute-start.18 = (bf16[4,128,512]{2,1,0:T(8,128)(2,1)S(1)}, bf16[4,128,512]{2,1,0:T(8,128)(2,1)S(1)}, u32[]{:S(2)}, u32[]{:S(2)}) collective-permute-start(bf16[4,128,512]{2,1,0:T(8,128)(2,1)S(1)} %get-tuple-element.270), channel_id=1, source_target_pairs={{0,1},{1,0},{2,3},{3,2},{4,5},{5,4},{6,7},{7,6},{8,9},{9,8},{10,11... | collective-permute-start | bytes 1572872 | tf_op jit(solution)/shard_map/ppermute | solution.py:963
  246.5 15.4 %collective-permute-start.19 = (bf16[8,48,512]{2,1,0:T(8,128)(2,1)S(1)}, bf16[8,48,512]{2,1,0:T(8,128)(2,1)S(1)}, u32[]{:S(2)}, u32[]{:S(2)}) collective-permute-start(bf16[8,48,512]{2,1,0:T(8,128)(2,1)S(1)} %get-tuple-element.258), channel_id=1, source_target_pairs={{0,16},{8,24},{16,0},{24,8},{1,17},{9,25},{17,1},{25,9},{2,18},{10... | collective-permute-start | bytes 1179656 | tf_op jit(solution)/shard_map/ppermute | solution.py:960
  252.8 14.7 %collective-permute-start.20 = (bf16[272,512]{1,0:T(8,128)(2,1)S(1)}, bf16[272,512]{1,0:T(8,128)(2,1)S(1)}, u32[]{:S(2)}, u32[]{:S(2)}) collective-permute-start(bf16[272,512]{1,0:T(8,128)(2,1)S(1)} %get-tuple-element.266), channel_id=1, source_target_pairs={{0,2},{1,3},{2,0},{3,1},{4,6},{5,7},{6,4},{7,5},{8,10},{9,11},{10,... | collective-permute-start | bytes 835592 | tf_op jit(solution)/shard_map/ppermute | solution.py:966
  255.0 22.4 %collective-permute-start.21 = (bf16[272,512]{1,0:T(8,128)(2,1)S(1)}, bf16[272,512]{1,0:T(8,128)(2,1)S(1)}, u32[]{:S(2)}, u32[]{:S(2)}) collective-permute-start(bf16[272,512]{1,0:T(8,128)(2,1)S(1)} %get-tuple-element.265), channel_id=1, source_target_pairs={{0,4},{1,5},{2,6},{3,7},{4,0},{5,1},{6,2},{7,3},{8,12},{9,13},{10,... | collective-permute-start | bytes 835592 | tf_op jit(solution)/shard_map/ppermute | solution.py:966
  257.6 19.8 %collective-permute-start.22 = (bf16[272,512]{1,0:T(8,128)(2,1)S(1)}, bf16[272,512]{1,0:T(8,128)(2,1)S(1)}, u32[]{:S(2)}, u32[]{:S(2)}) collective-permute-start(bf16[272,512]{1,0:T(8,128)(2,1)S(1)} %get-tuple-element.264), channel_id=1, source_target_pairs={{0,6},{1,7},{2,4},{3,5},{4,2},{5,3},{6,0},{7,1},{8,14},{9,15},{10,... | collective-permute-start | bytes 835592 | tf_op jit(solution)/shard_map/ppermute | solution.py:966
  279.6 10.8 %collective-permute-start.26 = (bf16[2,128,512]{2,1,0:T(8,128)(2,1)S(1)}, bf16[2,128,512]{2,1,0:T(8,128)(2,1)S(1)}, u32[]{:S(2)}, u32[]{:S(2)}) collective-permute-start(bf16[2,128,512]{2,1,0:T(8,128)(2,1)S(1)} %get-tuple-element.277), channel_id=1, source_target_pairs={{0,8},{8,0},{16,24},{24,16},{1,9},{9,1},{17,25},{25,17},{2,10},{10... | collective-permute-start | bytes 786440 | tf_op jit(solution)/shard_map/ppermute | solution.py:957
  280.6 28.2 %all-to-all-start.4 = ((bf16[4,128,512]{2,1,0:T(8,128)(2,1)}), bf16[4,128,512]{2,1,0:T(8,128)(2,1)S(1)}, u32[]{:S(2)}, u32[]{:S(2)}) async-start(bf16[4,128,512]{2,1,0:T(8,128)(2,1)} %add_convert_fusion.9), calls=%async_computation.4 | async-start | bytes 1048576 | tf_op jit(solution)/shard_map/all_to_all | solution.py:981
  289.0 14.0 %collective-permute-start.24 = (bf16[4,128,512]{2,1,0:T(8,128)(2,1)S(1)}, bf16[4,128,512]{2,1,0:T(8,128)(2,1)S(1)}, u32[]{:S(2)}, u32[]{:S(2)}) collective-permute-start(bf16[4,128,512]{2,1,0:T(8,128)(2,1)S(1)} %get-tuple-element.268), channel_id=1, source_target_pairs={{0,1},{1,0},{2,3},{3,2},{4,5},{5,4},{6,7},{7,6},{8,9},{9,8},{10,11... | collective-permute-start | bytes 1572872 | tf_op jit(solution)/shard_map/ppermute | solution.py:963
  303.2 6.4 %collective-permute-start.27 = (bf16[128,512]{1,0:T(8,128)(2,1)S(1)}, bf16[128,512]{1,0:T(8,128)(2,1)S(1)}, u32[]{:S(2)}, u32[]{:S(2)}) collective-permute-start(bf16[128,512]{1,0:T(8,128)(2,1)S(1)} %get-tuple-element.272), channel_id=1, source_target_pairs={{0,2},{1,3},{2,0},{3,1},{4,6},{5,7},{6,4},{7,5},{8,10},{9,11},{10,... | collective-permute-start | bytes 393224 | tf_op jit(solution)/shard_map/ppermute | solution.py:966
  305.0 12.1 %collective-permute-start.28 = (bf16[128,512]{1,0:T(8,128)(2,1)S(1)}, bf16[128,512]{1,0:T(8,128)(2,1)S(1)}, u32[]{:S(2)}, u32[]{:S(2)}) collective-permute-start(bf16[128,512]{1,0:T(8,128)(2,1)S(1)} %get-tuple-element.274), channel_id=1, source_target_pairs={{0,4},{1,5},{2,6},{3,7},{4,0},{5,1},{6,2},{7,3},{8,12},{9,13},{10,... | collective-permute-start | bytes 393224 | tf_op jit(solution)/shard_map/ppermute | solution.py:966
  307.4 9.8 %collective-permute-start.29 = (bf16[128,512]{1,0:T(8,128)(2,1)S(1)}, bf16[128,512]{1,0:T(8,128)(2,1)S(1)}, u32[]{:S(2)}, u32[]{:S(2)}) collective-permute-start(bf16[128,512]{1,0:T(8,128)(2,1)S(1)} %get-tuple-element.273), channel_id=1, source_target_pairs={{0,6},{1,7},{2,4},{3,5},{4,2},{5,3},{6,0},{7,1},{8,14},{9,15},{10,... | collective-permute-start | bytes 393224 | tf_op jit(solution)/shard_map/ppermute | solution.py:966
  308.9 11.0 %collective-permute-start.25 = (bf16[2,128,512]{2,1,0:T(8,128)(2,1)S(1)}, bf16[2,128,512]{2,1,0:T(8,128)(2,1)S(1)}, u32[]{:S(2)}, u32[]{:S(2)}) collective-permute-start(bf16[2,128,512]{2,1,0:T(8,128)(2,1)S(1)} %get-tuple-element.279), channel_id=1, source_target_pairs={{0,8},{8,0},{16,24},{24,16},{1,9},{9,1},{17,25},{25,17},{2,10},{10... | collective-permute-start | bytes 786440 | tf_op jit(solution)/shard_map/ppermute | solution.py:957
  (32 other events, 137.6 us)

commit v3 on v2

--- a/solution.py
+++ b/solution.py
@@ -1193,26 +1193,26 @@
         x_kept, x_send, i_kept, i_send, fs_first, c_first, out_parts, *fs_moves[1:], *c_moves[1:]
     )
     x_came, i_came = over_core(x_send), over_core(i_send)
-    fs_parts = z_parts(total([fs_first, *moves[:extra]]))
-    x_came, i_came, fs_first = together(x_came, i_came, fs_parts[0])
+    fs_sum = total([fs_first, *moves[:extra]])
+    fs_got = exchange_z(fs_sum)
+    x_came, i_came, fs_sum = together(x_came, i_came, fs_sum)
     x_moves_y = y_parts(total([x_kept, x_came]).reshape(seq_count, half, width))
     x_first, i_came, i_kept = together(x_moves_y[0], i_came, i_kept)
     i_moves = x_moves(i_kept, i_came)
     c_sum = by_owner(total([c_first, *moves[extra:]]), 0)
     i_first, c_sum, *x_moves_y = together(i_moves[0], c_sum, x_first, *x_moves_y[1:])
-    x_parts = exchange_z(total(x_moves_y))
+    x_parts = z_parts(total(x_moves_y))
     i_sum = by_owner(total([i_first, *i_moves[1:]]), 0)
     w_moves = y_parts(jnp.concatenate([c_sum, i_sum], axis=1))
-    w_first, out_parts, fs_first, *fs_parts = together(w_moves[0], out_parts, fs_first, *fs_parts[1:])
-    fs_parts = [fs_first] + fs_parts
-    grad_source = home(unxor([v[-half:] for v in fs_parts], z_place))
+    w_first, out_parts, fs_got = together(w_moves[0], out_parts, fs_got)
+    grad_source = home(fs_got[:, -half:])
     out_tokens = home(out_parts)
-    f_own = sum((v[:-half].astype(F32) for v in fs_parts[1:]), fs_parts[0][:-half].astype(F32))
+    f_own = jnp.sum(fs_got[:, :-half].astype(F32), axis=0)
     w_parts = z_parts(total([w_first, *w_moves[1:]]))
-    w_first, x_parts = together(w_parts[0], x_parts)
+    w_first = w_parts[0]
     w_own = sum(w_parts[1:], w_first.astype(F32))
     c_own, i_own = w_own[: 5 * rows], w_own[5 * rows :]
-    grad_tokens = home(x_parts)
+    grad_tokens = home(unxor(x_parts, z_place))
     f_in = hidden // width * rows
     c_own = c_own.reshape(5, rows, width)
     return (

time: 326 us -> 314 us (0.963); the launches traced: 321 us -> 314 us
  waiting for transfers between devices: 124 us -> 104 us
  Pallas kernels: 96 us -> 107 us
  other arithmetic: 28.6 us -> 32.7 us
  starting transfers between devices: 60.2 us -> 56.5 us
    pallas_call x4, Pallas kernels: 80.9 us -> 92.2 us  [call(): pl.pallas_call(wrapped, out_shape=out_shape, in_specs=[SMEM if kind is SM...]
    ppermute x6, waiting for transfers between devices: 23.4 us -> 12.5 us  [over_z(): lax.ppermute(v, 'seq', [(i, i ^ k * y_count) for i in range(seq_count)])]
    ppermute x6, waiting for transfers between devices: 44.6 us -> 36.3 us  [over_y(): lax.ppermute(v, 'seq', [(i, i ^ k) for i in range(seq_count)])]
    ppermute x13, starting transfers between devices: 6.8 us -> 2.65 us  [over_core(): return lax.ppermute(v, 'dp', [(i, i ^ 1) for i in range(dp_count)])]
    all_to_all x5, waiting for transfers between devices: 29 us -> 33.1 us  [exchange_z(): return lax.all_to_all(v, 'seq', 0, 0, tiled=True, axis_index_groups=groups)]
    ppermute x13, waiting for transfers between devices: 18.2 us -> 14.6 us  [over_core(): return lax.ppermute(v, 'dp', [(i, i ^ 1) for i in range(dp_count)])]
    convert_element_type x8, other arithmetic: 6.12 us -> 9.43 us  [total(): return out.astype(BF)]
  transfers between devices with their start and end apart: 35 -> 35, of which waited for: 22 -> 20; matrix products, arithmetic and copies ran while one was open for 6% -> 9% of each run, Pallas kernels for 26% -> 30%
where the time goes in v3:
time: 314 us
  Pallas kernels  107 us (34%)
  waiting for transfers between devices  104 us (33%)
  starting transfers between devices  56.5 us (18%)
  other arithmetic  32.7 us (10%)
  local copies, waits for them, and re-layouts  12.6 us (4%)
    pallas_call x4, Pallas kernels, call(): pl.pallas_call(wrapped, out_shape=out_shape, in_specs=[SMEM if kind is SM...  92.2 us
    ppermute x6, waiting for transfers between devices, over_y(): lax.ppermute(v, 'seq', [(i, i ^ k) for i in range(seq_count)])  36.3 us
    all_to_all x5, waiting for transfers between devices, exchange_z(): return lax.all_to_all(v, 'seq', 0, 0, tiled=True, axis_index_groups=groups)  33.1 us
    all_to_all x5, starting transfers between devices, exchange_z(): return lax.all_to_all(v, 'seq', 0, 0, tiled=True, axis_index_groups=groups)  23.9 us
    pallas_call x3, Pallas kernels, call(): pl.pallas_call(kernel, out_shape=out_shape, in_specs=in_specs, out_specs=...  15 us
    ppermute x13, waiting for transfers between devices, over_core(): return lax.ppermute(v, 'dp', [(i, i ^ 1) for i in range(dp_count)])  14.6 us
    ppermute x6, waiting for transfers between devices, over_z(): lax.ppermute(v, 'seq', [(i, i ^ k * y_count) for i in range(seq_count)])  12.5 us
    ppermute x5, starting transfers between devices, over_x(): lax.ppermute(v, 'dp', [(i, i ^ 2 * k) for i in range(dp_count)])  12 us
  transfers between devices with their start and end apart: 35, of which 20 were waited for; matrix products, arithmetic and copies ran while one was open for 9% of the time, Pallas kernels for 30%

profile of v3, /device:TPU:0, one launch (start us, length us, event | category | flops | bytes accessed | tf_op | source)
XLA Modules:
  0.0 314.5 jit_solution(4825163329590138457)
XLA Ops:
  3.1 3.0 collective-permute-start.2
  10.4 5.5 %all-to-all-start = ((bf16[4,224,512]{2,1,0:T(8,128)(2,1)}), bf16[4,224,512]{2,1,0:T(8,128)(2,1)S(1)}, u32[]{:S(2)}, u32[]{:S(2)}) async-start(bf16[4,224,512]{2,1,0:T(8,128)(2,1)} %pad_maximum_fusion.4), calls=%async_computation | async-start | bytes 1835008 | tf_op jit(solution)/shard_map/all_to_all | solution.py:981
  17.9 4.5 %collective-permute-done.3 = bf16[224,512]{1,0:T(8,128)(2,1)S(1)} collective-permute-done((bf16[224,512]{1,0:T(8,128)(2,1)S(1)}, bf16[224,512]{1,0:T(8,128)(2,1)S(1)}, u32[]{:S(2)}, u32[]{:S(2)}) %collective-permute-start.3) | collective-permute-done | bytes 229408 | tf_op jit(solution)/shard_map/ppermute | solution.py:960
  23.7 14.1 %all-to-all-done = bf16[4,224,512]{2,1,0:T(8,128)(2,1)S(1)} async-done(((bf16[4,224,512]{2,1,0:T(8,128)(2,1)}), bf16[4,224,512]{2,1,0:T(8,128)(2,1)S(1)}, u32[]{:S(2)}, u32[]{:S(2)}) %all-to-all-start) | async-done | bytes 917536 | tf_op jit(solution)/shard_map/all_to_all | solution.py:981
  39.3 3.5 %all-to-all-start.1 = ((bf16[4,320,512]{2,1,0:T(8,128)(2,1)}), bf16[4,320,512]{2,1,0:T(8,128)(2,1)S(1)}, u32[]{:S(2)}, u32[]{:S(2)}) async-start(bf16[4,320,512]{2,1,0:T(8,128)(2,1)} %pad_maximum_fusion.2), calls=%async_computation.1 | async-start | bytes 2621440 | tf_op jit(solution)/shard_map/all_to_all | solution.py:981
  42.9 16.2 %collective-permute-done.4 = bf16[4,224,512]{2,1,0:T(8,128)(2,1)S(1)} collective-permute-done((bf16[4,224,512]{2,1,0:T(8,128)(2,1)S(1)}, bf16[4,224,512]{2,1,0:T(8,128)(2,1)S(1)}, u32[]{:S(2)}, u32[]{:S(2)}) %collective-permute-start.4) | collective-permute-done | bytes 917536 | tf_op jit(solution)/shard_map/ppermute | solution.py:963
  62.3 11.1 %all-to-all-done.1 = bf16[4,320,512]{2,1,0:T(8,128)(2,1)S(1)} async-done(((bf16[4,320,512]{2,1,0:T(8,128)(2,1)}), bf16[4,320,512]{2,1,0:T(8,128)(2,1)S(1)}, u32[]{:S(2)}, u32[]{:S(2)}) %all-to-all-start.1) | async-done | bytes 1310752 | tf_op jit(solution)/shard_map/all_to_all | solution.py:981
  73.4 3.7 %all-to-all-start.2 = ((bf16[4,384,512]{2,1,0:T(8,128)(2,1)}), bf16[4,384,512]{2,1,0:T(8,128)(2,1)S(1)}, u32[]{:S(2)}, u32[]{:S(2)}) async-start(bf16[4,384,512]{2,1,0:T(8,128)(2,1)} %pad_maximum_fusion.1), calls=%async_computation.2 | async-start | bytes 3145728 | tf_op jit(solution)/shard_map/all_to_all | solution.py:981
  81.0 21.0 %shard_map.212 = (bf16[512,512]{1,0:T(8,128)(2,1)}, bf16[2048,1024]{1,0:T(8,128)(2,1)}, bf16[3,32,16,512]{3,2,1,0:T(8,128)(2,1)}, bf16[512,512]{1,0:T(8,128)(2,1)}, f32[8,1,512]{2,1,0:T(1,128)}) custom-call(s32[2,8]{1,0:T(2,128)} %pad.11.refs_0_, s32[4]{0:T(128)} %pad_add_fusion.2.refs_1_.place_ref, bf16[8,224,512]{2,1,0:T(8,128)(2,1)} %bitcast.194, ...), custom_call_target="tpu_custom_call" | custom-call | flops 1840000000 | bytes 1024 | tf_op jit(solution)/shard_map/pallas_call | solution.py:110
  102.0 7.5 %collective-permute-done.6 = bf16[4,320,512]{2,1,0:T(8,128)(2,1)} collective-permute-done((bf16[4,320,512]{2,1,0:T(8,128)(2,1)S(1)}, bf16[4,320,512]{2,1,0:T(8,128)(2,1)}, u32[]{:S(2)}, u32[]{:S(2)}) %collective-permute-start.6) | collective-permute-done | bytes 1310752 | tf_op jit(solution)/shard_map/ppermute | solution.py:963
  109.6 3.8 %all-to-all-done.2.cot_ref = bf16[4,384,512]{2,1,0:T(8,128)(2,1)S(1)} async-done(((bf16[4,384,512]{2,1,0:T(8,128)(2,1)}), bf16[4,384,512]{2,1,0:T(8,128)(2,1)S(1)}, u32[]{:S(2)}, u32[]{:S(2)}) %all-to-all-start.2) | async-done | bytes 1572896 | tf_op jit(solution)/shard_map/all_to_all | solution.py:981
  113.4 3.5 %maximum_select_fusion = bf16[2,4,320,512]{3,2,0,1:T(8,128)(2,1)} fusion(bf16[1,4,320,512]{3,2,0,1:T(8,128)(2,1)} %bitcast.38, bf16[1,4,320,512]{3,2,0,1:T(8,128)(2,1)S(1)} %bitcast.198, pred[]{:T(512)S(6)} %eq.8), kind=kLoop, calls=%fused_computation | loop fusion | flops 3932160 | bytes 5242881 | tf_op jit(solution)/shard_map/jit(_where)/select_n | solution.py:918
  118.8 3.4 %collective-permute-done.7.refs_4_.refs_9_.refs_10_ = bf16[8,320,512]{2,1,0:T(8,128)(2,1)} collective-permute-done((bf16[8,320,512]{2,1,0:T(8,128)(2,1)}, bf16[8,320,512]{2,1,0:T(8,128)(2,1)}, u32[]{:S(2)}, u32[]{:S(2)}) %collective-permute-start.7) | collective-permute-done | bytes 2621472 | tf_op jit(solution)/shard_map/ppermute | solution.py:957
  122.2 15.4 %shard_map.213 = (bf16[512,512]{1,0:T(8,128)(2,1)}, bf16[2048,1024]{1,0:T(8,128)(2,1)}, bf16[6,32,16,512]{3,2,1,0:T(8,128)(2,1)}, f32[512,512]{1,0:T(8,128)}, f3...) custom-call(s32[2,8]{1,0:T(2,128)} %pad.13.refs_0_, ...), custom_call_target="tpu_custom_call" | custom-call | flops 1955000064 | bytes 1024 | tf_op jit(solution)/shard_map/pallas_call | solution.py:110
  137.5 5.1 %collective-permute-done.8 = bf16[4,256,512]{2,1,0:T(8,128)(2,1)S(1)} collective-permute-done((bf16[4,256,512]{2,1,0:T(8,128)(2,1)S(1)}, bf16[4,256,512]{2,1,0:T(8,128)(2,1)S(1)}, u32[]{:S(2)}, u32[]{:S(2)}) %collective-permute-start.8) | collective-permute-done | bytes 1048608 | tf_op jit(solution)/shard_map/ppermute | solution.py:963
  143.3 4.1 %collective-permute-done.9.refs_1_ = bf16[8,256,512]{2,1,0:T(8,128)(2,1)S(1)} collective-permute-done((bf16[8,256,512]{2,1,0:T(8,128)(2,1)S(1)}, bf16[8,256,512]{2,1,0:T(8,128)(2,1)S(1)}, u32[]{:S(2)}, u32[]{:S(2)}) %collective-permute-start.9) | collective-permute-done | bytes 2097184 | tf_op jit(solution)/shard_map/ppermute | solution.py:957
  147.5 11.2 %shard_map.214 = (bf16[512,512]{1,0:T(8,128)(2,1)}, f32[512,512]{1,0:T(8,128)S(1)}, bf16[512,512]{1,0:T(8,128)(2,1)S(1)}, f32[8,512]{1,0:T(8,128)S(1)}, bf16[512...) custom-call(s32[4]{0:T(128)S(1)} %copy-done.8, ...), custom_call_target="tpu_custom_call" | custom-call | flops 1380000000 | bytes 1024 | tf_op jit(solution)/shard_map/pallas_call | solution.py:54
  162.8 2.5 collective-permute-done.10
  168.6 3.5 %all-to-all-start.3 = ((bf16[4,128,512]{2,1,0:T(8,128)(2,1)}), bf16[4,128,512]{2,1,0:T(8,128)(2,1)S(1)}, u32[]{:S(2)}, u32[]{:S(2)}) async-start(bf16[4,128,512]{2,1,0:T(8,128)(2,1)} %bitcast.50), calls=%async_computation.3 | async-start | bytes 1048576 | tf_op jit(solution)/shard_map/all_to_all | solution.py:981
  172.1 23.0 %shard_map.217 = (bf16[1024,512]{1,0:T(8,128)(2,1)}, bf16[1024,512]{1,0:T(8,128)(2,1)}, bf16[2,8,80,512]{3,2,1,0:T(8,128)(2,1)}, bf16[2,8,80,512]{3,2,1,0:T(8,12...) custom-call(s32[2,8]{1,0:T(2,128)} %pad.13.refs_0_, s32[4]{0:T(128)} %pad_add_fusion.2.refs_1_.place_ref, ...), custom_call_target="tpu_custom_call" | custom-call | flops 3449999872 | bytes 1024 | tf_op jit(solution)/shard_map/pallas_call | solution.py:110
  196.2 4.0 %collective-permute-done.12 = bf16[1024,512]{1,0:T(8,128)(2,1)} collective-permute-done((bf16[1024,512]{1,0:T(8,128)(2,1)}, bf16[1024,512]{1,0:T(8,128)(2,1)}, u32[]{:S(2)}, u32[]{:S(2)}) %collective-permute-start.12) | collective-permute-done | bytes 1048608 | tf_op jit(solution)/shard_map/ppermute | solution.py:957
  202.9 4.5 %collective-permute-start.14 = (bf16[4,272,512]{2,1,0:T(8,128)(2,1)}, bf16[4,272,512]{2,1,0:T(8,128)(2,1)S(1)}, u32[]{:S(2)}, u32[]{:S(2)}) collective-permute-start(bf16[4,272,512]{2,1,0:T(8,128)(2,1)} %get-tuple-element.243), channel_id=1, source_target_pairs={{0,1},{1,0},{2,3},{3,2},{4,5},{5,4},{6,7},{7,6},{8,9},{9,8},{10,11... | collective-permute-start | bytes 3342344 | tf_op jit(solution)/shard_map/ppermute | solution.py:963
  207.5 2.5 fusion.9
  210.0 3.0 collective-permute-start.15
  213.0 32.8 %shard_map.218 = (bf16[1024,512]{1,0:T(8,128)(2,1)}, bf16[1024,512]{1,0:T(8,128)(2,1)}, bf16[2,8,48,512]{3,2,1,0:T(8,128)(2,1)}, bf16[2,8,48,512]{3,2,1,0:T(8,128)(2,1)}) custom-call(s32[2,8]{1,0:T(2,128)} %pad.11.refs_0_, s32[4]{0:T(128)} %pad_add_fusion.2.refs_1_.place_ref, bf16[512,512]{1,0:T(8,128)(2,1)} %get-tuple-element.103.refs_2_, ...), custom_call_target="tpu_custom_call" | custom-call | flops 3104999936 | bytes 1024 | tf_op jit(solution)/shard_map/pallas_call | solution.py:110
  247.7 7.6 %all-to-all-start.4 = ((bf16[4,272,512]{2,1,0:T(8,128)(2,1)}), bf16[4,272,512]{2,1,0:T(8,128)(2,1)S(1)}, u32[]{:S(2)}, u32[]{:S(2)}) async-start(bf16[4,272,512]{2,1,0:T(8,128)(2,1)} %add_convert_fusion.3), calls=%async_computation.4 | async-start | bytes 2228224 | tf_op jit(solution)/shard_map/all_to_all | solution.py:981
  260.3 3.0 collective-permute-start.19
  264.6 7.5 %collective-permute-done.18 = bf16[4,128,512]{2,1,0:T(8,128)(2,1)} collective-permute-done((bf16[4,128,512]{2,1,0:T(8,128)(2,1)}, bf16[4,128,512]{2,1,0:T(8,128)(2,1)}, u32[]{:S(2)}, u32[]{:S(2)}) %collective-permute-start.18) | collective-permute-done | bytes 524320 | tf_op jit(solution)/shard_map/ppermute | solution.py:963
  282.4 4.0 %all-to-all-done.4 = bf16[4,272,512]{2,1,0:T(8,128)(2,1)S(1)} async-done(((bf16[4,272,512]{2,1,0:T(8,128)(2,1)}), bf16[4,272,512]{2,1,0:T(8,128)(2,1)S(1)}, u32[]{:S(2)}, u32[]{:S(2)}) %all-to-all-start.4) | async-done | bytes 1114144 | tf_op jit(solution)/shard_map/all_to_all | solution.py:981
  289.2 3.1 %collective-permute-done.22 = bf16[128,512]{1,0:T(8,128)(2,1)S(1)} collective-permute-done((bf16[128,512]{1,0:T(8,128)(2,1)S(1)}, bf16[128,512]{1,0:T(8,128)(2,1)S(1)}, u32[]{:S(2)}, u32[]{:S(2)}) %collective-permute-start.22) | collective-permute-done | bytes 131104 | tf_op jit(solution)/shard_map/ppermute | solution.py:966
  296.3 2.6 collective-permute-start.27
  304.6 7.2 %collective-permute-done.28 = bf16[128,512]{1,0:T(8,128)(2,1)S(1)} collective-permute-done((bf16[128,512]{1,0:T(8,128)(2,1)S(1)}, bf16[128,512]{1,0:T(8,128)(2,1)S(1)}, u32[]{:S(2)}, u32[]{:S(2)}) %collective-permute-start.28) | collective-permute-done | bytes 131104 | tf_op jit(solution)/shard_map/ppermute | solution.py:966
  (198 shorter events, 65.2 us)
Async XLA Ops:
  2.3 5.8 %collective-permute-start.1 = (bf16[3,2,128,512]{3,2,1,0:T(8,128)(2,1)S(1)}, bf16[3,2,128,512]{3,2,1,0:T(8,128)(2,1)S(1)}, u32[]{:S(2)}, u32[]{:S(2)}) collective-permute-start(bf16[3,2,128,512]{3,2,1,0:T(8,128)(2,1)S(1)} %get-tuple-element.251), channel_id=1, source_target_pairs={{0,8},{8,0},{16,24},{24,16},{1,9},{9,1},{17,25},{25,17},{2,10},{10... | collective-permute-start | bytes 2359304 | tf_op jit(solution)/shard_map/ppermute | solution.py:957
  3.1 5.1 %collective-permute-start.2 = (bf16[48,512]{1,0:T(8,128)(2,1)S(1)}, bf16[48,512]{1,0:T(8,128)(2,1)S(1)}, u32[]{:S(2)}, u32[]{:S(2)}) collective-permute-start(bf16[48,512]{1,0:T(8,128)(2,1)S(1)} %bitcast.228), channel_id=1, source_target_pairs={{0,16},{8,24},{16,0},{24,8},{1,17},{9,25},{17,1},{25,9},{2,18},{10... | collective-permute-start | bytes 147464 | tf_op jit(solution)/shard_map/ppermute | solution.py:960
  10.4 27.4 %all-to-all-start = ((bf16[4,224,512]{2,1,0:T(8,128)(2,1)}), bf16[4,224,512]{2,1,0:T(8,128)(2,1)S(1)}, u32[]{:S(2)}, u32[]{:S(2)}) async-start(bf16[4,224,512]{2,1,0:T(8,128)(2,1)} %pad_maximum_fusion.4), calls=%async_computation | async-start | bytes 1835008 | tf_op jit(solution)/shard_map/all_to_all | solution.py:981
  16.3 6.1 %collective-permute-start.3 = (bf16[224,512]{1,0:T(8,128)(2,1)S(1)}, bf16[224,512]{1,0:T(8,128)(2,1)S(1)}, u32[]{:S(2)}, u32[]{:S(2)}) collective-permute-start(bf16[224,512]{1,0:T(8,128)(2,1)S(1)} %get-tuple-element.274), channel_id=1, source_target_pairs={{0,16},{8,24},{16,0},{24,8},{1,17},{9,25},{17,1},{25,9},{2,18},{10... | collective-permute-start | bytes 688136 | tf_op jit(solution)/shard_map/ppermute | solution.py:960
  37.8 21.3 %collective-permute-start.4 = (bf16[4,224,512]{2,1,0:T(8,128)(2,1)S(1)}, bf16[4,224,512]{2,1,0:T(8,128)(2,1)S(1)}, u32[]{:S(2)}, u32[]{:S(2)}) collective-permute-start(bf16[4,224,512]{2,1,0:T(8,128)(2,1)S(1)} %all-to-all-done), channel_id=1, source_target_pairs={{0,1},{1,0},{2,3},{3,2},{4,5},{5,4},{6,7},{7,6},{8,9},{9,8},{10,11... | collective-permute-start | bytes 2752520 | tf_op jit(solution)/shard_map/ppermute | solution.py:963
  39.3 34.1 %all-to-all-start.1 = ((bf16[4,320,512]{2,1,0:T(8,128)(2,1)}), bf16[4,320,512]{2,1,0:T(8,128)(2,1)S(1)}, u32[]{:S(2)}, u32[]{:S(2)}) async-start(bf16[4,320,512]{2,1,0:T(8,128)(2,1)} %pad_maximum_fusion.2), calls=%async_computation.1 | async-start | bytes 2621440 | tf_op jit(solution)/shard_map/all_to_all | solution.py:981
  59.6 13.8 %collective-permute-start.5 = (bf16[8,224,512]{2,1,0:T(8,128)(2,1)S(1)}, bf16[8,224,512]{2,1,0:T(8,128)(2,1)}, u32[]{:S(2)}, u32[]{:S(2)}) collective-permute-start(bf16[8,224,512]{2,1,0:T(8,128)(2,1)S(1)} %bitcast.193), channel_id=1, source_target_pairs={{0,8},{8,0},{16,24},{24,16},{1,9},{9,1},{17,25},{25,17},{2,10},{10... | collective-permute-start | bytes 5505032 | tf_op jit(solution)/shard_map/ppermute | solution.py:957
  73.4 40.0 %all-to-all-start.2 = ((bf16[4,384,512]{2,1,0:T(8,128)(2,1)}), bf16[4,384,512]{2,1,0:T(8,128)(2,1)S(1)}, u32[]{:S(2)}, u32[]{:S(2)}) async-start(bf16[4,384,512]{2,1,0:T(8,128)(2,1)} %pad_maximum_fusion.1), calls=%async_computation.2 | async-start | bytes 3145728 | tf_op jit(solution)/shard_map/all_to_all | solution.py:981
  78.5 31.0 %collective-permute-start.6 = (bf16[4,320,512]{2,1,0:T(8,128)(2,1)S(1)}, bf16[4,320,512]{2,1,0:T(8,128)(2,1)}, u32[]{:S(2)}, u32[]{:S(2)}) collective-permute-start(bf16[4,320,512]{2,1,0:T(8,128)(2,1)S(1)} %all-to-all-done.1), channel_id=1, source_target_pairs={{0,1},{1,0},{2,3},{3,2},{4,5},{5,4},{6,7},{7,6},{8,9},{9,8},{10,11... | collective-permute-start | bytes 3932168 | tf_op jit(solution)/shard_map/ppermute | solution.py:963
  116.9 5.3 %collective-permute-start.7 = (bf16[8,320,512]{2,1,0:T(8,128)(2,1)}, bf16[8,320,512]{2,1,0:T(8,128)(2,1)}, u32[]{:S(2)}, u32[]{:S(2)}) collective-permute-start(bf16[8,320,512]{2,1,0:T(8,128)(2,1)} %bitcast.40.refs_3_.refs_8_.refs_9_), channel_id=1, source_target_pairs={{0,8},{8,0},{16,24},{24,16},{1,9},{9,1},{17,25},{25,17},{2,10},{10... | collective-permute-start | bytes 7864328 | tf_op jit(solution)/shard_map/ppermute | solution.py:957
  117.0 25.6 %collective-permute-start.8 = (bf16[4,256,512]{2,1,0:T(8,128)(2,1)S(1)}, bf16[4,256,512]{2,1,0:T(8,128)(2,1)S(1)}, u32[]{:S(2)}, u32[]{:S(2)}) collective-permute-start(bf16[4,256,512]{2,1,0:T(8,128)(2,1)S(1)} %slice.122), channel_id=1, source_target_pairs={{0,1},{1,0},{2,3},{3,2},{4,5},{5,4},{6,7},{7,6},{8,9},{9,8},{10,11... | collective-permute-start | bytes 3145736 | tf_op jit(solution)/shard_map/ppermute | solution.py:963
  160.7 4.6 %collective-permute-start.10 = (bf16[2,8,144,512]{3,2,1,0:T(8,128)(2,1)S(1)}, bf16[2,8,144,512]{3,2,1,0:T(8,128)(2,1)S(1)}, u32[]{:S(2)}, u32[]{:S(2)}) collective-permute-start(bf16[2,8,144,512]{3,2,1,0:T(8,128)(2,1)S(1)} %shard_map.215), channel_id=1, source_target_pairs={{0,8},{8,0},{16,24},{24,16},{1,9},{9,1},{17,25},{25,17},{2,10},{10... | collective-permute-start | bytes 7077896 | tf_op jit(solution)/shard_map/ppermute | solution.py:957
  167.1 28.2 %collective-permute-start.11 = (bf16[8,144,512]{2,1,0:T(8,128)(2,1)}, bf16[8,144,512]{2,1,0:T(8,128)(2,1)S(1)}, u32[]{:S(2)}, u32[]{:S(2)}) collective-permute-start(bf16[8,144,512]{2,1,0:T(8,128)(2,1)} %get-tuple-element.239), channel_id=1, source_target_pairs={{0,16},{8,24},{16,0},{24,8},{1,17},{9,25},{17,1},{25,9},{2,18},{10... | collective-permute-start | bytes 3538952 | tf_op jit(solution)/shard_map/ppermute | solution.py:960
  168.6 26.4 %all-to-all-start.3 = ((bf16[4,128,512]{2,1,0:T(8,128)(2,1)}), bf16[4,128,512]{2,1,0:T(8,128)(2,1)S(1)}, u32[]{:S(2)}, u32[]{:S(2)}) async-start(bf16[4,128,512]{2,1,0:T(8,128)(2,1)} %bitcast.50), calls=%async_computation.3 | async-start | bytes 1048576 | tf_op jit(solution)/shard_map/all_to_all | solution.py:981
  195.3 4.9 %collective-permute-start.13 = (bf16[2,8,80,512]{3,2,1,0:T(8,128)(2,1)}, bf16[2,8,80,512]{3,2,1,0:T(8,128)(2,1)}, u32[]{:S(2)}, u32[]{:S(2)}) collective-permute-start(bf16[2,8,80,512]{3,2,1,0:T(8,128)(2,1)} %get-tuple-element.148), channel_id=1, source_target_pairs={{0,8},{8,0},{16,24},{24,16},{1,9},{9,1},{17,25},{25,17},{2,10},{10... | collective-permute-start | bytes 3932168 | tf_op jit(solution)/shard_map/ppermute | solution.py:957
  195.4 4.9 %collective-permute-start.12 = (bf16[1024,512]{1,0:T(8,128)(2,1)}, bf16[1024,512]{1,0:T(8,128)(2,1)}, u32[]{:S(2)}, u32[]{:S(2)}) collective-permute-start(bf16[1024,512]{1,0:T(8,128)(2,1)} %get-tuple-element.147), channel_id=1, source_target_pairs={{0,8},{8,0},{16,24},{24,16},{1,9},{9,1},{17,25},{25,17},{2,10},{10... | collective-permute-start | bytes 3145736 | tf_op jit(solution)/shard_map/ppermute | solution.py:957
  202.9 42.9 %collective-permute-start.14 = (bf16[4,272,512]{2,1,0:T(8,128)(2,1)}, bf16[4,272,512]{2,1,0:T(8,128)(2,1)S(1)}, u32[]{:S(2)}, u32[]{:S(2)}) collective-permute-start(bf16[4,272,512]{2,1,0:T(8,128)(2,1)} %get-tuple-element.243), channel_id=1, source_target_pairs={{0,1},{1,0},{2,3},{3,2},{4,5},{5,4},{6,7},{7,6},{8,9},{9,8},{10,11... | collective-permute-start | bytes 3342344 | tf_op jit(solution)/shard_map/ppermute | solution.py:963
  210.0 35.8 %collective-permute-start.15 = (bf16[8,80,512]{2,1,0:T(8,128)(2,1)}, bf16[8,80,512]{2,1,0:T(8,128)(2,1)}, u32[]{:S(2)}, u32[]{:S(2)}) collective-permute-start(bf16[8,80,512]{2,1,0:T(8,128)(2,1)} %get-tuple-element.241), channel_id=1, source_target_pairs={{0,16},{8,24},{16,0},{24,8},{1,17},{9,25},{17,1},{25,9},{2,18},{10... | collective-permute-start | bytes 1966088 | tf_op jit(solution)/shard_map/ppermute | solution.py:960
  245.8 9.6 %collective-permute-start.16 = (bf16[1024,512]{1,0:T(8,128)(2,1)}, bf16[1024,512]{1,0:T(8,128)(2,1)}, u32[]{:S(2)}, u32[]{:S(2)}) collective-permute-start(bf16[1024,512]{1,0:T(8,128)(2,1)} %get-tuple-element.167), channel_id=1, source_target_pairs={{0,8},{8,0},{16,24},{24,16},{1,9},{9,1},{17,25},{25,17},{2,10},{10... | collective-permute-start | bytes 3145736 | tf_op jit(solution)/shard_map/ppermute | solution.py:957
  245.9 9.5 %collective-permute-start.17 = (bf16[2,8,48,512]{3,2,1,0:T(8,128)(2,1)}, bf16[2,8,48,512]{3,2,1,0:T(8,128)(2,1)}, u32[]{:S(2)}, u32[]{:S(2)}) collective-permute-start(bf16[2,8,48,512]{3,2,1,0:T(8,128)(2,1)} %get-tuple-element.168), channel_id=1, source_target_pairs={{0,8},{8,0},{16,24},{24,16},{1,9},{9,1},{17,25},{25,17},{2,10},{10... | collective-permute-start | bytes 2359304 | tf_op jit(solution)/shard_map/ppermute | solution.py:957
  247.7 38.7 %all-to-all-start.4 = ((bf16[4,272,512]{2,1,0:T(8,128)(2,1)}), bf16[4,272,512]{2,1,0:T(8,128)(2,1)S(1)}, u32[]{:S(2)}, u32[]{:S(2)}) async-start(bf16[4,272,512]{2,1,0:T(8,128)(2,1)} %add_convert_fusion.3), calls=%async_computation.4 | async-start | bytes 2228224 | tf_op jit(solution)/shard_map/all_to_all | solution.py:981
  257.8 14.3 %collective-permute-start.18 = (bf16[4,128,512]{2,1,0:T(8,128)(2,1)}, bf16[4,128,512]{2,1,0:T(8,128)(2,1)}, u32[]{:S(2)}, u32[]{:S(2)}) collective-permute-start(bf16[4,128,512]{2,1,0:T(8,128)(2,1)} %get-tuple-element.254), channel_id=1, source_target_pairs={{0,1},{1,0},{2,3},{3,2},{4,5},{5,4},{6,7},{7,6},{8,9},{9,8},{10,11... | collective-permute-start | bytes 1572872 | tf_op jit(solution)/shard_map/ppermute | solution.py:963
  260.3 12.4 %collective-permute-start.19 = (bf16[8,48,512]{2,1,0:T(8,128)(2,1)}, bf16[8,48,512]{2,1,0:T(8,128)(2,1)}, u32[]{:S(2)}, u32[]{:S(2)}) collective-permute-start(bf16[8,48,512]{2,1,0:T(8,128)(2,1)} %get-tuple-element.246), channel_id=1, source_target_pairs={{0,16},{8,24},{16,0},{24,8},{1,17},{9,25},{17,1},{25,9},{2,18},{10... | collective-permute-start | bytes 1179656 | tf_op jit(solution)/shard_map/ppermute | solution.py:960
  274.8 20.2 %collective-permute-start.26 = (bf16[4,128,512]{2,1,0:T(8,128)(2,1)}, bf16[4,128,512]{2,1,0:T(8,128)(2,1)}, u32[]{:S(2)}, u32[]{:S(2)}) collective-permute-start(bf16[4,128,512]{2,1,0:T(8,128)(2,1)} %get-tuple-element.252), channel_id=1, source_target_pairs={{0,1},{1,0},{2,3},{3,2},{4,5},{5,4},{6,7},{7,6},{8,9},{9,8},{10,11... | collective-permute-start | bytes 1572872 | tf_op jit(solution)/shard_map/ppermute | solution.py:963
  278.0 10.6 %collective-permute-start.21 = (bf16[128,512]{1,0:T(8,128)(2,1)}, bf16[128,512]{1,0:T(8,128)(2,1)S(1)}, u32[]{:S(2)}, u32[]{:S(2)}) collective-permute-start(bf16[128,512]{1,0:T(8,128)(2,1)} %get-tuple-element.265), channel_id=1, source_target_pairs={{0,2},{1,3},{2,0},{3,1},{4,6},{5,7},{6,4},{7,5},{8,10},{9,11},{10,... | collective-permute-start | bytes 393224 | tf_op jit(solution)/shard_map/ppermute | solution.py:966
  279.8 12.6 %collective-permute-start.22 = (bf16[128,512]{1,0:T(8,128)(2,1)S(1)}, bf16[128,512]{1,0:T(8,128)(2,1)S(1)}, u32[]{:S(2)}, u32[]{:S(2)}) collective-permute-start(bf16[128,512]{1,0:T(8,128)(2,1)S(1)} %get-tuple-element.264), channel_id=1, source_target_pairs={{0,4},{1,5},{2,6},{3,7},{4,0},{5,1},{6,2},{7,3},{8,12},{9,13},{10,... | collective-permute-start | bytes 393224 | tf_op jit(solution)/shard_map/ppermute | solution.py:966
  282.1 10.3 %collective-permute-start.23 = (bf16[128,512]{1,0:T(8,128)(2,1)S(1)}, bf16[128,512]{1,0:T(8,128)(2,1)S(1)}, u32[]{:S(2)}, u32[]{:S(2)}) collective-permute-start(bf16[128,512]{1,0:T(8,128)(2,1)S(1)} %get-tuple-element.263), channel_id=1, source_target_pairs={{0,6},{1,7},{2,4},{3,5},{4,2},{5,3},{6,0},{7,1},{8,14},{9,15},{10,... | collective-permute-start | bytes 393224 | tf_op jit(solution)/shard_map/ppermute | solution.py:966
  287.9 4.6 %collective-permute-start.25 = (bf16[2,128,512]{2,1,0:T(8,128)(2,1)S(1)}, bf16[2,128,512]{2,1,0:T(8,128)(2,1)S(1)}, u32[]{:S(2)}, u32[]{:S(2)}) collective-permute-start(bf16[2,128,512]{2,1,0:T(8,128)(2,1)S(1)} %get-tuple-element.260), channel_id=1, source_target_pairs={{0,8},{8,0},{16,24},{24,16},{1,9},{9,1},{17,25},{25,17},{2,10},{10... | collective-permute-start | bytes 786440 | tf_op jit(solution)/shard_map/ppermute | solution.py:957
  288.6 5.1 %collective-permute-start.20 = (bf16[2,128,512]{2,1,0:T(8,128)(2,1)S(1)}, bf16[2,128,512]{2,1,0:T(8,128)(2,1)S(1)}, u32[]{:S(2)}, u32[]{:S(2)}) collective-permute-start(bf16[2,128,512]{2,1,0:T(8,128)(2,1)S(1)} %get-tuple-element.268), channel_id=1, source_target_pairs={{0,8},{8,0},{16,24},{24,16},{1,9},{9,1},{17,25},{25,17},{2,10},{10... | collective-permute-start | bytes 786440 | tf_op jit(solution)/shard_map/ppermute | solution.py:957
  296.3 8.3 %collective-permute-start.27 = (bf16[128,512]{1,0:T(8,128)(2,1)S(1)}, bf16[128,512]{1,0:T(8,128)(2,1)S(1)}, u32[]{:S(2)}, u32[]{:S(2)}) collective-permute-start(bf16[128,512]{1,0:T(8,128)(2,1)S(1)} %get-tuple-element.256), channel_id=1, source_target_pairs={{0,2},{1,3},{2,0},{3,1},{4,6},{5,7},{6,4},{7,5},{8,10},{9,11},{10,... | collective-permute-start | bytes 393224 | tf_op jit(solution)/shard_map/ppermute | solution.py:966
  298.9 12.9 %collective-permute-start.28 = (bf16[128,512]{1,0:T(8,128)(2,1)S(1)}, bf16[128,512]{1,0:T(8,128)(2,1)S(1)}, u32[]{:S(2)}, u32[]{:S(2)}) collective-permute-start(bf16[128,512]{1,0:T(8,128)(2,1)S(1)} %get-tuple-element.258), channel_id=1, source_target_pairs={{0,4},{1,5},{2,6},{3,7},{4,0},{5,1},{6,2},{7,3},{8,12},{9,13},{10,... | collective-permute-start | bytes 393224 | tf_op jit(solution)/shard_map/ppermute | solution.py:966
  299.0 12.8 %collective-permute-start.29 = (bf16[128,512]{1,0:T(8,128)(2,1)S(1)}, bf16[128,512]{1,0:T(8,128)(2,1)S(1)}, u32[]{:S(2)}, u32[]{:S(2)}) collective-permute-start(bf16[128,512]{1,0:T(8,128)(2,1)S(1)} %get-tuple-element.257), channel_id=1, source_target_pairs={{0,6},{1,7},{2,4},{3,5},{4,2},{5,3},{6,0},{7,1},{8,14},{9,15},{10,... | collective-permute-start | bytes 393224 | tf_op jit(solution)/shard_map/ppermute | solution.py:966
  (32 other events, 146.7 us)

commit v4 on v3

--- a/solution.py
+++ b/solution.py
@@ -1200,13 +1200,13 @@
     x_first, i_came, i_kept = together(x_moves_y[0], i_came, i_kept)
     i_moves = x_moves(i_kept, i_came)
     c_sum = by_owner(total([c_first, *moves[extra:]]), 0)
-    i_first, c_sum, *x_moves_y = together(i_moves[0], c_sum, x_first, *x_moves_y[1:])
+    out_tokens = home(out_parts)
+    out_tokens, i_first, c_sum, *x_moves_y = together(out_tokens, i_moves[0], c_sum, x_first, *x_moves_y[1:])
     x_parts = z_parts(total(x_moves_y))
     i_sum = by_owner(total([i_first, *i_moves[1:]]), 0)
     w_moves = y_parts(jnp.concatenate([c_sum, i_sum], axis=1))
-    w_first, out_parts, fs_got = together(w_moves[0], out_parts, fs_got)
+    w_first, fs_got = together(w_moves[0], fs_got)
     grad_source = home(fs_got[:, -half:])
-    out_tokens = home(out_parts)
     f_own = jnp.sum(fs_got[:, :-half].astype(F32), axis=0)
     w_parts = z_parts(total([w_first, *w_moves[1:]]))
     w_first = w_parts[0]

time: 314 us -> 311 us (level)
  starting transfers between devices: 56.5 us -> 49.6 us
    all_to_all x5, waiting for transfers between devices: 33.1 us -> 40.7 us  [exchange_z(): return lax.all_to_all(v, 'seq', 0, 0, tiled=True, axis_index_groups=groups)]
    ppermute x6, starting transfers between devices: 8.51 us -> 3.6 us  [over_y(): lax.ppermute(v, 'seq', [(i, i ^ k) for i in range(seq_count)])]
    ppermute x13, starting transfers between devices: 2.65 us -> 6.37 us  [over_core(): return lax.ppermute(v, 'dp', [(i, i ^ 1) for i in range(dp_count)])]
    ppermute x6, waiting for transfers between devices: 12.5 us -> 9.24 us  [over_z(): lax.ppermute(v, 'seq', [(i, i ^ k * y_count) for i in range(seq_count)])]
  transfers between devices with their start and end apart: 35 -> 35, of which waited for: 20 -> 18; matrix products, arithmetic and copies ran while one was open for 9% -> 8% of each run, Pallas kernels for 30% -> 31%
where the time goes in v4:
time: 311 us; the launch traced here: 308 us
  Pallas kernels  109 us (35%)
  waiting for transfers between devices  105 us (34%)
  starting transfers between devices  49.6 us (16%)
  other arithmetic  29.9 us (10%)
  local copies, waits for them, and re-layouts  13.8 us (4%)
    pallas_call x4, Pallas kernels, call(): pl.pallas_call(wrapped, out_shape=out_shape, in_specs=[SMEM if kind is SM...  93.8 us
    all_to_all x5, waiting for transfers between devices, exchange_z(): return lax.all_to_all(v, 'seq', 0, 0, tiled=True, axis_index_groups=groups)  40.7 us
    ppermute x6, waiting for transfers between devices, over_y(): lax.ppermute(v, 'seq', [(i, i ^ k) for i in range(seq_count)])  33.4 us
    all_to_all x5, starting transfers between devices, exchange_z(): return lax.all_to_all(v, 'seq', 0, 0, tiled=True, axis_index_groups=groups)  21.2 us
    pallas_call x3, Pallas kernels, call(): pl.pallas_call(kernel, out_shape=out_shape, in_specs=in_specs, out_specs=...  15 us
    ppermute x13, waiting for transfers between devices, over_core(): return lax.ppermute(v, 'dp', [(i, i ^ 1) for i in range(dp_count)])  14.6 us
    ppermute x5, starting transfers between devices, over_x(): lax.ppermute(v, 'dp', [(i, i ^ 2 * k) for i in range(dp_count)])  9.5 us
    ppermute x6, waiting for transfers between devices, over_z(): lax.ppermute(v, 'seq', [(i, i ^ k * y_count) for i in range(seq_count)])  9.24 us
  transfers between devices with their start and end apart: 35, of which 18 were waited for; matrix products, arithmetic and copies ran while one was open for 8% of the time, Pallas kernels for 31%

profile of v4, /device:TPU:0, one launch (start us, length us, event | category | flops | bytes accessed | tf_op | source)
XLA Modules:
  0.0 308.5 jit_solution(7314598237167920055)
XLA Ops:
  3.1 3.0 collective-permute-start.2
  6.2 2.0 collective-permute-done.2
  10.4 5.5 %all-to-all-start = ((bf16[4,224,512]{2,1,0:T(8,128)(2,1)}), bf16[4,224,512]{2,1,0:T(8,128)(2,1)S(1)}, u32[]{:S(2)}, u32[]{:S(2)}) async-start(bf16[4,224,512]{2,1,0:T(8,128)(2,1)} %pad_maximum_fusion.4), calls=%async_computation | async-start | bytes 1835008 | tf_op jit(solution)/shard_map/all_to_all | solution.py:981
  17.9 4.5 %collective-permute-done.3 = bf16[224,512]{1,0:T(8,128)(2,1)S(1)} collective-permute-done((bf16[224,512]{1,0:T(8,128)(2,1)S(1)}, bf16[224,512]{1,0:T(8,128)(2,1)S(1)}, u32[]{:S(2)}, u32[]{:S(2)}) %collective-permute-start.3) | collective-permute-done | bytes 229408 | tf_op jit(solution)/shard_map/ppermute | solution.py:960
  23.6 14.1 %all-to-all-done = bf16[4,224,512]{2,1,0:T(8,128)(2,1)S(1)} async-done(((bf16[4,224,512]{2,1,0:T(8,128)(2,1)}), bf16[4,224,512]{2,1,0:T(8,128)(2,1)S(1)}, u32[]{:S(2)}, u32[]{:S(2)}) %all-to-all-start) | async-done | bytes 917536 | tf_op jit(solution)/shard_map/all_to_all | solution.py:981
  39.3 3.5 %all-to-all-start.1 = ((bf16[4,320,512]{2,1,0:T(8,128)(2,1)}), bf16[4,320,512]{2,1,0:T(8,128)(2,1)S(1)}, u32[]{:S(2)}, u32[]{:S(2)}) async-start(bf16[4,320,512]{2,1,0:T(8,128)(2,1)} %pad_maximum_fusion.2), calls=%async_computation.1 | async-start | bytes 2621440 | tf_op jit(solution)/shard_map/all_to_all | solution.py:981
  42.9 16.2 %collective-permute-done.4 = bf16[4,224,512]{2,1,0:T(8,128)(2,1)S(1)} collective-permute-done((bf16[4,224,512]{2,1,0:T(8,128)(2,1)S(1)}, bf16[4,224,512]{2,1,0:T(8,128)(2,1)S(1)}, u32[]{:S(2)}, u32[]{:S(2)}) %collective-permute-start.4) | collective-permute-done | bytes 917536 | tf_op jit(solution)/shard_map/ppermute | solution.py:963
  62.3 11.1 %all-to-all-done.1 = bf16[4,320,512]{2,1,0:T(8,128)(2,1)S(1)} async-done(((bf16[4,320,512]{2,1,0:T(8,128)(2,1)}), bf16[4,320,512]{2,1,0:T(8,128)(2,1)S(1)}, u32[]{:S(2)}, u32[]{:S(2)}) %all-to-all-start.1) | async-done | bytes 1310752 | tf_op jit(solution)/shard_map/all_to_all | solution.py:981
  73.4 3.7 %all-to-all-start.2 = ((bf16[4,384,512]{2,1,0:T(8,128)(2,1)}), bf16[4,384,512]{2,1,0:T(8,128)(2,1)S(1)}, u32[]{:S(2)}, u32[]{:S(2)}) async-start(bf16[4,384,512]{2,1,0:T(8,128)(2,1)} %pad_maximum_fusion.1), calls=%async_computation.2 | async-start | bytes 3145728 | tf_op jit(solution)/shard_map/all_to_all | solution.py:981
  81.0 18.5 %shard_map.212 = (bf16[512,512]{1,0:T(8,128)(2,1)}, bf16[2048,1024]{1,0:T(8,128)(2,1)}, bf16[3,32,16,512]{3,2,1,0:T(8,128)(2,1)}, bf16[512,512]{1,0:T(8,128)(2,1)}, f32[8,1,512]{2,1,0:T(1,128)}) custom-call(s32[2,8]{1,0:T(2,128)} %pad.11.refs_0_, s32[4]{0:T(128)} %pad_add_fusion.2.refs_1_.place_ref, bf16[8,224,512]{2,1,0:T(8,128)(2,1)} %bitcast.194, ...), custom_call_target="tpu_custom_call" | custom-call | flops 1840000000 | bytes 1024 | tf_op jit(solution)/shard_map/pallas_call | solution.py:110
  99.5 10.1 %collective-permute-done.6 = bf16[4,320,512]{2,1,0:T(8,128)(2,1)} collective-permute-done((bf16[4,320,512]{2,1,0:T(8,128)(2,1)S(1)}, bf16[4,320,512]{2,1,0:T(8,128)(2,1)}, u32[]{:S(2)}, u32[]{:S(2)}) %collective-permute-start.6) | collective-permute-done | bytes 1310752 | tf_op jit(solution)/shard_map/ppermute | solution.py:963
  109.6 3.8 %all-to-all-done.2.cot_ref = bf16[4,384,512]{2,1,0:T(8,128)(2,1)S(1)} async-done(((bf16[4,384,512]{2,1,0:T(8,128)(2,1)}), bf16[4,384,512]{2,1,0:T(8,128)(2,1)S(1)}, u32[]{:S(2)}, u32[]{:S(2)}) %all-to-all-start.2) | async-done | bytes 1572896 | tf_op jit(solution)/shard_map/all_to_all | solution.py:981
  113.4 3.5 %maximum_select_fusion = bf16[2,4,320,512]{3,2,0,1:T(8,128)(2,1)} fusion(bf16[1,4,320,512]{3,2,0,1:T(8,128)(2,1)} %bitcast.38, bf16[1,4,320,512]{3,2,0,1:T(8,128)(2,1)S(1)} %bitcast.198, pred[]{:T(512)S(6)} %eq.8), kind=kLoop, calls=%fused_computation | loop fusion | flops 3932160 | bytes 5242881 | tf_op jit(solution)/shard_map/jit(_where)/select_n | solution.py:918
  118.8 3.4 %collective-permute-done.7.refs_4_.refs_9_.refs_10_ = bf16[8,320,512]{2,1,0:T(8,128)(2,1)} collective-permute-done((bf16[8,320,512]{2,1,0:T(8,128)(2,1)}, bf16[8,320,512]{2,1,0:T(8,128)(2,1)}, u32[]{:S(2)}, u32[]{:S(2)}) %collective-permute-start.7) | collective-permute-done | bytes 2621472 | tf_op jit(solution)/shard_map/ppermute | solution.py:957
  122.2 18.6 %shard_map.213 = (bf16[512,512]{1,0:T(8,128)(2,1)}, bf16[2048,1024]{1,0:T(8,128)(2,1)}, bf16[6,32,16,512]{3,2,1,0:T(8,128)(2,1)}, f32[512,512]{1,0:T(8,128)}, f3...) custom-call(s32[2,8]{1,0:T(2,128)} %pad.13.refs_0_, ...), custom_call_target="tpu_custom_call" | custom-call | flops 1955000064 | bytes 1024 | tf_op jit(solution)/shard_map/pallas_call | solution.py:110
  143.3 4.1 %collective-permute-done.9.refs_1_ = bf16[8,256,512]{2,1,0:T(8,128)(2,1)S(1)} collective-permute-done((bf16[8,256,512]{2,1,0:T(8,128)(2,1)S(1)}, bf16[8,256,512]{2,1,0:T(8,128)(2,1)S(1)}, u32[]{:S(2)}, u32[]{:S(2)}) %collective-permute-start.9) | collective-permute-done | bytes 2097184 | tf_op jit(solution)/shard_map/ppermute | solution.py:957
  147.5 11.2 %shard_map.214 = (bf16[512,512]{1,0:T(8,128)(2,1)}, f32[512,512]{1,0:T(8,128)S(1)}, bf16[512,512]{1,0:T(8,128)(2,1)S(1)}, f32[8,512]{1,0:T(8,128)S(1)}, bf16[512...) custom-call(s32[4]{0:T(128)S(1)} %copy-done.8, ...), custom_call_target="tpu_custom_call" | custom-call | flops 1380000000 | bytes 1024 | tf_op jit(solution)/shard_map/pallas_call | solution.py:54
  162.8 2.5 collective-permute-done.10
  168.6 3.5 %all-to-all-start.3 = ((bf16[4,128,512]{2,1,0:T(8,128)(2,1)}), bf16[4,128,512]{2,1,0:T(8,128)(2,1)S(1)}, u32[]{:S(2)}, u32[]{:S(2)}) async-start(bf16[4,128,512]{2,1,0:T(8,128)(2,1)} %bitcast.50), calls=%async_computation.3 | async-start | bytes 1048576 | tf_op jit(solution)/shard_map/all_to_all | solution.py:981
  172.1 27.7 %shard_map.217 = (bf16[1024,512]{1,0:T(8,128)(2,1)}, bf16[1024,512]{1,0:T(8,128)(2,1)}, bf16[2,8,80,512]{3,2,1,0:T(8,128)(2,1)}, bf16[2,8,80,512]{3,2,1,0:T(8,12...) custom-call(s32[2,8]{1,0:T(2,128)} %pad.13.refs_0_, s32[4]{0:T(128)} %pad_add_fusion.2.refs_1_.place_ref, ...), custom_call_target="tpu_custom_call" | custom-call | flops 3449999872 | bytes 1024 | tf_op jit(solution)/shard_map/pallas_call | solution.py:110
  200.7 4.0 %collective-permute-done.12 = bf16[1024,512]{1,0:T(8,128)(2,1)} collective-permute-done((bf16[1024,512]{1,0:T(8,128)(2,1)}, bf16[1024,512]{1,0:T(8,128)(2,1)}, u32[]{:S(2)}, u32[]{:S(2)}) %collective-permute-start.12) | collective-permute-done | bytes 1048608 | tf_op jit(solution)/shard_map/ppermute | solution.py:957
  208.0 2.5 fusion.9
  211.1 29.0 %shard_map.218 = (bf16[1024,512]{1,0:T(8,128)(2,1)}, bf16[1024,512]{1,0:T(8,128)(2,1)}, bf16[2,8,48,512]{3,2,1,0:T(8,128)(2,1)}, bf16[2,8,48,512]{3,2,1,0:T(8,128)(2,1)}) custom-call(s32[2,8]{1,0:T(2,128)} %pad.11.refs_0_, s32[4]{0:T(128)} %pad_add_fusion.2.refs_1_.place_ref, bf16[512,512]{1,0:T(8,128)(2,1)} %get-tuple-element.103.refs_2_, ...), custom_call_target="tpu_custom_call" | custom-call | flops 3104999936 | bytes 1024 | tf_op jit(solution)/shard_map/pallas_call | solution.py:110
  240.2 3.7 %collective-permute-start.17 = (bf16[1024,512]{1,0:T(8,128)(2,1)}, bf16[1024,512]{1,0:T(8,128)(2,1)}, u32[]{:S(2)}, u32[]{:S(2)}) collective-permute-start(bf16[1024,512]{1,0:T(8,128)(2,1)} %get-tuple-element.168), channel_id=1, source_target_pairs={{0,8},{8,0},{16,24},{24,16},{1,9},{9,1},{17,25},{25,17},{2,10},{10... | collective-permute-start | bytes 3145736 | tf_op jit(solution)/shard_map/ppermute | solution.py:957
  246.6 4.9 %all-to-all-start.4 = ((bf16[4,272,512]{2,1,0:T(8,128)(2,1)}), bf16[4,272,512]{2,1,0:T(8,128)(2,1)S(1)}, u32[]{:S(2)}, u32[]{:S(2)}) async-start(bf16[4,272,512]{2,1,0:T(8,128)(2,1)} %add_convert_fusion.3), calls=%async_computation.4 | async-start | bytes 2228224 | tf_op jit(solution)/shard_map/all_to_all | solution.py:981
  255.5 2.9 collective-permute-start.24
  261.9 5.2 %collective-permute-done.19 = bf16[4,128,512]{2,1,0:T(8,128)(2,1)S(1)} collective-permute-done((bf16[4,128,512]{2,1,0:T(8,128)(2,1)S(1)}, bf16[4,128,512]{2,1,0:T(8,128)(2,1)S(1)}, u32[]{:S(2)}, u32[]{:S(2)}) %collective-permute-start.19) | collective-permute-done | bytes 524320 | tf_op jit(solution)/shard_map/ppermute | solution.py:963
  271.3 2.4 collective-permute-start.21
  274.0 11.6 %all-to-all-done.4 = bf16[4,272,512]{2,1,0:T(8,128)(2,1)S(1)} async-done(((bf16[4,272,512]{2,1,0:T(8,128)(2,1)}), bf16[4,272,512]{2,1,0:T(8,128)(2,1)S(1)}, u32[]{:S(2)}, u32[]{:S(2)}) %all-to-all-start.4) | async-done | bytes 1114144 | tf_op jit(solution)/shard_map/all_to_all | solution.py:981
  290.9 2.1 collective-permute-start.27
  293.1 2.3 collective-permute-start.29
  298.2 7.6 %collective-permute-done.28 = bf16[128,512]{1,0:T(8,128)(2,1)S(1)} collective-permute-done((bf16[128,512]{1,0:T(8,128)(2,1)S(1)}, bf16[128,512]{1,0:T(8,128)(2,1)S(1)}, u32[]{:S(2)}, u32[]{:S(2)}) %collective-permute-start.28) | collective-permute-done | bytes 131104 | tf_op jit(solution)/shard_map/ppermute | solution.py:966
  (200 shorter events, 57.8 us)
Async XLA Ops:
  2.3 5.8 %collective-permute-start.1 = (bf16[3,2,128,512]{3,2,1,0:T(8,128)(2,1)S(1)}, bf16[3,2,128,512]{3,2,1,0:T(8,128)(2,1)S(1)}, u32[]{:S(2)}, u32[]{:S(2)}) collective-permute-start(bf16[3,2,128,512]{3,2,1,0:T(8,128)(2,1)S(1)} %get-tuple-element.251), channel_id=1, source_target_pairs={{0,8},{8,0},{16,24},{24,16},{1,9},{9,1},{17,25},{25,17},{2,10},{10... | collective-permute-start | bytes 2359304 | tf_op jit(solution)/shard_map/ppermute | solution.py:957
  3.1 5.1 %collective-permute-start.2 = (bf16[48,512]{1,0:T(8,128)(2,1)S(1)}, bf16[48,512]{1,0:T(8,128)(2,1)S(1)}, u32[]{:S(2)}, u32[]{:S(2)}) collective-permute-start(bf16[48,512]{1,0:T(8,128)(2,1)S(1)} %bitcast.227), channel_id=1, source_target_pairs={{0,16},{8,24},{16,0},{24,8},{1,17},{9,25},{17,1},{25,9},{2,18},{10... | collective-permute-start | bytes 147464 | tf_op jit(solution)/shard_map/ppermute | solution.py:960
  10.4 27.4 %all-to-all-start = ((bf16[4,224,512]{2,1,0:T(8,128)(2,1)}), bf16[4,224,512]{2,1,0:T(8,128)(2,1)S(1)}, u32[]{:S(2)}, u32[]{:S(2)}) async-start(bf16[4,224,512]{2,1,0:T(8,128)(2,1)} %pad_maximum_fusion.4), calls=%async_computation | async-start | bytes 1835008 | tf_op jit(solution)/shard_map/all_to_all | solution.py:981
  16.3 6.1 %collective-permute-start.3 = (bf16[224,512]{1,0:T(8,128)(2,1)S(1)}, bf16[224,512]{1,0:T(8,128)(2,1)S(1)}, u32[]{:S(2)}, u32[]{:S(2)}) collective-permute-start(bf16[224,512]{1,0:T(8,128)(2,1)S(1)} %get-tuple-element.274), channel_id=1, source_target_pairs={{0,16},{8,24},{16,0},{24,8},{1,17},{9,25},{17,1},{25,9},{2,18},{10... | collective-permute-start | bytes 688136 | tf_op jit(solution)/shard_map/ppermute | solution.py:960
  37.8 21.3 %collective-permute-start.4 = (bf16[4,224,512]{2,1,0:T(8,128)(2,1)S(1)}, bf16[4,224,512]{2,1,0:T(8,128)(2,1)S(1)}, u32[]{:S(2)}, u32[]{:S(2)}) collective-permute-start(bf16[4,224,512]{2,1,0:T(8,128)(2,1)S(1)} %all-to-all-done), channel_id=1, source_target_pairs={{0,1},{1,0},{2,3},{3,2},{4,5},{5,4},{6,7},{7,6},{8,9},{9,8},{10,11... | collective-permute-start | bytes 2752520 | tf_op jit(solution)/shard_map/ppermute | solution.py:963
  39.3 34.1 %all-to-all-start.1 = ((bf16[4,320,512]{2,1,0:T(8,128)(2,1)}), bf16[4,320,512]{2,1,0:T(8,128)(2,1)S(1)}, u32[]{:S(2)}, u32[]{:S(2)}) async-start(bf16[4,320,512]{2,1,0:T(8,128)(2,1)} %pad_maximum_fusion.2), calls=%async_computation.1 | async-start | bytes 2621440 | tf_op jit(solution)/shard_map/all_to_all | solution.py:981
  59.6 13.8 %collective-permute-start.5 = (bf16[8,224,512]{2,1,0:T(8,128)(2,1)S(1)}, bf16[8,224,512]{2,1,0:T(8,128)(2,1)}, u32[]{:S(2)}, u32[]{:S(2)}) collective-permute-start(bf16[8,224,512]{2,1,0:T(8,128)(2,1)S(1)} %bitcast.193), channel_id=1, source_target_pairs={{0,8},{8,0},{16,24},{24,16},{1,9},{9,1},{17,25},{25,17},{2,10},{10... | collective-permute-start | bytes 5505032 | tf_op jit(solution)/shard_map/ppermute | solution.py:957
  73.4 40.0 %all-to-all-start.2 = ((bf16[4,384,512]{2,1,0:T(8,128)(2,1)}), bf16[4,384,512]{2,1,0:T(8,128)(2,1)S(1)}, u32[]{:S(2)}, u32[]{:S(2)}) async-start(bf16[4,384,512]{2,1,0:T(8,128)(2,1)} %pad_maximum_fusion.1), calls=%async_computation.2 | async-start | bytes 3145728 | tf_op jit(solution)/shard_map/all_to_all | solution.py:981
  78.5 31.0 %collective-permute-start.6 = (bf16[4,320,512]{2,1,0:T(8,128)(2,1)S(1)}, bf16[4,320,512]{2,1,0:T(8,128)(2,1)}, u32[]{:S(2)}, u32[]{:S(2)}) collective-permute-start(bf16[4,320,512]{2,1,0:T(8,128)(2,1)S(1)} %all-to-all-done.1), channel_id=1, source_target_pairs={{0,1},{1,0},{2,3},{3,2},{4,5},{5,4},{6,7},{7,6},{8,9},{9,8},{10,11... | collective-permute-start | bytes 3932168 | tf_op jit(solution)/shard_map/ppermute | solution.py:963
  116.9 5.3 %collective-permute-start.7 = (bf16[8,320,512]{2,1,0:T(8,128)(2,1)}, bf16[8,320,512]{2,1,0:T(8,128)(2,1)}, u32[]{:S(2)}, u32[]{:S(2)}) collective-permute-start(bf16[8,320,512]{2,1,0:T(8,128)(2,1)} %bitcast.40.refs_3_.refs_8_.refs_9_), channel_id=1, source_target_pairs={{0,8},{8,0},{16,24},{24,16},{1,9},{9,1},{17,25},{25,17},{2,10},{10... | collective-permute-start | bytes 7864328 | tf_op jit(solution)/shard_map/ppermute | solution.py:957
  117.0 25.6 %collective-permute-start.8 = (bf16[4,256,512]{2,1,0:T(8,128)(2,1)S(1)}, bf16[4,256,512]{2,1,0:T(8,128)(2,1)S(1)}, u32[]{:S(2)}, u32[]{:S(2)}) collective-permute-start(bf16[4,256,512]{2,1,0:T(8,128)(2,1)S(1)} %slice.122), channel_id=1, source_target_pairs={{0,1},{1,0},{2,3},{3,2},{4,5},{5,4},{6,7},{7,6},{8,9},{9,8},{10,11... | collective-permute-start | bytes 3145736 | tf_op jit(solution)/shard_map/ppermute | solution.py:963
  143.2 4.2 %collective-permute-start.9 = (bf16[8,256,512]{2,1,0:T(8,128)(2,1)S(1)}, bf16[8,256,512]{2,1,0:T(8,128)(2,1)S(1)}, u32[]{:S(2)}, u32[]{:S(2)}) collective-permute-start(bf16[8,256,512]{2,1,0:T(8,128)(2,1)S(1)} %bitcast.191), channel_id=1, source_target_pairs={{0,8},{8,0},{16,24},{24,16},{1,9},{9,1},{17,25},{25,17},{2,10},{10... | collective-permute-start | bytes 6291464 | tf_op jit(solution)/shard_map/ppermute | solution.py:957
  160.7 4.6 %collective-permute-start.10 = (bf16[2,8,144,512]{3,2,1,0:T(8,128)(2,1)S(1)}, bf16[2,8,144,512]{3,2,1,0:T(8,128)(2,1)S(1)}, u32[]{:S(2)}, u32[]{:S(2)}) collective-permute-start(bf16[2,8,144,512]{3,2,1,0:T(8,128)(2,1)S(1)} %shard_map.215), channel_id=1, source_target_pairs={{0,8},{8,0},{16,24},{24,16},{1,9},{9,1},{17,25},{25,17},{2,10},{10... | collective-permute-start | bytes 7077896 | tf_op jit(solution)/shard_map/ppermute | solution.py:957
  167.1 32.7 %collective-permute-start.11 = (bf16[8,144,512]{2,1,0:T(8,128)(2,1)}, bf16[8,144,512]{2,1,0:T(8,128)(2,1)S(1)}, u32[]{:S(2)}, u32[]{:S(2)}) collective-permute-start(bf16[8,144,512]{2,1,0:T(8,128)(2,1)} %get-tuple-element.239), channel_id=1, source_target_pairs={{0,16},{8,24},{16,0},{24,8},{1,17},{9,25},{17,1},{25,9},{2,18},{10... | collective-permute-start | bytes 3538952 | tf_op jit(solution)/shard_map/ppermute | solution.py:960
  168.6 31.2 %all-to-all-start.3 = ((bf16[4,128,512]{2,1,0:T(8,128)(2,1)}), bf16[4,128,512]{2,1,0:T(8,128)(2,1)S(1)}, u32[]{:S(2)}, u32[]{:S(2)}) async-start(bf16[4,128,512]{2,1,0:T(8,128)(2,1)} %bitcast.50), calls=%async_computation.3 | async-start | bytes 1048576 | tf_op jit(solution)/shard_map/all_to_all | solution.py:981
  199.8 4.9 %collective-permute-start.13 = (bf16[2,8,80,512]{3,2,1,0:T(8,128)(2,1)}, bf16[2,8,80,512]{3,2,1,0:T(8,128)(2,1)}, u32[]{:S(2)}, u32[]{:S(2)}) collective-permute-start(bf16[2,8,80,512]{3,2,1,0:T(8,128)(2,1)} %get-tuple-element.148), channel_id=1, source_target_pairs={{0,8},{8,0},{16,24},{24,16},{1,9},{9,1},{17,25},{25,17},{2,10},{10... | collective-permute-start | bytes 3932168 | tf_op jit(solution)/shard_map/ppermute | solution.py:957
  199.9 4.9 %collective-permute-start.12 = (bf16[1024,512]{1,0:T(8,128)(2,1)}, bf16[1024,512]{1,0:T(8,128)(2,1)}, u32[]{:S(2)}, u32[]{:S(2)}) collective-permute-start(bf16[1024,512]{1,0:T(8,128)(2,1)} %get-tuple-element.147), channel_id=1, source_target_pairs={{0,8},{8,0},{16,24},{24,16},{1,9},{9,1},{17,25},{25,17},{2,10},{10... | collective-permute-start | bytes 3145736 | tf_op jit(solution)/shard_map/ppermute | solution.py:957
  207.5 32.7 %collective-permute-start.14 = (bf16[4,272,512]{2,1,0:T(8,128)(2,1)}, bf16[4,272,512]{2,1,0:T(8,128)(2,1)S(1)}, u32[]{:S(2)}, u32[]{:S(2)}) collective-permute-start(bf16[4,272,512]{2,1,0:T(8,128)(2,1)} %get-tuple-element.243), channel_id=1, source_target_pairs={{0,1},{1,0},{2,3},{3,2},{4,5},{5,4},{6,7},{7,6},{8,9},{9,8},{10,11... | collective-permute-start | bytes 3342344 | tf_op jit(solution)/shard_map/ppermute | solution.py:963
  210.6 29.6 %collective-permute-start.15 = (bf16[8,80,512]{2,1,0:T(8,128)(2,1)}, bf16[8,80,512]{2,1,0:T(8,128)(2,1)}, u32[]{:S(2)}, u32[]{:S(2)}) collective-permute-start(bf16[8,80,512]{2,1,0:T(8,128)(2,1)} %get-tuple-element.241), channel_id=1, source_target_pairs={{0,16},{8,24},{16,0},{24,8},{1,17},{9,25},{17,1},{25,9},{2,18},{10... | collective-permute-start | bytes 1966088 | tf_op jit(solution)/shard_map/ppermute | solution.py:960
  240.2 11.3 %collective-permute-start.17 = (bf16[1024,512]{1,0:T(8,128)(2,1)}, bf16[1024,512]{1,0:T(8,128)(2,1)}, u32[]{:S(2)}, u32[]{:S(2)}) collective-permute-start(bf16[1024,512]{1,0:T(8,128)(2,1)} %get-tuple-element.168), channel_id=1, source_target_pairs={{0,8},{8,0},{16,24},{24,16},{1,9},{9,1},{17,25},{25,17},{2,10},{10... | collective-permute-start | bytes 3145736 | tf_op jit(solution)/shard_map/ppermute | solution.py:957
  243.9 7.6 %collective-permute-start.18 = (bf16[2,8,48,512]{3,2,1,0:T(8,128)(2,1)}, bf16[2,8,48,512]{3,2,1,0:T(8,128)(2,1)}, u32[]{:S(2)}, u32[]{:S(2)}) collective-permute-start(bf16[2,8,48,512]{3,2,1,0:T(8,128)(2,1)} %get-tuple-element.169), channel_id=1, source_target_pairs={{0,8},{8,0},{16,24},{24,16},{1,9},{9,1},{17,25},{25,17},{2,10},{10... | collective-permute-start | bytes 2359304 | tf_op jit(solution)/shard_map/ppermute | solution.py:957
  244.8 14.9 %collective-permute-start.16 = (bf16[2,128,512]{2,1,0:T(8,128)(2,1)}, bf16[2,128,512]{2,1,0:T(8,128)(2,1)}, u32[]{:S(2)}, u32[]{:S(2)}) collective-permute-start(bf16[2,128,512]{2,1,0:T(8,128)(2,1)} %get-tuple-element.268), channel_id=1, source_target_pairs={{0,8},{8,0},{16,24},{24,16},{1,9},{9,1},{17,25},{25,17},{2,10},{10... | collective-permute-start | bytes 786440 | tf_op jit(solution)/shard_map/ppermute | solution.py:957
  246.6 39.0 %all-to-all-start.4 = ((bf16[4,272,512]{2,1,0:T(8,128)(2,1)}), bf16[4,272,512]{2,1,0:T(8,128)(2,1)S(1)}, u32[]{:S(2)}, u32[]{:S(2)}) async-start(bf16[4,272,512]{2,1,0:T(8,128)(2,1)} %add_convert_fusion.3), calls=%async_computation.4 | async-start | bytes 2228224 | tf_op jit(solution)/shard_map/all_to_all | solution.py:981
  253.1 14.1 %collective-permute-start.19 = (bf16[4,128,512]{2,1,0:T(8,128)(2,1)S(1)}, bf16[4,128,512]{2,1,0:T(8,128)(2,1)S(1)}, u32[]{:S(2)}, u32[]{:S(2)}) collective-permute-start(bf16[4,128,512]{2,1,0:T(8,128)(2,1)S(1)} %get-tuple-element.254), channel_id=1, source_target_pairs={{0,1},{1,0},{2,3},{3,2},{4,5},{5,4},{6,7},{7,6},{8,9},{9,8},{10,11... | collective-permute-start | bytes 1572872 | tf_op jit(solution)/shard_map/ppermute | solution.py:963
  255.5 12.0 %collective-permute-start.24 = (bf16[8,48,512]{2,1,0:T(8,128)(2,1)S(1)}, bf16[8,48,512]{2,1,0:T(8,128)(2,1)S(1)}, u32[]{:S(2)}, u32[]{:S(2)}) collective-permute-start(bf16[8,48,512]{2,1,0:T(8,128)(2,1)S(1)} %get-tuple-element.245), channel_id=1, source_target_pairs={{0,16},{8,24},{16,0},{24,8},{1,17},{9,25},{17,1},{25,9},{2,18},{10... | collective-permute-start | bytes 1179656 | tf_op jit(solution)/shard_map/ppermute | solution.py:960
  267.8 22.9 %collective-permute-start.26 = (bf16[4,128,512]{2,1,0:T(8,128)(2,1)S(1)}, bf16[4,128,512]{2,1,0:T(8,128)(2,1)S(1)}, u32[]{:S(2)}, u32[]{:S(2)}) collective-permute-start(bf16[4,128,512]{2,1,0:T(8,128)(2,1)S(1)} %get-tuple-element.252), channel_id=1, source_target_pairs={{0,1},{1,0},{2,3},{3,2},{4,5},{5,4},{6,7},{7,6},{8,9},{9,8},{10,11... | collective-permute-start | bytes 1572872 | tf_op jit(solution)/shard_map/ppermute | solution.py:963
  269.6 18.2 %collective-permute-start.20 = (bf16[128,512]{1,0:T(8,128)(2,1)}, bf16[128,512]{1,0:T(8,128)(2,1)}, u32[]{:S(2)}, u32[]{:S(2)}) collective-permute-start(bf16[128,512]{1,0:T(8,128)(2,1)} %get-tuple-element.265), channel_id=1, source_target_pairs={{0,2},{1,3},{2,0},{3,1},{4,6},{5,7},{6,4},{7,5},{8,10},{9,11},{10,... | collective-permute-start | bytes 393224 | tf_op jit(solution)/shard_map/ppermute | solution.py:966
  271.3 17.4 %collective-permute-start.21 = (bf16[128,512]{1,0:T(8,128)(2,1)}, bf16[128,512]{1,0:T(8,128)(2,1)S(1)}, u32[]{:S(2)}, u32[]{:S(2)}) collective-permute-start(bf16[128,512]{1,0:T(8,128)(2,1)} %get-tuple-element.264), channel_id=1, source_target_pairs={{0,4},{1,5},{2,6},{3,7},{4,0},{5,1},{6,2},{7,3},{8,12},{9,13},{10,... | collective-permute-start | bytes 393224 | tf_op jit(solution)/shard_map/ppermute | solution.py:966
  273.7 15.1 %collective-permute-start.22 = (bf16[128,512]{1,0:T(8,128)(2,1)}, bf16[128,512]{1,0:T(8,128)(2,1)S(1)}, u32[]{:S(2)}, u32[]{:S(2)}) collective-permute-start(bf16[128,512]{1,0:T(8,128)(2,1)} %get-tuple-element.263), channel_id=1, source_target_pairs={{0,6},{1,7},{2,4},{3,5},{4,2},{5,3},{6,0},{7,1},{8,14},{9,15},{10,... | collective-permute-start | bytes 393224 | tf_op jit(solution)/shard_map/ppermute | solution.py:966
  290.9 7.3 %collective-permute-start.27 = (bf16[128,512]{1,0:T(8,128)(2,1)S(1)}, bf16[128,512]{1,0:T(8,128)(2,1)S(1)}, u32[]{:S(2)}, u32[]{:S(2)}) collective-permute-start(bf16[128,512]{1,0:T(8,128)(2,1)S(1)} %get-tuple-element.256), channel_id=1, source_target_pairs={{0,2},{1,3},{2,0},{3,1},{4,6},{5,7},{6,4},{7,5},{8,10},{9,11},{10,... | collective-permute-start | bytes 393224 | tf_op jit(solution)/shard_map/ppermute | solution.py:966
  293.0 12.8 %collective-permute-start.28 = (bf16[128,512]{1,0:T(8,128)(2,1)S(1)}, bf16[128,512]{1,0:T(8,128)(2,1)S(1)}, u32[]{:S(2)}, u32[]{:S(2)}) collective-permute-start(bf16[128,512]{1,0:T(8,128)(2,1)S(1)} %get-tuple-element.258), channel_id=1, source_target_pairs={{0,4},{1,5},{2,6},{3,7},{4,0},{5,1},{6,2},{7,3},{8,12},{9,13},{10,... | collective-permute-start | bytes 393224 | tf_op jit(solution)/shard_map/ppermute | solution.py:966
  293.1 12.7 %collective-permute-start.29 = (bf16[128,512]{1,0:T(8,128)(2,1)S(1)}, bf16[128,512]{1,0:T(8,128)(2,1)S(1)}, u32[]{:S(2)}, u32[]{:S(2)}) collective-permute-start(bf16[128,512]{1,0:T(8,128)(2,1)S(1)} %get-tuple-element.257), channel_id=1, source_target_pairs={{0,6},{1,7},{2,4},{3,5},{4,2},{5,3},{6,0},{7,1},{8,14},{9,15},{10,... | collective-permute-start | bytes 393224 | tf_op jit(solution)/shard_map/ppermute | solution.py:966
  (33 other events, 145.0 us)
